TPU v7x, 32 devices: a whole 2x2x4 slice. The times are simulated.
32 devices in a mesh: rep: 4 (over z), dp: 4 (over y, core), tensor: 2 (over x).
Axes of the slice: x: 2, y: 2, z: 4, core: 2. Of those that a mesh axis runs over, the one named last changes fastest.
Arguments:
- grad_proj: float32 [16, 3072, 1536], P(('rep', 'dp'), 'tensor'), as said below
- grad_conv: float32 [16, 4, 3328], P(('rep', 'dp'), None, 'tensor'), may hold values from -24 to 24
- param_proj: float32 [3072, 1536], P('tensor', 'dp'), may hold values from -6 to 6
- m_proj: float32 [3072, 1536], P('tensor', 'dp'), may hold values from -2 to 2
- v_proj: float32 [3072, 1536], P('tensor', 'dp'), may hold values from 0.02 to 0.2
- ema_proj: float32 [3072, 1536], P(('tensor', 'dp')), may hold values from -6 to 6
- param_conv: float32 [4, 3328], P(None, 'tensor'), may hold values from -3 to 3
- m_conv: float32 [4, 3328], P(None, 'tensor'), may hold values from -2 to 2
- v_conv: float32 [4, 3328], P(None, 'tensor'), may hold values from 0.02 to 0.2
Outputs:
- new_param_proj: float32 [3072, 1536], P('tensor', 'dp')
- new_m_proj: float32 [3072, 1536], P('tensor', 'dp')
- new_v_proj: float32 [3072, 1536], P('tensor', 'dp')
- new_ema_proj: float32 [3072, 1536], P(('tensor', 'dp'))
- weights_proj: bfloat16 [3072, 1536], P('tensor')
- new_param_conv: float32 [4, 3328], P(None, 'tensor')
- new_m_conv: float32 [4, 3328], P(None, 'tensor')
- new_v_conv: float32 [4, 3328], P(None, 'tensor')
Inputs may be any that keep to these rules, and one draw needn't show every extreme that they name: `grad_proj`: Real-valued gradients with entries of magnitude below 3100.
All inputs are finite; a program needn't handle non-finite values.
Results may differ from a plain program's by a relative error of at most 0.001.
Values may be sent and summed in bfloat16 or wider, within the bound.
No kernel may reach another device: no remote copies, remote signals or barrier semaphores. Data moves between devices by JAX's collectives and lax.ppermute only.
A program may use at most 128 MiB of HBM per device.

v0:
```python
import math

import jax
import jax.numpy as jnp
from jax import lax
from jax.sharding import PartitionSpec as P

D = 1536
INNER = 3072
CONV = 3328
KCONV = 4


def adamw_step(param_in, first_in, second_in, grad_in):
    first_out = 0.9 * first_in + 0.1 * grad_in
    second_out = 0.95 * second_in + 0.05 * grad_in * grad_in
    bias_one = 1.0 - 0.9**10
    bias_two = 1.0 - 0.95**10
    update = first_out / bias_one / (jnp.sqrt(second_out / bias_two) + 1e-08)
    param_out = param_in - 0.25 * (update + 0.1 * param_in)
    return (param_out, first_out, second_out)


def clip_from(square_sum):
    clip_limit = 0.5 * math.sqrt(INNER * D + KCONV * CONV)
    return jnp.minimum(1.0, clip_limit / (jnp.sqrt(square_sum) + 1e-06))


def body(grad_proj, grad_conv, param_proj, m_proj, v_proj, ema_proj, param_conv, m_conv, v_conv):
    replica_count = lax.axis_size("rep") * lax.axis_size("dp")
    conv_avg = lax.psum(grad_conv[0], ("rep", "dp")) / replica_count
    conv_square = jnp.sum(conv_avg * conv_avg)
    first_owner = lax.axis_index("dp") == 0
    owner_sum = lax.psum_scatter(grad_proj[0], "dp", scatter_dimension=1, tiled=True)
    proj_avg = lax.psum(owner_sum, "rep") / replica_count
    conv_share = jnp.where(first_owner, conv_square, jnp.float32(0.0))
    square_sum = lax.psum(jnp.sum(proj_avg * proj_avg) + conv_share, ("dp", "tensor"))
    clip_factor = clip_from(square_sum)
    new_param_proj, new_m_proj, new_v_proj = adamw_step(
        param_proj, m_proj, v_proj, clip_factor * proj_avg
    )
    new_param_conv, new_m_conv, new_v_conv = adamw_step(
        param_conv, m_conv, v_conv, clip_factor * conv_avg
    )
    ema_count = ema_proj.shape[0]
    full_block = lax.all_gather(
        new_param_proj.astype(jnp.bfloat16), "dp", axis=1, tiled=True
    ).astype(new_param_proj.dtype)
    weights_proj = full_block.astype(jnp.bfloat16)
    row_block = lax.dynamic_slice_in_dim(full_block, lax.axis_index("dp") * ema_count, ema_count, 0)
    new_ema_proj = 0.9 * ema_proj + 0.1 * row_block
    return (
        new_param_proj,
        new_m_proj,
        new_v_proj,
        new_ema_proj,
        weights_proj,
        new_param_conv,
        new_m_conv,
        new_v_conv,
    )


def solution(mesh):
    in_specs = (
        P(("rep", "dp"), "tensor", None),
        P(("rep", "dp"), None, "tensor"),
        P("tensor", "dp"),
        P("tensor", "dp"),
        P("tensor", "dp"),
        P(("tensor", "dp"), None),
        P(None, "tensor"),
        P(None, "tensor"),
        P(None, "tensor"),
    )
    out_specs = (
        P("tensor", "dp"),
        P("tensor", "dp"),
        P("tensor", "dp"),
        P(("tensor", "dp"), None),
        P("tensor", None),
        P(None, "tensor"),
        P(None, "tensor"),
        P(None, "tensor"),
    )
    return jax.shard_map(body, mesh=mesh, in_specs=in_specs, out_specs=out_specs, check_vma=False)
```

profile of v0, /device:TPU:1, one launch (start us, length us, event | category | flops | bytes accessed | tf_op | source)
XLA Modules:
  0.0 264.5 jit_solution(619298078873082308)
XLA Ops:
  7.2 0.0 reduce-scatter.2.cloned.1.call-start
  7.2 0.7 reduce-scatter.2.cloned.1.call-update
  7.9 0.0 copy-start.2
  7.9 0.0 all-reduce.2.cloned.1.call-start
  8.0 83.2 %reduce-scatter.2.cloned.1.call-done = f32[1536,384]{1,0:T(8,128)} async-done(((f32[1536,1536]{1,0:T(8,128)}), f32[1536,384]{1,0:T(8,128)}) %reduce-scatter.2.cloned.1.call-update) | async-done | bytes 2359312 | tf_op jit(solution)/shard_map/reduce_scatter | solution.py:34
  91.1 0.0 all-reduce.2.cloned.1.call-update
  91.2 0.0 all-gather.2.cloned.1.call-start
  91.2 0.0 copy-done.2
  91.2 58.9 %psum.22 = f32[4,1664]{1,0:T(4,128)S(1)} all-reduce(f32[4,1664]{1,0:T(4,128)S(1)} %bitcast.3), channel_id=1, replica_groups=mesh['rep'=4,'dp'=4,'tensor'=2] {'rep','dp'}, use_global_device_ids=true, to_apply=%region_3.0 | all-reduce | flops 6656 | bytes 53248 | tf_op jit(solution)/shard_map/psum | solution.py:31
  150.1 0.6 multiply_reduce_fusion.1
  151.4 38.1 %all-reduce.2.cloned.1.call-done = f32[1536,384]{1,0:T(8,128)} async-done(((f32[1536,384]{1,0:T(8,128)}), f32[1536,384]{1,0:T(8,128)}) %all-reduce.2.cloned.1.call-update) | async-done | bytes 2359312 | tf_op jit(solution)/shard_map/psum | solution.py:35
  189.5 3.0 %multiply_reduce_fusion = f32[]{:T(128)} fusion(f32[1536,384]{1,0:T(8,128)} %all-reduce.2.cloned.1.call-done), kind=kLoop, calls=%fused_computation.5 | loop fusion | flops 1769471 | bytes 2359300 | tf_op jit(solution)/shard_map/reduce_sum | solution.py:37
  193.2 14.3 %psum.23 = f32[]{:T(128)} all-reduce(f32[]{:T(128)S(6)} %add.50), channel_id=1, replica_groups=mesh['rep'=4,'dp'=4,'tensor'=2] {'dp','tensor'}, use_global_device_ids=true, to_apply=%region_5.6 | all-reduce | flops 1 | bytes 8 | tf_op jit(solution)/shard_map/psum | solution.py:37
  208.3 0.0 copy-done
  208.3 0.0 copy-start.3
  208.3 0.0 copy-start.4
  208.3 0.0 copy-start.5
  208.3 7.6 %fusion.3 = (bf16[1536,384]{1,0:T(8,128)(2,1)}, f32[1536,384]{1,0:T(8,128)}, f32[1536,384]{1,0:T(8,128)}, f32[1536,384]{1,0:T(8,128)}) fusion(f32[1536,384]{1,0:T(8,128)} %param.11, f32[1536,384]{1,0:T(8,128)S(1)} %copy-done, f32[]{:T(128)S(6)} %mul.105, f32[1536,384]{1,0:T(8,128)} %param.12, f32[1536,384]{1,0:T(8,128)} %param.13), kind=kLoop, calls=%fused_computation.11 | loop fusion | flops 10027008 | bytes 17694724 | tf_op jit(solution)/shard_map/convert_element_type | solution.py:47
  215.9 0.0 all-gather.2.cloned.1.call-update
  215.9 0.0 copy-done.3
  216.0 0.7 multiply_subtract_fusion.1
  216.7 35.2 %all-gather.2.cloned.1.call-done = bf16[1536,1536]{1,0:T(8,128)(2,1)} async-done(((bf16[1536,384]{1,0:T(8,128)(2,1)}), bf16[1536,1536]{1,0:T(8,128)(2,1)}) %all-gather.2.cloned.1.call-update) | async-done | bytes 4718608 | tf_op jit(solution)/shard_map/all_gather | solution.py:46
  251.9 3.9 %multiply_add_fusion = f32[384,1536]{1,0:T(8,128)} fusion(f32[384,1536]{1,0:T(8,128)} %param.14, bf16[1536,1536]{1,0:T(8,128)(2,1)} %all-gather.2.cloned.1.call-done, s32[]{:T(128)S(6)} %select_n.8), kind=kLoop, calls=%fused_computation.2 | loop fusion | flops 2359296 | bytes 5898244 | tf_op jit(solution)/shard_map/add | solution.py:51
  255.8 2.2 copy.19
  (5 shorter events, 0.0 us)
Async XLA Ops:
  7.2 84.0 %reduce-scatter.2.cloned.1.call-start = ((), (), s32[]{:S(2)}) async-start(), calls=%async_computation.1 | async-start | bytes 11796480 | tf_op jit(solution)/shard_map/reduce_scatter | solution.py:34
  7.9 83.3 %copy-start.2 = (f32[1,4,1664]{2,1,0:T(4,128)S(1)}, f32[1,4,1664]{2,1,0:T(4,128)}, u32[]{:S(2)}) copy-start(f32[1,4,1664]{2,1,0:T(4,128)} %param.10) | copy-start | bytes 79876
  7.9 181.6 %all-reduce.2.cloned.1.call-start = ((), (), s32[]{:S(2)}) async-start(), calls=%async_computation.2 | async-start | bytes 4718592 | tf_op jit(solution)/shard_map/psum | solution.py:35
  91.2 160.7 %all-gather.2.cloned.1.call-start = ((), (), s32[]{:S(2)}) async-start(), calls=%async_computation.3 | async-start | bytes 5898240 | tf_op jit(solution)/shard_map/all_gather | solution.py:46
  189.5 18.7 %copy-start = (f32[1536,384]{1,0:T(8,128)S(1)}, f32[1536,384]{1,0:T(8,128)}, u32[]{:S(2)}) copy-start(f32[1536,384]{1,0:T(8,128)} %all-reduce.2.cloned.1.call-done) | copy-start | bytes 7077892
  208.3 7.7 %copy-start.3 = (f32[4,1664]{1,0:T(4,128)S(1)}, f32[4,1664]{1,0:T(4,128)}, u32[]{:S(2)}) copy-start(f32[4,1664]{1,0:T(4,128)} %param.15) | copy-start | bytes 79876
  208.3 7.7 %copy-start.4 = (f32[4,1664]{1,0:T(4,128)S(1)}, f32[4,1664]{1,0:T(4,128)}, u32[]{:S(2)}) copy-start(f32[4,1664]{1,0:T(4,128)} %param.16) | copy-start | bytes 79876
  208.3 7.7 %copy-start.5 = (f32[4,1664]{1,0:T(4,128)S(1)}, f32[4,1664]{1,0:T(4,128)}, u32[]{:S(2)}) copy-start(f32[4,1664]{1,0:T(4,128)} %param.17) | copy-start | bytes 79876
  251.9 3.9 %copy-start.1 = (bf16[1536,1536]{1,0:T(8,128)(2,1)S(1)}, bf16[1536,1536]{1,0:T(8,128)(2,1)}, u32[]{:S(2)}) copy-start(bf16[1536,1536]{1,0:T(8,128)(2,1)} %all-gather.2.cloned.1.call-done) | copy-start | bytes 14155780
Sparse Core Ops, SparseCore 0:
  10.6 80.4 reduce-scatter.1
  93.5 95.9 all-reduce.1
  216.1 35.7 all-gather.1
where the time goes:
time: 265 us
  waiting for transfers between devices  157 us (59%)
  blocking collectives  73.2 us (28%)
  other arithmetic  15.9 us (6%)
  between operations  15.9 us (6%)
    reduce_scatter x1, waiting for transfers between devices, body(): lax.psum_scatter(grad_proj[0], 'dp', scatter_dimension=1, tiled=True)  83.2 us
    psum x1, blocking collectives, body(): conv_avg = lax.psum(grad_conv[0], ('rep', 'dp')) / replica_count  58.9 us
    psum x1, waiting for transfers between devices, body(): proj_avg = lax.psum(owner_sum, 'rep') / replica_count  38.1 us
    all_gather x1, waiting for transfers between devices, body(): lax.all_gather(new_param_proj.astype(jnp.bfloat16), 'dp', axis=1, tiled=T...  35.2 us
    psum x1, blocking collectives, body(): lax.psum(jnp.sum(proj_avg * proj_avg) + conv_share, ('dp', 'tensor'))  14.3 us
    convert_element_type x1, other arithmetic, body(): new_param_proj.astype(jnp.bfloat16)  7.62 us
  transfers between devices with their start and end apart: 3, of which 3 were waited for; matrix products, arithmetic and copies ran while one was open for 0% of the time, Pallas kernels for 0%

commit v1 on v0

v1 whole, which is shorter than its diff:
```python
import math

import jax
import jax.numpy as jnp
from jax import lax
from jax.sharding import PartitionSpec as P

D = 1536
INNER = 3072
CONV = 3328
KCONV = 4

CORES = 2
REDUCE_CHUNKS = 4
GATHER_CHUNKS = 4
F16_SAFE_REPLICAS = 16


def adamw_step(param_in, first_in, second_in, grad_in):
    first_out = 0.9 * first_in + 0.1 * grad_in
    second_out = 0.95 * second_in + 0.05 * grad_in * grad_in
    bias_one = 1.0 - 0.9**10
    bias_two = 1.0 - 0.95**10
    update = first_out / bias_one / (jnp.sqrt(second_out / bias_two) + 1e-08)
    param_out = param_in - 0.25 * (update + 0.1 * param_in)
    return (param_out, first_out, second_out)


def clip_from(square_sum):
    clip_limit = 0.5 * math.sqrt(INNER * D + KCONV * CONV)
    return jnp.minimum(1.0, clip_limit / (jnp.sqrt(square_sum) + 1e-06))


def butterfly_sum(value, axis):
    size = lax.axis_size(axis)
    step = 1
    while step < size:
        value = value + lax.ppermute(value, axis, [(i, i ^ step) for i in range(size)])
        step *= 2
    return value


def widen(x):
    return x.astype(jnp.float32)


def narrow(x):
    return x.astype(jnp.float16)


def tile_squares(x):
    return jnp.sum(x * x, axis=0, keepdims=True)


def body(grad_proj, grad_conv, param_proj, m_proj, v_proj, ema_proj, param_conv, m_conv, v_conv):
    reps, owners, tensors = lax.axis_size("rep"), lax.axis_size("dp"), lax.axis_size("tensor")
    replica_count = reps * owners
    chips = owners // CORES
    rows, cols = param_proj.shape
    me = lax.axis_index("dp")
    chip, core = me // CORES, me % CORES
    rep = lax.axis_index("rep")

    def core_swap(x):
        return lax.ppermute(x, "dp", [(i, i ^ 1) for i in range(owners)])

    def chip_shift(x, off):
        pairs = [
            (a * CORES + c, ((a + off) % chips) * CORES + c) for a in range(chips) for c in range(CORES)
        ]
        return lax.ppermute(x, "dp", pairs)

    grad = grad_proj[0]
    scale = 1.0 / max(1, 2 ** math.ceil(math.log2(replica_count / F16_SAFE_REPLICAS)))

    conv_avg = butterfly_sum(butterfly_sum(grad_conv[0], "dp"), "rep") / replica_count
    conv_square = jnp.sum(conv_avg * conv_avg)

    parts = REDUCE_CHUNKS
    part_rows = rows // parts
    group_sums = []
    for i in range(parts):

        def block(owner):
            piece = lax.dynamic_slice(grad, (i * part_rows, owner * cols), (part_rows, cols))
            return piece * scale if scale != 1.0 else piece

        from_chips = []
        for off in range(1, chips):
            other = (chip + off) % chips
            got = core_swap(narrow(block(other * CORES + 1 - core)))
            pair_sum = block(other * CORES + core) + widen(got)
            from_chips.append(chip_shift(narrow(pair_sum), off))
        got = core_swap(narrow(block(chip * CORES + 1 - core)))
        total = block(me) + widen(got)
        for got in from_chips:
            total = total + widen(got)
        group_sums.append(total)

    if reps == 4:
        is_end = (rep == 0) | (rep == 3)
        middle_totals, totals = [], []
        for step in range(parts + 2):
            if step < parts:
                payload = narrow(group_sums[step])
                if step >= 2:
                    payload = jnp.where(is_end, payload, middle_totals[step - 2])
            else:
                payload = middle_totals[step - 2]
            got = lax.ppermute(payload, "rep", [(0, 1), (1, 0), (2, 3), (3, 2)])
            if step < parts:
                half = narrow(group_sums[step] + widen(got))
                other_half = lax.ppermute(half, "rep", [(1, 2), (2, 1)])
                middle_totals.append(narrow(widen(half) + widen(other_half)))
            if step >= 2:
                totals.append(jnp.where(is_end, got, middle_totals[step - 2]))
    else:
        totals = [lax.psum(s, "rep") for s in group_sums]

    inverse = 1.0 / (replica_count * scale)
    avgs = [widen(t) * inverse for t in totals]
    square = sum(tile_squares(a) for a in avgs)
    square = square + jnp.where(me == 0, conv_square, 0.0) * (lax.broadcasted_iota(jnp.int32, square.shape, 1) == 0)
    square = butterfly_sum(butterfly_sum(square, "dp"), "tensor")
    clip_factor = clip_from(jnp.sum(square))
    proj_avg = jnp.concatenate(avgs, axis=0)

    weights = adamw_step(param_proj, m_proj, v_proj, clip_factor * proj_avg)[0].astype(jnp.bfloat16)
    weights, proj_avg, clip_factor = lax.optimization_barrier((weights, proj_avg, clip_factor))

    full = jnp.zeros((rows, cols * owners), jnp.bfloat16)
    full = lax.dynamic_update_slice(full, weights, (0, me * cols))
    full = lax.dynamic_update_slice(full, core_swap(weights), (0, (me ^ 1) * cols))
    parts = GATHER_CHUNKS
    part_rows = rows // parts
    for i in range(parts):
        for off in range(1, chips):
            to_chip, from_chip = (chip + off) % chips, (chip - off) % chips
            out_row = ((to_chip * parts) // chips + i) % parts * part_rows
            in_row = ((chip * parts) // chips + i) % parts * part_rows
            piece = lax.dynamic_slice(weights, (out_row, 0), (part_rows, cols))
            got = chip_shift(piece, off)
            got_other = core_swap(got)
            full = lax.dynamic_update_slice(full, got, (in_row, (from_chip * CORES + core) * cols))
            full = lax.dynamic_update_slice(full, got_other, (in_row, (from_chip * CORES + 1 - core) * cols))

    new_param_proj, new_m_proj, new_v_proj = adamw_step(param_proj, m_proj, v_proj, clip_factor * proj_avg)
    new_param_conv, new_m_conv, new_v_conv = adamw_step(param_conv, m_conv, v_conv, clip_factor * conv_avg)
    ema_count = ema_proj.shape[0]
    row_block = lax.dynamic_slice_in_dim(full, me * ema_count, ema_count, 0)
    new_ema_proj = 0.9 * ema_proj + 0.1 * widen(row_block)
    return (
        new_param_proj,
        new_m_proj,
        new_v_proj,
        new_ema_proj,
        full,
        new_param_conv,
        new_m_conv,
        new_v_conv,
    )


def solution(mesh):
    in_specs = (
        P(("rep", "dp"), "tensor", None),
        P(("rep", "dp"), None, "tensor"),
        P("tensor", "dp"),
        P("tensor", "dp"),
        P("tensor", "dp"),
        P(("tensor", "dp"), None),
        P(None, "tensor"),
        P(None, "tensor"),
        P(None, "tensor"),
    )
    out_specs = (
        P("tensor", "dp"),
        P("tensor", "dp"),
        P("tensor", "dp"),
        P(("tensor", "dp"), None),
        P("tensor", None),
        P(None, "tensor"),
        P(None, "tensor"),
        P(None, "tensor"),
    )
    return jax.shard_map(body, mesh=mesh, in_specs=in_specs, out_specs=out_specs, check_vma=False)
```

time: 265 us -> 182 us (0.69)
  waiting for transfers between devices: 157 us -> 53.4 us
  blocking collectives: 73.2 us -> 0 us
  starting transfers between devices: 0.11 us -> 53.6 us
  local copies, waits for them, and re-layouts: 2.22 us -> 38.4 us
  other arithmetic: 15.9 us -> 33.1 us
  between operations: 15.9 us -> 2.38 us
    reduce_scatter x1 -> x0, waiting for transfers between devices: 83.2 us -> none  [body(): lax.psum_scatter(grad_proj[0], 'dp', scatter_dimension=1, tiled=True)]
    psum x2 -> x0, blocking collectives: 73.2 us -> none  [the longest x1 58.9 us: body(): conv_avg = lax.psum(grad_conv[0], ('rep', 'dp')) / replica_count]
    ppermute x0 -> x38, starting transfers between devices: none -> 53.6 us  [the longest x13 16.4 us: core_swap(): return lax.ppermute(x, 'dp', [(i, i ^ 1) for i in range(owners)])]
    ppermute x0 -> x38, waiting for transfers between devices: none -> 53.4 us  [the longest x8 30.2 us: chip_shift(): return lax.ppermute(x, 'dp', pairs)]
    psum x1 -> x0, waiting for transfers between devices: 38.1 us -> none  [body(): proj_avg = lax.psum(owner_sum, 'rep') / replica_count]
    dynamic_update_slice x0 -> x10, local copies, waits for them, and re-layouts: none -> 36.2 us  [the longest x4 17.8 us: body(): lax.dynamic_update_slice(full, got, (in_row, (from_chip * CORES + core) *...]
    all_gather x1 -> x0, waiting for transfers between devices: 35.2 us -> none  [body(): lax.all_gather(new_param_proj.astype(jnp.bfloat16), 'dp', axis=1, tiled=T...]
    concatenate x0 -> x1, other arithmetic: none -> 5.29 us  [body(): proj_avg = jnp.concatenate(avgs, axis=0)]
  transfers between devices with their start and end apart: 3 -> 38, of which waited for: 3 -> 18; matrix products, arithmetic and copies ran while one was open for 0% -> 30% of each run, Pallas kernels for 0% -> 0%
where the time goes in v1:
time: 182 us; the launch traced here: 181 us
  starting transfers between devices  53.6 us (29%)
  waiting for transfers between devices  53.4 us (29%)
  local copies, waits for them, and re-layouts  38.4 us (21%)
  other arithmetic  33.1 us (18%)
  between operations  2.38 us (1%)
    ppermute x8, waiting for transfers between devices, chip_shift(): return lax.ppermute(x, 'dp', pairs)  30.2 us
    dynamic_update_slice x4, local copies, waits for them, and re-layouts, body(): lax.dynamic_update_slice(full, got, (in_row, (from_chip * CORES + core) *...  17.8 us
    dynamic_update_slice x4, local copies, waits for them, and re-layouts, body(): lax.dynamic_update_slice(full, got_other, (in_row, (from_chip * CORES + 1...  16.6 us
    ppermute x6, waiting for transfers between devices, body(): got = lax.ppermute(payload, 'rep', [(0, 1), (1, 0), (2, 3), (3, 2)])  16.5 us
    ppermute x13, starting transfers between devices, core_swap(): return lax.ppermute(x, 'dp', [(i, i ^ 1) for i in range(owners)])  16.4 us
    ppermute x7, starting transfers between devices, butterfly_sum(): lax.ppermute(value, axis, [(i, i ^ step) for i in range(size)])  12.7 us
    ppermute x6, starting transfers between devices, body(): got = lax.ppermute(payload, 'rep', [(0, 1), (1, 0), (2, 3), (3, 2)])  12.4 us
    convert_element_type x6, other arithmetic, narrow(): return x.astype(jnp.float16)  8.99 us
  transfers between devices with their start and end apart: 38, of which 18 were waited for; matrix products, arithmetic and copies ran while one was open for 30% of the time, Pallas kernels for 0%

profile of v1, /device:TPU:1, one launch (start us, length us, event | category | flops | bytes accessed | tf_op | source)
XLA Modules:
  0.0 180.9 jit_solution(10580083667979550396)
XLA Ops:
  0.7 3.5 %fusion.17 = (f16[384,384]{1,0:T(8,128)(2,1)S(1)}, f16[384,384]{1,0:T(8,128)(2,1)S(1)}, f16[384,384]{1,0:T(8,128)(2,1)}, f16[384,384]{1,0:T(8,128)(2,1)S(1)}, f1...) fusion(f32[1,1536,1536]{2,1,0:T(8,128)} %param.9, ...), kind=kLoop, calls=%fused_computation.56 | loop fusion | flops 1179648 | bytes 7077896 | tf_op jit(solution)/shard_map/convert_element_type | solution.py:48
  10.0 6.4 %collective-permute-done.5 = f16[384,384]{1,0:T(8,128)(2,1)S(1)} collective-permute-done((f16[384,384]{1,0:T(8,128)(2,1)S(1)}, f16[384,384]{1,0:T(8,128)(2,1)S(1)}, u32[]{:S(2)}, u32[]{:S(2)}) %collective-permute-start.5) | collective-permute-done | bytes 294944 | tf_op jit(solution)/shard_map/ppermute | solution.py:71
  22.1 3.4 %collective-permute-done.14 = f16[384,384]{1,0:T(8,128)(2,1)S(1)} collective-permute-done((f16[384,384]{1,0:T(8,128)(2,1)S(1)}, f16[384,384]{1,0:T(8,128)(2,1)S(1)}, u32[]{:S(2)}, u32[]{:S(2)}) %collective-permute-start.14) | collective-permute-done | bytes 294944 | tf_op jit(solution)/shard_map/ppermute | solution.py:71
  31.7 4.0 %collective-permute-start.15 = (f16[384,384]{1,0:T(8,128)(2,1)S(1)}, f16[384,384]{1,0:T(8,128)(2,1)S(1)}, u32[]{:S(2)}, u32[]{:S(2)}) collective-permute-start(f16[384,384]{1,0:T(8,128)(2,1)S(1)} %get-tuple-element.34), channel_id=1, source_target_pairs={{0,8},{8,0},{16,24},{24,16},{1,9},{9,1},{17,25},{25,17},{2,10},{10... | collective-permute-start | bytes 884744 | tf_op jit(solution)/shard_map/ppermute | solution.py:110
  38.6 3.8 %collective-permute-start.9 = (f16[384,384]{1,0:T(8,128)(2,1)S(1)}, f16[384,384]{1,0:T(8,128)(2,1)S(1)}, u32[]{:S(2)}, u32[]{:S(2)}) collective-permute-start(f16[384,384]{1,0:T(8,128)(2,1)S(1)} %get-tuple-element.41), channel_id=1, source_target_pairs={{0,2},{2,0},{4,6},{6,4},{1,3},{3,1},{5,7},{7,5},{8,10},{10,8},{12,... | collective-permute-start | bytes 884744 | tf_op jit(solution)/shard_map/ppermute | solution.py:65
  43.0 6.2 %collective-permute-done.8 = f16[384,384]{1,0:T(8,128)(2,1)S(1)} collective-permute-done((f16[384,384]{1,0:T(8,128)(2,1)S(1)}, f16[384,384]{1,0:T(8,128)(2,1)S(1)}, u32[]{:S(2)}, u32[]{:S(2)}) %collective-permute-start.8) | collective-permute-done | bytes 294944 | tf_op jit(solution)/shard_map/ppermute | solution.py:110
  55.0 4.7 %collective-permute-done.11 = f16[384,384]{1,0:T(8,128)(2,1)S(1)} collective-permute-done((f16[384,384]{1,0:T(8,128)(2,1)S(1)}, f16[384,384]{1,0:T(8,128)(2,1)S(1)}, u32[]{:S(2)}, u32[]{:S(2)}) %collective-permute-start.11) | collective-permute-done | bytes 294944 | tf_op jit(solution)/shard_map/ppermute | solution.py:71
  61.0 3.9 %collective-permute-start.17 = (f16[384,384]{1,0:T(8,128)(2,1)S(1)}, f16[384,384]{1,0:T(8,128)(2,1)S(1)}, u32[]{:S(2)}, u32[]{:S(2)}) collective-permute-start(f16[384,384]{1,0:T(8,128)(2,1)S(1)} %convert_select_fusion), channel_id=1, source_target_pairs={{0,8},{8,0},{16,24},{24,16},{1,9},{9,1},{17,25},{25,17},{2,10},{10... | collective-permute-start | bytes 884744 | tf_op jit(solution)/shard_map/ppermute | solution.py:110
  65.8 4.3 %collective-permute-done.17 = f16[384,384]{1,0:T(8,128)(2,1)S(1)} collective-permute-done((f16[384,384]{1,0:T(8,128)(2,1)S(1)}, f16[384,384]{1,0:T(8,128)(2,1)S(1)}, u32[]{:S(2)}, u32[]{:S(2)}) %collective-permute-start.17) | collective-permute-done | bytes 294944 | tf_op jit(solution)/shard_map/ppermute | solution.py:110
  86.0 3.8 %collective-permute-done.21 = f16[384,384]{1,0:T(8,128)(2,1)S(1)} collective-permute-done((f16[384,384]{1,0:T(8,128)(2,1)S(1)}, f16[384,384]{1,0:T(8,128)(2,1)S(1)}, u32[]{:S(2)}, u32[]{:S(2)}) %collective-permute-start.21) | collective-permute-done | bytes 294944 | tf_op jit(solution)/shard_map/ppermute | solution.py:110
  90.8 5.8 %collective-permute-start.26 = (f32[1,384]{1,0:T(1,128)S(1)}, f32[1,384]{1,0:T(1,128)S(1)}, u32[]{:S(2)}, u32[]{:S(2)}) collective-permute-start(f32[1,384]{1,0:T(1,128)S(1)} %fusion.26), channel_id=1, source_target_pairs={{0,2},{2,0},{4,6},{6,4},{1,3},{3,1},{5,7},{7,5},{8,10},{10,8},{12,... | collective-permute-start | bytes 4616 | tf_op jit(solution)/shard_map/ppermute | solution.py:38
  103.6 5.3 %pad_maximum_fusion = (f32[1536,384]{1,0:T(8,128)S(1)}, bf16[1536,384]{1,0:T(8,128)(2,1)S(1)}) fusion(f32[384,384]{1,0:T(8,128)} %get-tuple-element.29, f32[384,384]{1,0:T(8,128)} %get-tuple-element.27, f32[384,384]{1,0:T(8,128)} %get-tuple-element.23, f32[384,384]{1,0:T(8,128)} %get-tuple-element.25, f32[1536,384]{1,0:T(8,128)S(1)} %copy-done, ...), kind=kLoop, calls=%fused_computation.9 | loop fusion | flops 11796480 | bytes 12976132 | tf_op jit(solution)/shard_map/concatenate | solution.py:126
  115.6 4.1 %multiply_subtract_fusion = (f32[1536,384]{1,0:T(8,128)}, f32[1536,384]{1,0:T(8,128)}, f32[1536,384]{1,0:T(8,128)}) fusion(f32[1536,384]{1,0:T(8,128)S(1)} %copy-done, f32[1536,384]{1,0:T(8,128)S(1)} %get-tuple-element.12, f32[]{:T(128)S(6)} %min_shard_map.3, f32[1536,384]{1,0:T(8,128)S(1)} %copy-done.2, f32[1536,384]{1,0:T(8,128)S(1)} %copy-done.1), kind=kLoop, calls=%fused_computation.11 | loop fusion | flops 9437184 | bytes 16515076 | tf_op jit(solution)/shard_map/sub | solution.py:25
  122.8 5.1 %collective-permute-done.32 = bf16[384,384]{1,0:T(8,128)(2,1)} collective-permute-done((bf16[384,384]{1,0:T(8,128)(2,1)}, bf16[384,384]{1,0:T(8,128)(2,1)}, u32[]{:S(2)}, u32[]{:S(2)}) %collective-permute-start.32) | collective-permute-done | bytes 294944 | tf_op jit(solution)/shard_map/ppermute | solution.py:71
  129.1 5.1 %collective-permute-done.34 = bf16[384,384]{1,0:T(8,128)(2,1)} collective-permute-done((bf16[384,384]{1,0:T(8,128)(2,1)}, bf16[384,384]{1,0:T(8,128)(2,1)}, u32[]{:S(2)}, u32[]{:S(2)}) %collective-permute-start.34) | collective-permute-done | bytes 294944 | tf_op jit(solution)/shard_map/ppermute | solution.py:71
  135.4 5.1 %collective-permute-done.36 = bf16[384,384]{1,0:T(8,128)(2,1)} collective-permute-done((bf16[384,384]{1,0:T(8,128)(2,1)}, bf16[384,384]{1,0:T(8,128)(2,1)}, u32[]{:S(2)}, u32[]{:S(2)}) %collective-permute-start.36) | collective-permute-done | bytes 294944 | tf_op jit(solution)/shard_map/ppermute | solution.py:71
  143.4 4.8 %dynamic_update_slice.32 = bf16[1536,1536]{1,0:T(8,128)(2,1)S(1)} dynamic-update-slice(bf16[1536,1536]{1,0:T(8,128)(2,1)S(1)} %constant_dynamic-update-slice_fusion, bf16[384,384]{1,0:T(8,128)(2,1)} %collective-permute-done.30, s32[]{:T(128)S(6)} %select_n.205, s32[]{:T(128)S(6)} %select_n.207) | dynamic-update-slice | bytes 589828 | tf_op jit(solution)/shard_map/dynamic_update_slice | solution.py:144
  148.3 4.3 %dynamic_update_slice.33 = bf16[1536,1536]{1,0:T(8,128)(2,1)S(1)} dynamic-update-slice(bf16[1536,1536]{1,0:T(8,128)(2,1)S(1)} %dynamic_update_slice.32, bf16[384,384]{1,0:T(8,128)(2,1)S(1)} %collective-permute-done.31, s32[]{:T(128)S(6)} %select_n.205, s32[]{:T(128)S(6)} %select_n.208) | dynamic-update-slice | bytes 589828 | tf_op jit(solution)/shard_map/dynamic_update_slice | solution.py:145
  152.6 4.4 %dynamic_update_slice.34 = bf16[1536,1536]{1,0:T(8,128)(2,1)S(1)} dynamic-update-slice(bf16[1536,1536]{1,0:T(8,128)(2,1)S(1)} %dynamic_update_slice.33, bf16[384,384]{1,0:T(8,128)(2,1)} %collective-permute-done.32, s32[]{:T(128)S(6)} %select_n.212, s32[]{:T(128)S(6)} %select_n.207) | dynamic-update-slice | bytes 589828 | tf_op jit(solution)/shard_map/dynamic_update_slice | solution.py:144
  157.0 4.3 %dynamic_update_slice.35 = bf16[1536,1536]{1,0:T(8,128)(2,1)S(1)} dynamic-update-slice(bf16[1536,1536]{1,0:T(8,128)(2,1)S(1)} %dynamic_update_slice.34, bf16[384,384]{1,0:T(8,128)(2,1)S(1)} %collective-permute-done.33, s32[]{:T(128)S(6)} %select_n.212, s32[]{:T(128)S(6)} %select_n.208) | dynamic-update-slice | bytes 589828 | tf_op jit(solution)/shard_map/dynamic_update_slice | solution.py:145
  161.3 4.4 %dynamic_update_slice.36 = bf16[1536,1536]{1,0:T(8,128)(2,1)S(1)} dynamic-update-slice(bf16[1536,1536]{1,0:T(8,128)(2,1)S(1)} %dynamic_update_slice.35, bf16[384,384]{1,0:T(8,128)(2,1)} %collective-permute-done.34, s32[]{:T(128)S(6)} %select_n.216, s32[]{:T(128)S(6)} %select_n.207) | dynamic-update-slice | bytes 589828 | tf_op jit(solution)/shard_map/dynamic_update_slice | solution.py:144
  165.7 4.3 %dynamic_update_slice.37 = bf16[1536,1536]{1,0:T(8,128)(2,1)S(1)} dynamic-update-slice(bf16[1536,1536]{1,0:T(8,128)(2,1)S(1)} %dynamic_update_slice.36, bf16[384,384]{1,0:T(8,128)(2,1)S(1)} %collective-permute-done.35, s32[]{:T(128)S(6)} %select_n.216, s32[]{:T(128)S(6)} %select_n.208) | dynamic-update-slice | bytes 589828 | tf_op jit(solution)/shard_map/dynamic_update_slice | solution.py:145
  170.0 4.2 %dynamic_update_slice.38 = bf16[1536,1536]{1,0:T(8,128)(2,1)S(1)} dynamic-update-slice(bf16[1536,1536]{1,0:T(8,128)(2,1)S(1)} %dynamic_update_slice.37, bf16[384,384]{1,0:T(8,128)(2,1)} %collective-permute-done.36, s32[]{:T(128)S(6)} %select_n.220, s32[]{:T(128)S(6)} %select_n.207) | dynamic-update-slice | bytes 589828 | tf_op jit(solution)/shard_map/dynamic_update_slice | solution.py:144
  174.2 3.8 %dynamic_update_slice.39 = bf16[1536,1536]{1,0:T(8,128)(2,1)S(1)} dynamic-update-slice(bf16[1536,1536]{1,0:T(8,128)(2,1)S(1)} %dynamic_update_slice.38, bf16[384,384]{1,0:T(8,128)(2,1)S(1)} %collective-permute-done.37, s32[]{:T(128)S(6)} %select_n.220, s32[]{:T(128)S(6)} %select_n.208) | dynamic-update-slice | bytes 589828 | tf_op jit(solution)/shard_map/dynamic_update_slice | solution.py:145
  (101 shorter events, 69.5 us)
Async XLA Ops:
  6.9 9.5 %collective-permute-start.5 = (f16[384,384]{1,0:T(8,128)(2,1)S(1)}, f16[384,384]{1,0:T(8,128)(2,1)S(1)}, u32[]{:S(2)}, u32[]{:S(2)}) collective-permute-start(f16[384,384]{1,0:T(8,128)(2,1)S(1)} %fusion.11), channel_id=1, source_target_pairs={{0,4},{2,6},{4,0},{6,2},{1,5},{3,7},{5,1},{7,3},{8,12},{10,14},{12... | collective-permute-start | bytes 884744 | tf_op jit(solution)/shard_map/ppermute | solution.py:71
  9.3 12.8 %collective-permute-start.1 = (f16[384,384]{1,0:T(8,128)(2,1)S(1)}, f16[384,384]{1,0:T(8,128)(2,1)S(1)}, u32[]{:S(2)}, u32[]{:S(2)}) collective-permute-start(f16[384,384]{1,0:T(8,128)(2,1)S(1)} %get-tuple-element.43), channel_id=1, source_target_pairs={{0,2},{2,0},{4,6},{6,4},{1,3},{3,1},{5,7},{7,5},{8,10},{10,8},{12,... | collective-permute-start | bytes 884744 | tf_op jit(solution)/shard_map/ppermute | solution.py:65
  10.0 12.1 %collective-permute-start.12 = (f16[384,384]{1,0:T(8,128)(2,1)S(1)}, f16[384,384]{1,0:T(8,128)(2,1)S(1)}, u32[]{:S(2)}, u32[]{:S(2)}) collective-permute-start(f16[384,384]{1,0:T(8,128)(2,1)S(1)} %get-tuple-element.39), channel_id=1, source_target_pairs={{0,2},{2,0},{4,6},{6,4},{1,3},{3,1},{5,7},{7,5},{8,10},{10,8},{12,... | collective-permute-start | bytes 884744 | tf_op jit(solution)/shard_map/ppermute | solution.py:65
  20.4 15.3 %collective-permute-start = (f16[384,384]{1,0:T(8,128)(2,1)}, f16[384,384]{1,0:T(8,128)(2,1)S(1)}, u32[]{:S(2)}, u32[]{:S(2)}) collective-permute-start(f16[384,384]{1,0:T(8,128)(2,1)} %get-tuple-element.44), channel_id=1, source_target_pairs={{0,2},{2,0},{4,6},{6,4},{1,3},{3,1},{5,7},{7,5},{8,10},{10,8},{12,... | collective-permute-start | bytes 884744 | tf_op jit(solution)/shard_map/ppermute | solution.py:65
  27.9 7.8 %collective-permute-start.2 = (f16[384,384]{1,0:T(8,128)(2,1)S(1)}, f16[384,384]{1,0:T(8,128)(2,1)S(1)}, u32[]{:S(2)}, u32[]{:S(2)}) collective-permute-start(f16[384,384]{1,0:T(8,128)(2,1)S(1)} %get-tuple-element.35), channel_id=1, source_target_pairs={{0,4},{2,6},{4,0},{6,2},{1,5},{3,7},{5,1},{7,3},{8,12},{10,14},{12... | collective-permute-start | bytes 884744 | tf_op jit(solution)/shard_map/ppermute | solution.py:71
  29.3 13.2 %collective-permute-start.10 = (f16[384,384]{1,0:T(8,128)(2,1)}, f16[384,384]{1,0:T(8,128)(2,1)S(1)}, u32[]{:S(2)}, u32[]{:S(2)}) collective-permute-start(f16[384,384]{1,0:T(8,128)(2,1)} %get-tuple-element.40), channel_id=1, source_target_pairs={{0,2},{2,0},{4,6},{6,4},{1,3},{3,1},{5,7},{7,5},{8,10},{10,8},{12,... | collective-permute-start | bytes 884744 | tf_op jit(solution)/shard_map/ppermute | solution.py:65
  31.7 11.3 %collective-permute-start.15 = (f16[384,384]{1,0:T(8,128)(2,1)S(1)}, f16[384,384]{1,0:T(8,128)(2,1)S(1)}, u32[]{:S(2)}, u32[]{:S(2)}) collective-permute-start(f16[384,384]{1,0:T(8,128)(2,1)S(1)} %get-tuple-element.34), channel_id=1, source_target_pairs={{0,8},{8,0},{16,24},{24,16},{1,9},{9,1},{17,25},{25,17},{2,10},{10... | collective-permute-start | bytes 884744 | tf_op jit(solution)/shard_map/ppermute | solution.py:110
  37.0 12.2 %collective-permute-start.8 = (f16[384,384]{1,0:T(8,128)(2,1)S(1)}, f16[384,384]{1,0:T(8,128)(2,1)S(1)}, u32[]{:S(2)}, u32[]{:S(2)}) collective-permute-start(f16[384,384]{1,0:T(8,128)(2,1)S(1)} %convert_select_fusion.1), channel_id=1, source_target_pairs={{0,8},{8,0},{16,24},{24,16},{1,9},{9,1},{17,25},{25,17},{2,10},{10... | collective-permute-start | bytes 884744 | tf_op jit(solution)/shard_map/ppermute | solution.py:110
  38.6 16.4 %collective-permute-start.9 = (f16[384,384]{1,0:T(8,128)(2,1)S(1)}, f16[384,384]{1,0:T(8,128)(2,1)S(1)}, u32[]{:S(2)}, u32[]{:S(2)}) collective-permute-start(f16[384,384]{1,0:T(8,128)(2,1)S(1)} %get-tuple-element.41), channel_id=1, source_target_pairs={{0,2},{2,0},{4,6},{6,4},{1,3},{3,1},{5,7},{7,5},{8,10},{10,8},{12,... | collective-permute-start | bytes 884744 | tf_op jit(solution)/shard_map/ppermute | solution.py:65
  52.0 7.8 %collective-permute-start.11 = (f16[384,384]{1,0:T(8,128)(2,1)S(1)}, f16[384,384]{1,0:T(8,128)(2,1)S(1)}, u32[]{:S(2)}, u32[]{:S(2)}) collective-permute-start(f16[384,384]{1,0:T(8,128)(2,1)S(1)} %get-tuple-element.53), channel_id=1, source_target_pairs={{0,4},{2,6},{4,0},{6,2},{1,5},{3,7},{5,1},{7,3},{8,12},{10,14},{12... | collective-permute-start | bytes 884744 | tf_op jit(solution)/shard_map/ppermute | solution.py:71
  54.0 10.9 %collective-permute-start.22 = (f32[4,1664]{1,0:T(4,128)S(1)}, f32[4,1664]{1,0:T(4,128)S(1)}, u32[]{:S(2)}, u32[]{:S(2)}) collective-permute-start(f32[4,1664]{1,0:T(4,128)S(1)} %bitcast.66), channel_id=1, source_target_pairs={{0,2},{2,0},{4,6},{6,4},{1,3},{3,1},{5,7},{7,5},{8,10},{10,8},{12,... | collective-permute-start | bytes 79880 | tf_op jit(solution)/shard_map/ppermute | solution.py:38
  61.0 9.1 %collective-permute-start.17 = (f16[384,384]{1,0:T(8,128)(2,1)S(1)}, f16[384,384]{1,0:T(8,128)(2,1)S(1)}, u32[]{:S(2)}, u32[]{:S(2)}) collective-permute-start(f16[384,384]{1,0:T(8,128)(2,1)S(1)} %convert_select_fusion), channel_id=1, source_target_pairs={{0,8},{8,0},{16,24},{24,16},{1,9},{9,1},{17,25},{25,17},{2,10},{10... | collective-permute-start | bytes 884744 | tf_op jit(solution)/shard_map/ppermute | solution.py:110
  64.9 8.7 %collective-permute-start.23 = (f32[4,1664]{1,0:T(4,128)S(1)}, f32[4,1664]{1,0:T(4,128)S(1)}, u32[]{:S(2)}, u32[]{:S(2)}) collective-permute-start(f32[4,1664]{1,0:T(4,128)S(1)} %bitcast_add_fusion.8), channel_id=1, source_target_pairs={{0,4},{2,6},{4,0},{6,2},{1,5},{3,7},{5,1},{7,3},{8,12},{10,14},{12... | collective-permute-start | bytes 79880 | tf_op jit(solution)/shard_map/ppermute | solution.py:38
  65.1 14.2 %collective-permute-start.18 = (f16[384,384]{1,0:T(8,128)(2,1)S(1)}, f16[384,384]{1,0:T(8,128)(2,1)S(1)}, u32[]{:S(2)}, u32[]{:S(2)}) collective-permute-start(f16[384,384]{1,0:T(8,128)(2,1)S(1)} %get-tuple-element.55), channel_id=1, source_target_pairs={{8,16},{16,8},{9,17},{17,9},{10,18},{18,10},{11,19},{19,11},{12,20... | collective-permute-start | bytes 884744 | tf_op jit(solution)/shard_map/ppermute | solution.py:113
  80.6 9.2 %collective-permute-start.21 = (f16[384,384]{1,0:T(8,128)(2,1)S(1)}, f16[384,384]{1,0:T(8,128)(2,1)S(1)}, u32[]{:S(2)}, u32[]{:S(2)}) collective-permute-start(f16[384,384]{1,0:T(8,128)(2,1)S(1)} %add_convert_fusion), channel_id=1, source_target_pairs={{0,8},{8,0},{16,24},{24,16},{1,9},{9,1},{17,25},{25,17},{2,10},{10... | collective-permute-start | bytes 884744 | tf_op jit(solution)/shard_map/ppermute | solution.py:110
  108.9 33.0 %collective-permute-start.29 = (bf16[1536,384]{1,0:T(8,128)(2,1)S(1)}, bf16[1536,384]{1,0:T(8,128)(2,1)}, u32[]{:S(2)}, u32[]{:S(2)}) collective-permute-start(bf16[1536,384]{1,0:T(8,128)(2,1)S(1)} %get-tuple-element.13), channel_id=1, source_target_pairs={{0,2},{2,0},{4,6},{6,4},{1,3},{3,1},{5,7},{7,5},{8,10},{10,8},{12,... | collective-permute-start | bytes 3538952 | tf_op jit(solution)/shard_map/ppermute | solution.py:65
  112.6 8.9 %collective-permute-start.30 = (bf16[384,384]{1,0:T(8,128)(2,1)}, bf16[384,384]{1,0:T(8,128)(2,1)}, u32[]{:S(2)}, u32[]{:S(2)}) collective-permute-start(bf16[384,384]{1,0:T(8,128)(2,1)} %get-tuple-element.51), channel_id=1, source_target_pairs={{0,4},{2,6},{4,0},{6,2},{1,5},{3,7},{5,1},{7,3},{8,12},{10,14},{12... | collective-permute-start | bytes 884744 | tf_op jit(solution)/shard_map/ppermute | solution.py:71
  112.7 15.2 %collective-permute-start.32 = (bf16[384,384]{1,0:T(8,128)(2,1)}, bf16[384,384]{1,0:T(8,128)(2,1)}, u32[]{:S(2)}, u32[]{:S(2)}) collective-permute-start(bf16[384,384]{1,0:T(8,128)(2,1)} %get-tuple-element.50), channel_id=1, source_target_pairs={{0,4},{2,6},{4,0},{6,2},{1,5},{3,7},{5,1},{7,3},{8,12},{10,14},{12... | collective-permute-start | bytes 884744 | tf_op jit(solution)/shard_map/ppermute | solution.py:71
  114.1 20.1 %collective-permute-start.34 = (bf16[384,384]{1,0:T(8,128)(2,1)}, bf16[384,384]{1,0:T(8,128)(2,1)}, u32[]{:S(2)}, u32[]{:S(2)}) collective-permute-start(bf16[384,384]{1,0:T(8,128)(2,1)} %get-tuple-element.49), channel_id=1, source_target_pairs={{0,4},{2,6},{4,0},{6,2},{1,5},{3,7},{5,1},{7,3},{8,12},{10,14},{12... | collective-permute-start | bytes 884744 | tf_op jit(solution)/shard_map/ppermute | solution.py:71
  114.2 26.4 %collective-permute-start.36 = (bf16[384,384]{1,0:T(8,128)(2,1)}, bf16[384,384]{1,0:T(8,128)(2,1)}, u32[]{:S(2)}, u32[]{:S(2)}) collective-permute-start(bf16[384,384]{1,0:T(8,128)(2,1)} %get-tuple-element.48), channel_id=1, source_target_pairs={{0,4},{2,6},{4,0},{6,2},{1,5},{3,7},{5,1},{7,3},{8,12},{10,14},{12... | collective-permute-start | bytes 884744 | tf_op jit(solution)/shard_map/ppermute | solution.py:71
  121.6 26.7 %collective-permute-start.31 = (bf16[384,384]{1,0:T(8,128)(2,1)}, bf16[384,384]{1,0:T(8,128)(2,1)S(1)}, u32[]{:S(2)}, u32[]{:S(2)}) collective-permute-start(bf16[384,384]{1,0:T(8,128)(2,1)} %collective-permute-done.30), channel_id=1, source_target_pairs={{0,2},{2,0},{4,6},{6,4},{1,3},{3,1},{5,7},{7,5},{8,10},{10,8},{12,... | collective-permute-start | bytes 884744 | tf_op jit(solution)/shard_map/ppermute | solution.py:65
  127.9 29.1 %collective-permute-start.33 = (bf16[384,384]{1,0:T(8,128)(2,1)}, bf16[384,384]{1,0:T(8,128)(2,1)S(1)}, u32[]{:S(2)}, u32[]{:S(2)}) collective-permute-start(bf16[384,384]{1,0:T(8,128)(2,1)} %collective-permute-done.32), channel_id=1, source_target_pairs={{0,2},{2,0},{4,6},{6,4},{1,3},{3,1},{5,7},{7,5},{8,10},{10,8},{12,... | collective-permute-start | bytes 884744 | tf_op jit(solution)/shard_map/ppermute | solution.py:65
  134.2 31.5 %collective-permute-start.35 = (bf16[384,384]{1,0:T(8,128)(2,1)}, bf16[384,384]{1,0:T(8,128)(2,1)S(1)}, u32[]{:S(2)}, u32[]{:S(2)}) collective-permute-start(bf16[384,384]{1,0:T(8,128)(2,1)} %collective-permute-done.34), channel_id=1, source_target_pairs={{0,2},{2,0},{4,6},{6,4},{1,3},{3,1},{5,7},{7,5},{8,10},{10,8},{12,... | collective-permute-start | bytes 884744 | tf_op jit(solution)/shard_map/ppermute | solution.py:65
  140.5 33.7 %collective-permute-start.37 = (bf16[384,384]{1,0:T(8,128)(2,1)}, bf16[384,384]{1,0:T(8,128)(2,1)S(1)}, u32[]{:S(2)}, u32[]{:S(2)}) collective-permute-start(bf16[384,384]{1,0:T(8,128)(2,1)} %collective-permute-done.36), channel_id=1, source_target_pairs={{0,2},{2,0},{4,6},{6,4},{1,3},{3,1},{5,7},{7,5},{8,10},{10,8},{12,... | collective-permute-start | bytes 884744 | tf_op jit(solution)/shard_map/ppermute | solution.py:65
  (20 other events, 175.4 us)

commit v2 on v0

v2 whole, which is shorter than its diff:
```python
import math

import jax
import jax.numpy as jnp
from jax import lax
from jax.experimental import pallas as pl
from jax.experimental.pallas import tpu as pltpu
from jax.sharding import PartitionSpec as P

D = 1536
INNER = 3072
CONV = 3328
KCONV = 4

CORES = 2
CHUNKS = 3
LANES = 128
F16_SAFE_REPLICAS = 16
PARAMS = pltpu.CompilerParams(vmem_limit_bytes=16 * 2**20)
LARGE = pltpu.CompilerParams(vmem_limit_bytes=57 * 2**20)
SMALL = pl.CostEstimate(flops=1, bytes_accessed=1024, transcendentals=1)


def adamw_step(param_in, first_in, second_in, grad_in):
    first_out = 0.9 * first_in + 0.1 * grad_in
    second_out = 0.95 * second_in + 0.05 * grad_in * grad_in
    bias_one = 1.0 - 0.9**10
    bias_two = 1.0 - 0.95**10
    update = first_out / bias_one / (jnp.sqrt(second_out / bias_two) + 1e-08)
    param_out = param_in - 0.25 * (update + 0.1 * param_in)
    return (param_out, first_out, second_out)


def clip_from(square_sum):
    clip_limit = 0.5 * math.sqrt(INNER * D + KCONV * CONV)
    return jnp.minimum(1.0, clip_limit / (jnp.sqrt(square_sum) + 1e-06))


def exchange(value, axis, step):
    return lax.ppermute(value, axis, [(i, i ^ step) for i in range(lax.axis_size(axis))])


def steps_of(axis, first=1):
    steps = []
    while first < lax.axis_size(axis):
        steps.append((axis, first))
        first *= 2
    return steps


def widen(x):
    return x.astype(jnp.float32)


def narrow(x):
    return x.astype(jnp.float16)


def together(*values):
    return lax.optimization_barrier(values)


def columns_of(grad, owners, cols):
    rows, width = grad.shape
    if cols % LANES or rows % 8:
        return [lax.dynamic_slice(grad, (0, owner * cols), (rows, cols)) for owner in owners]
    steps = 6
    part = rows // steps

    def kernel(owners_ref, grad_ref, *outs):
        for k, out in enumerate(outs):
            out[...] = grad_ref[:, pl.ds(pl.multiple_of(owners_ref[k] * cols, LANES), cols)]

    return pl.pallas_call(
        kernel,
        grid=(steps,),
        in_specs=[pl.BlockSpec(memory_space=pltpu.SMEM), pl.BlockSpec((part, width), lambda i: (i, 0))],
        out_specs=[pl.BlockSpec((part, cols), lambda i: (i, 0))] * len(owners),
        out_shape=[jax.ShapeDtypeStruct((rows, cols), jnp.float32)] * len(owners),
        cost_estimate=SMALL,
        compiler_params=LARGE,
    )(jnp.stack(owners).astype(jnp.int32), grad)


def step_state(avgs, clip, param, first, second):
    rows, cols = param.shape
    chunks = len(avgs)
    part = rows // chunks

    def kernel(clip_ref, p_ref, m_ref, v_ref, *refs):
        p_out, m_out, v_out = refs[-3:]
        for k in range(chunks):

            @pl.when(pl.program_id(0) == k)
            def _():
                p, m, v = adamw_step(p_ref[...], m_ref[...], v_ref[...], clip_ref[0, 0] * refs[k][...])
                p_out[...], m_out[...], v_out[...] = p, m, v

    chunk = pl.BlockSpec((part, cols), lambda i: (i, 0))
    return pl.pallas_call(
        kernel,
        grid=(chunks,),
        in_specs=[pl.BlockSpec(memory_space=pltpu.SMEM)]
        + [chunk] * 3
        + [pl.BlockSpec((part, cols), lambda i: (0, 0))] * chunks,
        out_specs=[chunk] * 3,
        out_shape=[jax.ShapeDtypeStruct((rows, cols), jnp.float32)] * 3,
        cost_estimate=SMALL,
        compiler_params=PARAMS,
    )(clip, param, first, second, *avgs)


def place(full, shape, row_block, chip, core, mine, theirs):
    part, cols = mine.shape
    where = jnp.stack([jnp.int32(x) for x in (row_block, chip, core)])

    def kernel(where_ref, mine_ref, theirs_ref, *refs):
        out_ref = refs[-1]

        @pl.when(where_ref[2] == 0)
        def _():
            out_ref[:, :cols] = mine_ref[...]
            out_ref[:, cols:] = theirs_ref[...]

        @pl.when(where_ref[2] != 0)
        def _():
            out_ref[:, :cols] = theirs_ref[...]
            out_ref[:, cols:] = mine_ref[...]

    block = pl.BlockSpec((part, cols), lambda i, where: (0, 0))
    so_far = [] if full is None else [full]
    return pl.pallas_call(
        kernel,
        grid_spec=pltpu.PrefetchScalarGridSpec(
            num_scalar_prefetch=1,
            grid=(1,),
            in_specs=[block, block] + [pl.BlockSpec(memory_space=pl.ANY)] * len(so_far),
            out_specs=pl.BlockSpec((part, CORES * cols), lambda i, where: (where[0], where[1])),
        ),
        out_shape=jax.ShapeDtypeStruct(shape, jnp.bfloat16),
        input_output_aliases={3: 0} if so_far else {},
        cost_estimate=SMALL,
        compiler_params=PARAMS,
    )(where, mine, theirs, *so_far)


def average(so_far, ema, chip, core, mine, theirs):
    rows, width = ema.shape
    cols = mine.shape[1]
    where = jnp.stack([chip, core]).astype(jnp.int32)

    def kernel(where_ref, ema_ref, mine_ref, theirs_ref, *refs):
        out_ref = refs[-1]
        for c in range(CORES):

            @pl.when(where_ref[1] == c)
            def _():
                for k, ref in enumerate((mine_ref, theirs_ref) if c == 0 else (theirs_ref, mine_ref)):
                    at = slice(k * cols, (k + 1) * cols)
                    out_ref[:, at] = 0.9 * ema_ref[:, at] + 0.1 * widen(ref[...])

    so_far = [] if so_far is None else [so_far]
    block = pl.BlockSpec((rows, CORES * cols), lambda i, where: (0, where[0]))
    piece = pl.BlockSpec((rows, cols), lambda i, where: (0, 0))
    return pl.pallas_call(
        kernel,
        grid_spec=pltpu.PrefetchScalarGridSpec(
            num_scalar_prefetch=1,
            grid=(1,),
            in_specs=[block, piece, piece] + [pl.BlockSpec(memory_space=pl.ANY)] * len(so_far),
            out_specs=block,
        ),
        out_shape=jax.ShapeDtypeStruct(ema.shape, jnp.float32),
        input_output_aliases={4: 0} if so_far else {},
        cost_estimate=SMALL,
        compiler_params=PARAMS,
    )(where, ema, mine, theirs, *so_far)


def body(grad_proj, grad_conv, param_proj, m_proj, v_proj, ema_proj, param_conv, m_conv, v_conv):
    reps, owners = lax.axis_size("rep"), lax.axis_size("dp")
    replica_count = reps * owners
    chips = owners // CORES
    rows, cols = param_proj.shape
    shape = (rows, cols * owners)
    me = lax.axis_index("dp")
    chip, core = me // CORES, me % CORES
    rep = lax.axis_index("rep")
    part_rows = rows // CHUNKS
    aligned = cols % LANES == 0 and part_rows % 16 == 0

    def core_swap(x):
        return exchange(x, "dp", 1)

    def chip_shift(x, off):
        pairs = [
            (a * CORES + c, ((a + off) % chips) * CORES + c) for a in range(chips) for c in range(CORES)
        ]
        return lax.ppermute(x, "dp", pairs)

    def chunk(x, i):
        return x[i * part_rows : (i + 1) * part_rows]

    scale = 1.0 / max(1, 2 ** math.ceil(math.log2(replica_count / F16_SAFE_REPLICAS)))
    inverse = 1.0 / (replica_count * scale)
    grad = grad_proj[0]

    def scaled(x):
        return x * scale if scale != 1.0 else x

    others = [(chip + off) % chips for off in range(1, chips)]
    owners_needed = [other * CORES + 1 - core for other in (*others, chip)]
    owners_needed += [other * CORES + core for other in (*others, chip)]
    blocks = columns_of(grad, owners_needed, cols)
    to_swap, to_keep = blocks[:chips], blocks[chips:]
    conv_steps = [*steps_of("rep"), ("dp", 1), *steps_of("dp", CORES)]
    conv_sum = grad_conv[0]

    def conv_hop(first=None):
        sent = conv_sum if first is None else together(conv_sum, first)[0]
        return sent, exchange(sent, *conv_steps.pop(0))

    spans = [(0, part_rows), (part_rows, rows)]
    to_send = [[] for _ in others]
    last = None
    for start, stop in spans:
        swapped = [core_swap(x[start:stop]) for x in to_swap[:-1]]
        own_conv, got_conv = conv_hop(last)
        *swapped, own_conv, got_conv = together(*swapped, own_conv, got_conv)
        conv_sum = own_conv + got_conv
        for n, got in enumerate(swapped):
            last = narrow(scaled(to_keep[n][start:stop] + got))
            to_send[n].append(last)
    own_conv, got_conv = conv_hop(last)
    own_keep, got = together(to_keep[-1], core_swap(to_swap[-1]))
    own_sum = scaled(own_keep + got)

    def outgoing(n, i):
        return to_send[n][0] if i == 0 else to_send[n][1][(i - 1) * part_rows : i * part_rows]

    avgs, squares = [None] * CHUNKS, [None] * CHUNKS
    sums, halves, totals = {}, {}, {}
    is_end = (rep == 0) | (rep == 3)
    moving = {}

    def set_average(i, total):
        avgs[i] = total * inverse
        squares[i] = jnp.sum(avgs[i] * avgs[i], axis=0, keepdims=True)

    for r in range(CHUNKS + 3 if reps == 4 else CHUNKS + 1):
        if r == 1:
            moving["own_conv"], moving["conv"] = own_conv, got_conv
        names = list(moving)
        there = dict(zip(names, together(*[moving[k] for k in names]))) if names else {}
        moving = {}
        own = chunk(own_sum, r - 1) if 0 <= r - 1 < CHUNKS else None
        if own is not None:
            for n in range(len(others)):
                own = own + widen(there["chips", n])
            sums[r - 1] = narrow(own) if reps == 4 else own
        if "pair" in there:
            i = r - 2
            if i < CHUNKS:
                halves[i] = narrow(widen(sums[i]) + widen(there["pair"]))
            if i >= 2:
                set_average(i - 2, widen(jnp.where(is_end, there["pair"], totals[i - 2])))
                if i - 2 < CHUNKS - 1:
                    moving["square"] = squares[i - 2]
        if "middle" in there:
            i = r - 3
            totals[i] = narrow(widen(halves[i]) + widen(there["middle"]))
        if "conv" in there:
            conv_sum = there["own_conv"] + there["conv"]
        if "square" in there:
            squares[r - 5] = there["square"]

        if r < CHUNKS:
            for n in range(len(others)):
                payload = outgoing(n, r)
                if there:
                    payload = together(payload, next(iter(there.values())))[0]
                moving["chips", n] = chip_shift(payload, n + 1)
        if reps == 4:
            i = r - 1
            if 0 <= i < CHUNKS + 2:
                if i < 2:
                    payload = sums[i]
                elif i < CHUNKS:
                    payload = jnp.where(is_end, sums[i], totals[i - 2])
                else:
                    payload = totals[i - 2]
                moving["pair"] = lax.ppermute(payload, "rep", [(0, 1), (1, 0), (2, 3), (3, 2)])
            if 0 <= r - 2 < CHUNKS:
                moving["middle"] = lax.ppermute(halves[r - 2], "rep", [(1, 2), (2, 1)])
        if conv_steps and r >= 2:
            moving["own_conv"], moving["conv"] = conv_hop()
    if reps == 4:
        for name in ("pair",):
            got = moving[name]
        set_average(CHUNKS - 1, widen(jnp.where(is_end, got, totals[CHUNKS - 1])))
    else:
        for i in range(CHUNKS):
            set_average(i, lax.psum(sums[i], "rep"))
    while conv_steps:
        conv_sum = sum(conv_hop())
    conv_avg = conv_sum / replica_count
    conv_square = jnp.sum(conv_avg * conv_avg)

    square = sum(squares[1:], squares[0])
    square = square + jnp.where(me == 0, conv_square, 0.0) * (lax.broadcasted_iota(jnp.int32, square.shape, 1) == 0)
    for step in [*steps_of("dp"), *steps_of("tensor")]:
        square = square + exchange(square, *step)
    clip_factor = clip_from(jnp.sum(square, keepdims=True))

    def new_weights(i):
        return adamw_step(chunk(param_proj, i), chunk(m_proj, i), chunk(v_proj, i), clip_factor * avgs[i])[0]

    if not (aligned and chips == 2 and reps % 2 == 0 and CHUNKS == 3):
        weights = [new_weights(i).astype(jnp.bfloat16) for i in range(CHUNKS)]
        weights = jnp.concatenate(weights, axis=0)
        full = jnp.zeros(shape, jnp.bfloat16)
        for piece, owner in ((weights, me), (core_swap(weights), me ^ 1)):
            full = lax.dynamic_update_slice(full, piece, (0, owner * cols))
        for off in range(1, chips):
            got = chip_shift(weights, off)
            from_chip = (chip - off) % chips
            for piece, owner in ((got, from_chip * CORES + core), (core_swap(got), from_chip * CORES + 1 - core)):
                full = lax.dynamic_update_slice(full, piece, (0, owner * cols))
        results = adamw_step(param_proj, m_proj, v_proj, clip_factor * jnp.concatenate(avgs))
        conv_results = adamw_step(param_conv, m_conv, v_conv, clip_factor * conv_avg)
        ema_count = ema_proj.shape[0]
        row_block = lax.dynamic_slice_in_dim(full, me * ema_count, ema_count, 0)
        return (*results, 0.9 * ema_proj + 0.1 * widen(row_block), full, *conv_results)

    odd = rep % 2 == 1

    def either(values):
        return jnp.where(odd, values[1], values[0])

    inputs = [[chunk(x, i) for i in range(CHUNKS)] for x in (param_proj, m_proj, v_proj)] + [avgs]
    p, m, v, g = (either(values) for values in inputs)
    first = adamw_step(p, m, v, clip_factor * g)[0].astype(jnp.bfloat16)
    got_first = chip_shift(first, 1)
    clip, _ = together(clip_factor, first)
    p, m, v, g = (values[2] for values in inputs)
    third = adamw_step(p, m, v, clip * g)[0].astype(jnp.bfloat16)
    clip, _ = together(clip, third)
    results = step_state(avgs, clip, param_proj, m_proj, v_proj)
    weights = results[0].astype(jnp.bfloat16)
    weights, got_first, third = together(weights, got_first, third)

    got_third = chip_shift(third, 1)
    got_second = exchange(got_first, "rep", 1)
    got_first_other = core_swap(got_first)
    partner = core_swap(weights)
    full = None
    for i in range(CHUNKS):
        full = place(full, shape, i, chip, core, chunk(weights, i), chunk(partner, i))
    ema_rows = ema_proj.shape[0]

    def for_average(x):
        return lax.dynamic_slice_in_dim(x, me * ema_rows, ema_rows, 0)

    new_ema = average(None, ema_proj, chip, core, for_average(weights), for_average(partner))
    clip, _ = together(clip, new_ema)
    conv_results = adamw_step(param_conv, m_conv, v_conv, clip * conv_avg)
    got_first, got_first_other, _ = together(got_first, got_first_other, conv_results[0])
    full = place(full, shape, jnp.where(odd, 1, 0), 1 - chip, core, got_first, got_first_other)
    got_third, got_second, full = together(got_third, got_second, full)
    got_third_other, got_second_other = core_swap(got_third), core_swap(got_second)
    full = place(full, shape, jnp.where(odd, 0, 1), 1 - chip, core, got_second, got_second_other)
    full = place(full, shape, 2, 1 - chip, core, got_third, got_third_other)

    def assembled(a, b, c):
        return for_average(jnp.concatenate([jnp.where(odd, b, a), jnp.where(odd, a, b), c]))

    new_ema = average(
        new_ema,
        ema_proj,
        1 - chip,
        core,
        assembled(got_first, got_second, got_third),
        assembled(got_first_other, got_second_other, got_third_other),
    )
    return (*results, new_ema, full, *conv_results)


def solution(mesh):
    in_specs = (
        P(("rep", "dp"), "tensor", None),
        P(("rep", "dp"), None, "tensor"),
        P("tensor", "dp"),
        P("tensor", "dp"),
        P("tensor", "dp"),
        P(("tensor", "dp"), None),
        P(None, "tensor"),
        P(None, "tensor"),
        P(None, "tensor"),
    )
    out_specs = (
        P("tensor", "dp"),
        P("tensor", "dp"),
        P("tensor", "dp"),
        P(("tensor", "dp"), None),
        P("tensor", None),
        P(None, "tensor"),
        P(None, "tensor"),
        P(None, "tensor"),
    )
    return jax.shard_map(body, mesh=mesh, in_specs=in_specs, out_specs=out_specs, check_vma=False)
```

time: 265 us -> 143 us (0.54)
  waiting for transfers between devices: 157 us -> 35.1 us
  blocking collectives: 73.2 us -> 0 us
  starting transfers between devices: 0.11 us -> 44.1 us
  Pallas kernels: 0 us -> 25.6 us
  between operations: 15.9 us -> 2.32 us
  other arithmetic: 15.9 us -> 25.7 us
  local copies, waits for them, and re-layouts: 2.22 us -> 9.52 us
    reduce_scatter x1 -> x0, waiting for transfers between devices: 83.2 us -> none  [body(): lax.psum_scatter(grad_proj[0], 'dp', scatter_dimension=1, tiled=True)]
    psum x2 -> x0, blocking collectives: 73.2 us -> none  [the longest x1 58.9 us: body(): conv_avg = lax.psum(grad_conv[0], ('rep', 'dp')) / replica_count]
    ppermute x0 -> x28, starting transfers between devices: none -> 44.1 us  [the longest x15 23.4 us: exchange(): lax.ppermute(value, axis, [(i, i ^ step) for i in range(lax.axis_size(axi...]
    psum x1 -> x0, waiting for transfers between devices: 38.1 us -> none  [body(): proj_avg = lax.psum(owner_sum, 'rep') / replica_count]
    all_gather x1 -> x0, waiting for transfers between devices: 35.2 us -> none  [body(): lax.all_gather(new_param_proj.astype(jnp.bfloat16), 'dp', axis=1, tiled=T...]
    ppermute x0 -> x28, waiting for transfers between devices: none -> 35.1 us  [the longest x15 13.1 us: exchange(): lax.ppermute(value, axis, [(i, i ^ step) for i in range(lax.axis_size(axi...]
    pallas_call x0 -> x10, Pallas kernels: none -> 25.6 us  [the longest x6 9.21 us: place(): pl.pallas_call(kernel, grid_spec=pltpu.PrefetchScalarGridSpec(num_scalar_...]
    slice x0 -> x5, local copies, waits for them, and re-layouts: none -> 6.46 us  [the longest x2 2.84 us: body(): swapped = [core_swap(x[start:stop]) for x in to_swap[:-1]]]
  transfers between devices with their start and end apart: 3 -> 28, of which waited for: 3 -> 14; matrix products, arithmetic and copies ran while one was open for 0% -> 17% of each run, Pallas kernels for 0% -> 8%
where the time goes in v2:
time: 143 us; the launch traced here: 142 us
  starting transfers between devices  44.1 us (31%)
  waiting for transfers between devices  35.1 us (25%)
  other arithmetic  25.7 us (18%)
  Pallas kernels  25.6 us (18%)
  local copies, waits for them, and re-layouts  9.52 us (7%)
  between operations  2.32 us (2%)
    ppermute x15, starting transfers between devices, exchange(): lax.ppermute(value, axis, [(i, i ^ step) for i in range(lax.axis_size(axi...  23.4 us
    ppermute x5, starting transfers between devices, body(): lax.ppermute(payload, 'rep', [(0, 1), (1, 0), (2, 3), (3, 2)])  13.7 us
    ppermute x15, waiting for transfers between devices, exchange(): lax.ppermute(value, axis, [(i, i ^ step) for i in range(lax.axis_size(axi...  13.1 us
    ppermute x5, waiting for transfers between devices, chip_shift(): return lax.ppermute(x, 'dp', pairs)  12.4 us
    ppermute x5, waiting for transfers between devices, body(): lax.ppermute(payload, 'rep', [(0, 1), (1, 0), (2, 3), (3, 2)])  9.64 us
    pallas_call x6, Pallas kernels, place(): pl.pallas_call(kernel, grid_spec=pltpu.PrefetchScalarGridSpec(num_scalar_...  9.21 us
    pallas_call x1, Pallas kernels, columns_of(): pl.pallas_call(kernel, grid=(steps,), in_specs=[pl.BlockSpec(memory_space...  8.67 us
    convert_element_type x8, other arithmetic, narrow(): return x.astype(jnp.float16)  5.06 us
  transfers between devices with their start and end apart: 28, of which 14 were waited for; matrix products, arithmetic and copies ran while one was open for 17% of the time, Pallas kernels for 8%

profile of v2, /device:TPU:1, one launch (start us, length us, event | category | flops | bytes accessed | tf_op | source)
XLA Modules:
  0.0 142.3 jit_solution(2319438614543154489)
XLA Ops:
  1.3 8.7 %shard_map.152 = (f32[1536,384]{1,0:T(8,128)}, f32[1536,384]{1,0:T(8,128)}, f32[1536,384]{1,0:T(8,128)}, f32[1536,384]{1,0:T(8,128)}) custom-call(s32[4]{0:T(128)} %pad_add_fusion.2.owners_ref, f32[1536,1536]{1,0:T(8,128)} %bitcast.14), custom_call_target="tpu_custom_call" | custom-call | flops 1 | bytes 1024 | tf_op jit(solution)/shard_map/pallas_call | solution.py:74
  13.5 2.8 %collective-permute-start.3 = (f32[4,1664]{1,0:T(4,128)S(1)}, f32[4,1664]{1,0:T(4,128)S(1)}, u32[]{:S(2)}, u32[]{:S(2)}) collective-permute-start(f32[4,1664]{1,0:T(4,128)S(1)} %bitcast.15), channel_id=1, source_target_pairs={{0,8},{8,0},{16,24},{24,16},{1,9},{9,1},{17,25},{25,17},{2,10},{10... | collective-permute-start | bytes 79880 | tf_op jit(solution)/shard_map/ppermute | solution.py:40
  18.0 3.5 %collective-permute-start.4 = (f32[4,1664]{1,0:T(4,128)S(1)}, f32[4,1664]{1,0:T(4,128)S(1)}, u32[]{:S(2)}, u32[]{:S(2)}) collective-permute-start(f32[4,1664]{1,0:T(4,128)S(1)} %add.149), channel_id=1, source_target_pairs={{0,16},{8,24},{16,0},{24,8},{1,17},{9,25},{17,1},{25,9},{2,18},{10... | collective-permute-start | bytes 79880 | tf_op jit(solution)/shard_map/ppermute | solution.py:40
  25.2 6.3 %collective-permute-done.5 = f16[512,384]{1,0:T(8,128)(2,1)S(1)} collective-permute-done((f16[512,384]{1,0:T(8,128)(2,1)S(1)}, f16[512,384]{1,0:T(8,128)(2,1)S(1)}, u32[]{:S(2)}, u32[]{:S(2)}) %collective-permute-start.5) | collective-permute-done | bytes 393248 | tf_op jit(solution)/shard_map/ppermute | solution.py:199
  34.5 6.1 %collective-permute-done.7 = f16[512,384]{1,0:T(8,128)(2,1)S(1)} collective-permute-done((f16[512,384]{1,0:T(8,128)(2,1)S(1)}, f16[512,384]{1,0:T(8,128)(2,1)S(1)}, u32[]{:S(2)}, u32[]{:S(2)}) %collective-permute-start.7) | collective-permute-done | bytes 393248 | tf_op jit(solution)/shard_map/ppermute | solution.py:199
  43.6 2.5 %collective-permute-start.10 = (f16[512,384]{1,0:T(8,128)(2,1)}, f16[512,384]{1,0:T(8,128)(2,1)}, u32[]{:S(2)}, u32[]{:S(2)}) collective-permute-start(f16[512,384]{1,0:T(8,128)(2,1)} %fusion.17), channel_id=1, source_target_pairs={{0,8},{8,0},{16,24},{24,16},{1,9},{9,1},{17,25},{25,17},{2,10},{10... | collective-permute-start | bytes 1179656 | tf_op jit(solution)/shard_map/ppermute | solution.py:292
  48.3 6.4 %collective-permute-done.12 = f32[4,1664]{1,0:T(4,128)} collective-permute-done((f32[4,1664]{1,0:T(4,128)}, f32[4,1664]{1,0:T(4,128)}, u32[]{:S(2)}, u32[]{:S(2)}) %collective-permute-start.12) | collective-permute-done | bytes 26656 | tf_op jit(solution)/shard_map/ppermute | solution.py:40
  57.1 2.7 %collective-permute-start.13 = (f16[512,384]{1,0:T(8,128)(2,1)S(1)}, f16[512,384]{1,0:T(8,128)(2,1)S(1)}, u32[]{:S(2)}, u32[]{:S(2)}) collective-permute-start(f16[512,384]{1,0:T(8,128)(2,1)S(1)} %broadcast_select_fusion.5), channel_id=1, source_target_pairs={{0,8},{8,0},{16,24},{24,16},{1,9},{9,1},{17,25},{25,17},{2,10},{10... | collective-permute-start | bytes 1179656 | tf_op jit(solution)/shard_map/ppermute | solution.py:292
  59.9 5.2 %collective-permute-done.13 = f16[512,384]{1,0:T(8,128)(2,1)S(1)} collective-permute-done((f16[512,384]{1,0:T(8,128)(2,1)S(1)}, f16[512,384]{1,0:T(8,128)(2,1)S(1)}, u32[]{:S(2)}, u32[]{:S(2)}) %collective-permute-start.13) | collective-permute-done | bytes 393248 | tf_op jit(solution)/shard_map/ppermute | solution.py:292
  65.9 1.8 %collective-permute-start.15 = (f16[512,384]{1,0:T(8,128)(2,1)}, f16[512,384]{1,0:T(8,128)(2,1)}, u32[]{:S(2)}, u32[]{:S(2)}) collective-permute-start(f16[512,384]{1,0:T(8,128)(2,1)} %add_convert_fusion.3), channel_id=1, source_target_pairs={{0,8},{8,0},{16,24},{24,16},{1,9},{9,1},{17,25},{25,17},{2,10},{10... | collective-permute-start | bytes 1179656 | tf_op jit(solution)/shard_map/ppermute | solution.py:292
  67.6 2.2 %multiply_reduce_fusion.2 = (f32[384]{0:T(512)S(1)}, f32[512,384]{1,0:T(8,128)S(1)}, f16[512,384]{1,0:T(8,128)(2,1)}) fusion(f16[512,384]{1,0:T(8,128)(2,1)S(1)} %collective-permute-done.13, f16[512,384]{1,0:T(8,128)(2,1)} %copy-done.10, f16[512,384]{1,0:T(8,128)(2,1)S(1)} %add_convert_fusion.6, pred[]{:T(512)S(6)} %or.3, f16[512,384]{1,0:T(8,128)(2,1)} %copy-done.11, ...), kind=kLoop, calls=%fused_computation.41 | loop fusion | flops 3145344 | bytes 3540481 | tf_op jit(solution)/shard_map/reduce_sum | solution.py:248
  71.3 2.5 %collective-permute-done.15 = f16[512,384]{1,0:T(8,128)(2,1)} collective-permute-done((f16[512,384]{1,0:T(8,128)(2,1)}, f16[512,384]{1,0:T(8,128)(2,1)}, u32[]{:S(2)}, u32[]{:S(2)}) %collective-permute-start.15) | collective-permute-done | bytes 393248 | tf_op jit(solution)/shard_map/ppermute | solution.py:292
  75.0 5.3 %collective-permute-start.17 = (f16[512,384]{1,0:T(8,128)(2,1)S(1)}, f16[512,384]{1,0:T(8,128)(2,1)}, u32[]{:S(2)}, u32[]{:S(2)}) collective-permute-start(f16[512,384]{1,0:T(8,128)(2,1)S(1)} %add_convert_fusion.1), channel_id=1, source_target_pairs={{0,8},{8,0},{16,24},{24,16},{1,9},{9,1},{17,25},{25,17},{2,10},{10... | collective-permute-start | bytes 1179656 | tf_op jit(solution)/shard_map/ppermute | solution.py:292
  80.3 2.0 %multiply_reduce_fusion.3 = (f32[]{:T(128)}, f32[4,1664]{1,0:T(4,128)}) fusion(f32[4,1664]{1,0:T(4,128)} %add.156, f32[4,1664]{1,0:T(4,128)} %collective-permute-done.12), kind=kLoop, calls=%fused_computation.62 | loop fusion | flops 26623 | bytes 79876 | tf_op jit(solution)/shard_map/reduce_sum | solution.py:307
  82.9 2.0 %multiply_reduce_fusion.1 = (f32[384]{0:T(512)S(1)}, f32[512,384]{1,0:T(8,128)}) fusion(f16[512,384]{1,0:T(8,128)(2,1)} %collective-permute-done.15, f16[512,384]{1,0:T(8,128)(2,1)} %add_convert_fusion.3, pred[]{:T(512)S(6)} %or.3), kind=kLoop, calls=%fused_computation.37 | loop fusion | flops 982656 | bytes 1574401 | tf_op jit(solution)/shard_map/reduce_sum | solution.py:248
  85.6 2.0 %convert_multiply_fusion.1 = (f32[512,384]{1,0:T(8,128)}, f16[512,384]{1,0:T(8,128)(2,1)S(1)}) fusion(f16[512,384]{1,0:T(8,128)(2,1)} %collective-permute-done.17, f16[512,384]{1,0:T(8,128)(2,1)S(1)} %add_convert_fusion.1, pred[]{:T(512)S(6)} %or.3), kind=kLoop, calls=%fused_computation.10 | loop fusion | flops 589824 | bytes 1966081 | tf_op jit(solution)/shard_map/mul | solution.py:247
  88.5 7.7 %collective-permute-start.18 = (f32[1,384]{1,0:T(1,128)S(1)}, f32[1,384]{1,0:T(1,128)S(1)}, u32[]{:S(2)}, u32[]{:S(2)}) collective-permute-start(f32[1,384]{1,0:T(1,128)S(1)} %fusion.26), channel_id=1, source_target_pairs={{0,2},{2,0},{4,6},{6,4},{1,3},{3,1},{5,7},{7,5},{8,10},{10,8},{12,... | collective-permute-start | bytes 4616 | tf_op jit(solution)/shard_map/ppermute | solution.py:40
  97.2 2.2 %collective-permute-done.19 = f32[1,384]{1,0:T(1,128)S(1)} collective-permute-done((f32[1,384]{1,0:T(1,128)S(1)}, f32[1,384]{1,0:T(1,128)S(1)}, u32[]{:S(2)}, u32[]{:S(2)}) %collective-permute-start.19) | collective-permute-done | bytes 1568 | tf_op jit(solution)/shard_map/ppermute | solution.py:40
  103.2 2.8 %subtract_convert_fusion = bf16[512,384]{1,0:T(8,128)(2,1)S(1)} fusion(f32[1536,384]{1,0:T(8,128)} %v_ref.1, f32[512,384]{1,0:T(8,128)} %get-tuple-element.106.refs_1_, f32[512,384]{1,0:T(8,128)S(1)} %get-tuple-element.108.refs_0_, f32[1536,384]{1,0:T(8,128)} %m_ref.1, f32[1536,384]{1,0:T(8,128)S(1)} %copy-done, f32[]{:T(128)} %min.6, pred[]{:T(512)S(6)} %eq.35), kind=kLoop, calls=%fused_computation.34 | loop fusion | flops 4128768 | bytes 6684677 | tf_op jit(solution)/shard_map/convert_element_type | solution.py:342
  108.0 4.0 %shard_map.153 = (f32[1536,384]{1,0:T(8,128)}, f32[1536,384]{1,0:T(8,128)}, f32[1536,384]{1,0:T(8,128)}) custom-call(f32[1,1]{1,0:T(1,128)} %bitcast.6.clip_ref, f32[1536,384]{1,0:T(8,128)S(1)} %copy-done, f32[1536,384]{1,0:T(8,128)S(1)} %copy-done.1, f32[1536,384]{1,0:T(8,128)S(1)} %copy-done.2, f32[512,384]{1,0:T(8,128)S(1)} %get-tuple-element.108.refs_0_, ...), custom_call_target="tpu_custom_call" | custom-call | flops 1 | bytes 1024 | tf_op jit(solution)/shard_map/pallas_call | solution.py:100
  112.0 2.8 %convert_element_type.128 = bf16[1536,384]{1,0:T(8,128)(2,1)} convert(f32[1536,384]{1,0:T(8,128)} %get-tuple-element.45) | non-fusion elementwise | flops 589824 | bytes 3538944 | tf_op jit(solution)/shard_map/convert_element_type | solution.py:349
  114.8 2.7 %collective-permute-start.25 = (bf16[1536,384]{1,0:T(8,128)(2,1)}, bf16[1536,384]{1,0:T(8,128)(2,1)}, u32[]{:S(2)}, u32[]{:S(2)}) collective-permute-start(bf16[1536,384]{1,0:T(8,128)(2,1)} %convert_element_type.128), channel_id=1, source_target_pairs={{0,2},{2,0},{4,6},{6,4},{1,3},{3,1},{5,7},{7,5},{8,10},{10,8},{12,... | collective-permute-start | bytes 3538952 | tf_op jit(solution)/shard_map/ppermute | solution.py:40
  123.7 1.8 %shard_map.154.refs_0_ = f32[384,1536]{1,0:T(8,128)} custom-call(s32[2]{0:T(128)S(1)} %pad_add_fusion.4.where_ref, f32[384,1536]{1,0:T(8,128)S(1)} %copy-done.3, bf16[384,384]{1,0:T(8,128)(2,1)S(1)} %constant_dynamic-slice_fusion.1.mine_ref, bf16[384,384]{1,0:T(8,128)(2,1)S(1)} %constant_dynamic-slice_fusion.theirs_ref), custom_call_target="tpu_custom_call" | custom-call | flops 1 | bytes 1024 | tf_op jit(solution)/shard_map/pallas_call | solution.py:165
  138.9 1.8 %shard_map.159 = f32[384,1536]{1,0:T(8,128)} custom-call(s32[2]{0:T(128)S(1)} %pad_add_fusion.3.where_ref, f32[384,1536]{1,0:T(8,128)S(1)} %copy-done.3, bf16[384,384]{1,0:T(8,128)(2,1)S(1)} %fusion.24.mine_ref, bf16[384,384]{1,0:T(8,128)(2,1)S(1)} %fusion.22.theirs_ref, f32[384,1536]{1,0:T(8,128)} %shard_map.154.refs_0_), custom_call_target="tpu_custom_call", output_to_operand_aliasing={{}: (4, {})} | custom-call | flops 1 | bytes 1024 | tf_op jit(solution)/shard_map/pallas_call | solution.py:165
  (122 shorter events, 52.2 us)
Async XLA Ops:
  9.9 22.8 %collective-permute-start = (f32[1536,384]{1,0:T(8,128)}, f32[1536,384]{1,0:T(8,128)S(1)}, u32[]{:S(2)}, u32[]{:S(2)}) collective-permute-start(f32[1536,384]{1,0:T(8,128)} %get-tuple-element.54), channel_id=1, source_target_pairs={{0,2},{2,0},{4,6},{6,4},{1,3},{3,1},{5,7},{7,5},{8,10},{10,8},{12,... | collective-permute-start | bytes 7077896 | tf_op jit(solution)/shard_map/ppermute | solution.py:40
  11.7 11.1 %collective-permute-start.1 = (f32[1024,384]{1,0:T(8,128)S(1)}, f32[1024,384]{1,0:T(8,128)S(1)}, u32[]{:S(2)}, u32[]{:S(2)}) collective-permute-start(f32[1024,384]{1,0:T(8,128)S(1)} %slice.74), channel_id=1, source_target_pairs={{0,2},{2,0},{4,6},{6,4},{1,3},{3,1},{5,7},{7,5},{8,10},{10,8},{12,... | collective-permute-start | bytes 4718600 | tf_op jit(solution)/shard_map/ppermute | solution.py:40
  13.4 4.5 %collective-permute-start.2 = (f32[512,384]{1,0:T(8,128)S(1)}, f32[512,384]{1,0:T(8,128)S(1)}, u32[]{:S(2)}, u32[]{:S(2)}) collective-permute-start(f32[512,384]{1,0:T(8,128)S(1)} %slice.75), channel_id=1, source_target_pairs={{0,2},{2,0},{4,6},{6,4},{1,3},{3,1},{5,7},{7,5},{8,10},{10,8},{12,... | collective-permute-start | bytes 2359304 | tf_op jit(solution)/shard_map/ppermute | solution.py:40
  13.5 4.3 %collective-permute-start.3 = (f32[4,1664]{1,0:T(4,128)S(1)}, f32[4,1664]{1,0:T(4,128)S(1)}, u32[]{:S(2)}, u32[]{:S(2)}) collective-permute-start(f32[4,1664]{1,0:T(4,128)S(1)} %bitcast.15), channel_id=1, source_target_pairs={{0,8},{8,0},{16,24},{24,16},{1,9},{9,1},{17,25},{25,17},{2,10},{10... | collective-permute-start | bytes 79880 | tf_op jit(solution)/shard_map/ppermute | solution.py:40
  18.0 4.7 %collective-permute-start.4 = (f32[4,1664]{1,0:T(4,128)S(1)}, f32[4,1664]{1,0:T(4,128)S(1)}, u32[]{:S(2)}, u32[]{:S(2)}) collective-permute-start(f32[4,1664]{1,0:T(4,128)S(1)} %add.149), channel_id=1, source_target_pairs={{0,16},{8,24},{16,0},{24,8},{1,17},{9,25},{17,1},{25,9},{2,18},{10... | collective-permute-start | bytes 79880 | tf_op jit(solution)/shard_map/ppermute | solution.py:40
  21.5 10.0 %collective-permute-start.5 = (f16[512,384]{1,0:T(8,128)(2,1)S(1)}, f16[512,384]{1,0:T(8,128)(2,1)S(1)}, u32[]{:S(2)}, u32[]{:S(2)}) collective-permute-start(f16[512,384]{1,0:T(8,128)(2,1)S(1)} %add_convert_fusion.7), channel_id=1, source_target_pairs={{0,4},{2,6},{4,0},{6,2},{1,5},{3,7},{5,1},{7,3},{8,12},{10,14},{12... | collective-permute-start | bytes 1179656 | tf_op jit(solution)/shard_map/ppermute | solution.py:199
  23.0 8.5 %collective-permute-start.6 = (f32[4,1664]{1,0:T(4,128)S(1)}, f32[4,1664]{1,0:T(4,128)S(1)}, u32[]{:S(2)}, u32[]{:S(2)}) collective-permute-start(f32[4,1664]{1,0:T(4,128)S(1)} %add.152), channel_id=1, source_target_pairs={{0,2},{2,0},{4,6},{6,4},{1,3},{3,1},{5,7},{7,5},{8,10},{10,8},{12,... | collective-permute-start | bytes 79880 | tf_op jit(solution)/shard_map/ppermute | solution.py:40
  31.5 9.1 %collective-permute-start.7 = (f16[512,384]{1,0:T(8,128)(2,1)S(1)}, f16[512,384]{1,0:T(8,128)(2,1)S(1)}, u32[]{:S(2)}, u32[]{:S(2)}) collective-permute-start(f16[512,384]{1,0:T(8,128)(2,1)S(1)} %get-tuple-element.68), channel_id=1, source_target_pairs={{0,4},{2,6},{4,0},{6,2},{1,5},{3,7},{5,1},{7,3},{8,12},{10,14},{12... | collective-permute-start | bytes 1179656 | tf_op jit(solution)/shard_map/ppermute | solution.py:199
  33.1 8.9 %collective-permute-start.8 = (f16[512,384]{1,0:T(8,128)(2,1)S(1)}, f16[512,384]{1,0:T(8,128)(2,1)S(1)}, u32[]{:S(2)}, u32[]{:S(2)}) collective-permute-start(f16[512,384]{1,0:T(8,128)(2,1)S(1)} %fusion.18), channel_id=1, source_target_pairs={{0,8},{8,0},{16,24},{24,16},{1,9},{9,1},{17,25},{25,17},{2,10},{10... | collective-permute-start | bytes 1179656 | tf_op jit(solution)/shard_map/ppermute | solution.py:292
  42.1 12.6 %collective-permute-start.11 = (f16[512,384]{1,0:T(8,128)(2,1)S(1)}, f16[512,384]{1,0:T(8,128)(2,1)S(1)}, u32[]{:S(2)}, u32[]{:S(2)}) collective-permute-start(f16[512,384]{1,0:T(8,128)(2,1)S(1)} %add_convert_fusion.6), channel_id=1, source_target_pairs={{8,16},{16,8},{9,17},{17,9},{10,18},{18,10},{11,19},{19,11},{12,20... | collective-permute-start | bytes 1179656 | tf_op jit(solution)/shard_map/ppermute | solution.py:294
  43.6 11.0 %collective-permute-start.10 = (f16[512,384]{1,0:T(8,128)(2,1)}, f16[512,384]{1,0:T(8,128)(2,1)}, u32[]{:S(2)}, u32[]{:S(2)}) collective-permute-start(f16[512,384]{1,0:T(8,128)(2,1)} %fusion.17), channel_id=1, source_target_pairs={{0,8},{8,0},{16,24},{24,16},{1,9},{9,1},{17,25},{25,17},{2,10},{10... | collective-permute-start | bytes 1179656 | tf_op jit(solution)/shard_map/ppermute | solution.py:292
  46.2 8.5 %collective-permute-start.9 = (f16[512,384]{1,0:T(8,128)(2,1)}, f16[512,384]{1,0:T(8,128)(2,1)S(1)}, u32[]{:S(2)}, u32[]{:S(2)}) collective-permute-start(f16[512,384]{1,0:T(8,128)(2,1)} %get-tuple-element.70), channel_id=1, source_target_pairs={{0,4},{2,6},{4,0},{6,2},{1,5},{3,7},{5,1},{7,3},{8,12},{10,14},{12... | collective-permute-start | bytes 1179656 | tf_op jit(solution)/shard_map/ppermute | solution.py:199
  47.0 7.6 %collective-permute-start.12 = (f32[4,1664]{1,0:T(4,128)}, f32[4,1664]{1,0:T(4,128)}, u32[]{:S(2)}, u32[]{:S(2)}) collective-permute-start(f32[4,1664]{1,0:T(4,128)} %add.156), channel_id=1, source_target_pairs={{0,4},{2,6},{4,0},{6,2},{1,5},{3,7},{5,1},{7,3},{8,12},{10,14},{12... | collective-permute-start | bytes 79880 | tf_op jit(solution)/shard_map/ppermute | solution.py:40
  56.2 3.6 %collective-permute-start.14 = (f16[512,384]{1,0:T(8,128)(2,1)S(1)}, f16[512,384]{1,0:T(8,128)(2,1)S(1)}, u32[]{:S(2)}, u32[]{:S(2)}) collective-permute-start(f16[512,384]{1,0:T(8,128)(2,1)S(1)} %add_convert_fusion.4), channel_id=1, source_target_pairs={{8,16},{16,8},{9,17},{17,9},{10,18},{18,10},{11,19},{19,11},{12,20... | collective-permute-start | bytes 1179656 | tf_op jit(solution)/shard_map/ppermute | solution.py:294
  57.1 7.9 %collective-permute-start.13 = (f16[512,384]{1,0:T(8,128)(2,1)S(1)}, f16[512,384]{1,0:T(8,128)(2,1)S(1)}, u32[]{:S(2)}, u32[]{:S(2)}) collective-permute-start(f16[512,384]{1,0:T(8,128)(2,1)S(1)} %broadcast_select_fusion.5), channel_id=1, source_target_pairs={{0,8},{8,0},{16,24},{24,16},{1,9},{9,1},{17,25},{25,17},{2,10},{10... | collective-permute-start | bytes 1179656 | tf_op jit(solution)/shard_map/ppermute | solution.py:292
  65.9 7.8 %collective-permute-start.15 = (f16[512,384]{1,0:T(8,128)(2,1)}, f16[512,384]{1,0:T(8,128)(2,1)}, u32[]{:S(2)}, u32[]{:S(2)}) collective-permute-start(f16[512,384]{1,0:T(8,128)(2,1)} %add_convert_fusion.3), channel_id=1, source_target_pairs={{0,8},{8,0},{16,24},{24,16},{1,9},{9,1},{17,25},{25,17},{2,10},{10... | collective-permute-start | bytes 1179656 | tf_op jit(solution)/shard_map/ppermute | solution.py:292
  69.8 3.9 %collective-permute-start.16 = (f16[512,384]{1,0:T(8,128)(2,1)}, f16[512,384]{1,0:T(8,128)(2,1)}, u32[]{:S(2)}, u32[]{:S(2)}) collective-permute-start(f16[512,384]{1,0:T(8,128)(2,1)} %get-tuple-element.121), channel_id=1, source_target_pairs={{8,16},{16,8},{9,17},{17,9},{10,18},{18,10},{11,19},{19,11},{12,20... | collective-permute-start | bytes 1179656 | tf_op jit(solution)/shard_map/ppermute | solution.py:294
  75.0 10.6 %collective-permute-start.17 = (f16[512,384]{1,0:T(8,128)(2,1)S(1)}, f16[512,384]{1,0:T(8,128)(2,1)}, u32[]{:S(2)}, u32[]{:S(2)}) collective-permute-start(f16[512,384]{1,0:T(8,128)(2,1)S(1)} %add_convert_fusion.1), channel_id=1, source_target_pairs={{0,8},{8,0},{16,24},{24,16},{1,9},{9,1},{17,25},{25,17},{2,10},{10... | collective-permute-start | bytes 1179656 | tf_op jit(solution)/shard_map/ppermute | solution.py:292
  88.5 8.5 %collective-permute-start.18 = (f32[1,384]{1,0:T(1,128)S(1)}, f32[1,384]{1,0:T(1,128)S(1)}, u32[]{:S(2)}, u32[]{:S(2)}) collective-permute-start(f32[1,384]{1,0:T(1,128)S(1)} %fusion.26), channel_id=1, source_target_pairs={{0,2},{2,0},{4,6},{6,4},{1,3},{3,1},{5,7},{7,5},{8,10},{10,8},{12,... | collective-permute-start | bytes 4616 | tf_op jit(solution)/shard_map/ppermute | solution.py:40
  106.0 8.9 %collective-permute-start.21 = (bf16[512,384]{1,0:T(8,128)(2,1)S(1)}, bf16[512,384]{1,0:T(8,128)(2,1)S(1)}, u32[]{:S(2)}, u32[]{:S(2)}) collective-permute-start(bf16[512,384]{1,0:T(8,128)(2,1)S(1)} %subtract_convert_fusion), channel_id=1, source_target_pairs={{0,4},{2,6},{4,0},{6,2},{1,5},{3,7},{5,1},{7,3},{8,12},{10,14},{12... | collective-permute-start | bytes 1179656 | tf_op jit(solution)/shard_map/ppermute | solution.py:199
  114.8 7.8 %collective-permute-start.25 = (bf16[1536,384]{1,0:T(8,128)(2,1)}, bf16[1536,384]{1,0:T(8,128)(2,1)}, u32[]{:S(2)}, u32[]{:S(2)}) collective-permute-start(bf16[1536,384]{1,0:T(8,128)(2,1)} %convert_element_type.128), channel_id=1, source_target_pairs={{0,2},{2,0},{4,6},{6,4},{1,3},{3,1},{5,7},{7,5},{8,10},{10,8},{12,... | collective-permute-start | bytes 3538952 | tf_op jit(solution)/shard_map/ppermute | solution.py:40
  118.0 14.0 %collective-permute-start.24 = (bf16[512,384]{1,0:T(8,128)(2,1)S(1)}, bf16[512,384]{1,0:T(8,128)(2,1)S(1)}, u32[]{:S(2)}, u32[]{:S(2)}) collective-permute-start(bf16[512,384]{1,0:T(8,128)(2,1)S(1)} %collective-permute-done.21.mine_ref), channel_id=1, source_target_pairs={{0,2},{2,0},{4,6},{6,4},{1,3},{3,1},{5,7},{7,5},{8,10},{10,8},{12,... | collective-permute-start | bytes 1179656 | tf_op jit(solution)/shard_map/ppermute | solution.py:40
  118.1 15.7 %collective-permute-start.23 = (bf16[512,384]{1,0:T(8,128)(2,1)S(1)}, bf16[512,384]{1,0:T(8,128)(2,1)S(1)}, u32[]{:S(2)}, u32[]{:S(2)}) collective-permute-start(bf16[512,384]{1,0:T(8,128)(2,1)S(1)} %collective-permute-done.21.mine_ref), channel_id=1, source_target_pairs={{0,8},{8,0},{16,24},{24,16},{1,9},{9,1},{17,25},{25,17},{2,10},{10... | collective-permute-start | bytes 1179656 | tf_op jit(solution)/shard_map/ppermute | solution.py:40
  119.1 14.6 %collective-permute-start.22 = (bf16[512,384]{1,0:T(8,128)(2,1)}, bf16[512,384]{1,0:T(8,128)(2,1)S(1)}, u32[]{:S(2)}, u32[]{:S(2)}) collective-permute-start(bf16[512,384]{1,0:T(8,128)(2,1)} %fusion.20), channel_id=1, source_target_pairs={{0,4},{2,6},{4,0},{6,2},{1,5},{3,7},{5,1},{7,3},{8,12},{10,14},{12... | collective-permute-start | bytes 1179656 | tf_op jit(solution)/shard_map/ppermute | solution.py:199
  (21 other events, 119.0 us)

commit v3 on v0

v3 whole, which is shorter than its diff:
```python
import math

import jax
import jax.numpy as jnp
from jax import lax
from jax.experimental import pallas as pl
from jax.experimental.pallas import tpu as pltpu
from jax.sharding import PartitionSpec as P

D = 1536
INNER = 3072
CONV = 3328
KCONV = 4

CORES = 2
CHUNKS = 3
LANES = 128
F16_SAFE_REPLICAS = 16
PARAMS = pltpu.CompilerParams(vmem_limit_bytes=16 * 2**20)
SMALL = pl.CostEstimate(flops=1, bytes_accessed=1024, transcendentals=1)


def adamw_step(param_in, first_in, second_in, grad_in):
    first_out = 0.9 * first_in + 0.1 * grad_in
    second_out = 0.95 * second_in + 0.05 * grad_in * grad_in
    bias_one = 1.0 - 0.9**10
    bias_two = 1.0 - 0.95**10
    update = first_out / bias_one / (jnp.sqrt(second_out / bias_two) + 1e-08)
    param_out = param_in - 0.25 * (update + 0.1 * param_in)
    return (param_out, first_out, second_out)


def clip_from(square_sum):
    clip_limit = 0.5 * math.sqrt(INNER * D + KCONV * CONV)
    return jnp.minimum(1.0, clip_limit / (jnp.sqrt(square_sum) + 1e-06))


def exchange(value, axis, step):
    return lax.ppermute(value, axis, [(i, i ^ step) for i in range(lax.axis_size(axis))])


def steps_of(axis, first=1):
    steps = []
    while first < lax.axis_size(axis):
        steps.append((axis, first))
        first *= 2
    return steps


def widen(x):
    return x.astype(jnp.float32)


def narrow(x):
    return x.astype(jnp.float16)


def together(*values):
    return lax.optimization_barrier(values)


def step_state(avgs, clip, param, first, second):
    rows, cols = param.shape
    chunks = len(avgs)
    part = rows // chunks

    def kernel(clip_ref, p_ref, m_ref, v_ref, *refs):
        p_out, m_out, v_out, w_out, last_out = refs[-5:]
        for k in range(chunks):

            @pl.when(pl.program_id(0) == k)
            def _():
                p, m, v = adamw_step(p_ref[...], m_ref[...], v_ref[...], clip_ref[0, 0] * refs[k][...])
                p_out[...], m_out[...], v_out[...] = p, m, v
                w_out[...] = p.astype(jnp.bfloat16)
                last_out[...] = p.astype(jnp.bfloat16)

    chunk = pl.BlockSpec((part, cols), lambda i: (i, 0))
    alone = pl.BlockSpec((part, cols), lambda i: (0, 0))
    whole = jax.ShapeDtypeStruct((rows, cols), jnp.float32)
    return pl.pallas_call(
        kernel,
        grid=(chunks,),
        in_specs=[pl.BlockSpec(memory_space=pltpu.SMEM)] + [chunk] * 3 + [alone] * chunks,
        out_specs=[chunk] * 4 + [alone],
        out_shape=[whole, whole, whole]
        + [jax.ShapeDtypeStruct((rows, cols), jnp.bfloat16), jax.ShapeDtypeStruct((part, cols), jnp.bfloat16)],
        cost_estimate=SMALL,
        compiler_params=PARAMS,
    )(clip, param, first, second, *avgs)


def place(so_far, shape, ema, me, chip, core, pieces):
    rows, width = shape
    columns = width // 2
    cols = columns // CORES
    ema_rows = ema.shape[0]
    where = jnp.stack([jnp.int32(x) for x in (me, chip, core, *(block for block, _, _ in pieces))])
    values = [x for _, mine, theirs in pieces for x in (mine, theirs)]

    def kernel(where_ref, ema_ref, *refs):
        full_out, ema_out, near, ema_near, new_near, sems = refs[-6:]
        here = pl.ds(pl.multiple_of(where_ref[1] * columns, LANES), columns)
        load = pltpu.make_async_copy(ema_ref.at[:, here], ema_near, sems.at[0])
        load.start()
        stores = []
        for k in range(len(pieces)):
            mine, theirs = refs[2 * k], refs[2 * k + 1]
            at = pl.ds(pl.multiple_of(where_ref[3 + k] * mine.shape[0], 16), mine.shape[0])

            @pl.when(where_ref[2] == 0)
            def _():
                near[at, :cols] = mine[...]
                near[at, cols:] = theirs[...]

            @pl.when(where_ref[2] != 0)
            def _():
                near[at, :cols] = theirs[...]
                near[at, cols:] = mine[...]

            stores.append(pltpu.make_async_copy(near.at[at, :], full_out.at[at, here], sems.at[2 + k]))
            stores[-1].start()
        load.wait()
        mine_rows = near[pl.ds(pl.multiple_of(where_ref[0] * ema_rows, 16), ema_rows), :]
        new_near[...] = 0.9 * ema_near[...] + 0.1 * widen(mine_rows)
        stores.append(pltpu.make_async_copy(new_near, ema_out.at[:, here], sems.at[1]))
        stores[-1].start()
        for store in stores:
            store.wait()

    far = pl.BlockSpec(memory_space=pltpu.HBM)
    return pl.pallas_call(
        kernel,
        in_specs=[pl.BlockSpec(memory_space=pltpu.SMEM), far]
        + [pl.BlockSpec(memory_space=pltpu.VMEM)] * len(values)
        + [far] * len(so_far),
        out_specs=[far, far],
        out_shape=[jax.ShapeDtypeStruct(shape, jnp.bfloat16), jax.ShapeDtypeStruct(ema.shape, jnp.float32)],
        input_output_aliases={2 + len(values) + i: i for i in range(len(so_far))},
        scratch_shapes=[
            pltpu.VMEM((rows, columns), jnp.bfloat16),
            pltpu.VMEM((ema_rows, columns), jnp.float32),
            pltpu.VMEM((ema_rows, columns), jnp.float32),
            pltpu.SemaphoreType.DMA((2 + len(pieces),)),
        ],
        cost_estimate=SMALL,
        compiler_params=PARAMS,
    )(where, ema, *values, *so_far)


def body(grad_proj, grad_conv, param_proj, m_proj, v_proj, ema_proj, param_conv, m_conv, v_conv):
    reps, owners = lax.axis_size("rep"), lax.axis_size("dp")
    replica_count = reps * owners
    chips = owners // CORES
    rows, cols = param_proj.shape
    shape = (rows, cols * owners)
    me = lax.axis_index("dp")
    chip, core = me // CORES, me % CORES
    rep = lax.axis_index("rep")
    part_rows = rows // CHUNKS
    aligned = cols % LANES == 0 and part_rows % 16 == 0
    line = reps == 4

    def core_swap(x):
        return exchange(x, "dp", 1)

    def chip_shift(x, off):
        pairs = [
            (a * CORES + c, ((a + off) % chips) * CORES + c) for a in range(chips) for c in range(CORES)
        ]
        return lax.ppermute(x, "dp", pairs)

    def chunk(x, i):
        return x[i * part_rows : (i + 1) * part_rows]

    odd = rep % 2 == 1

    def either(values):
        return jnp.where(odd, values[1], values[0])

    scale = 1.0 / max(1, 2 ** math.ceil(math.log2(replica_count / F16_SAFE_REPLICAS)))
    inverse = 1.0 / (replica_count * scale)
    grad = grad_proj[0]

    def scaled(x):
        return x * scale if scale != 1.0 else x

    def block(owner_chip, owner_core, i):
        start = i * part_rows
        if owners != 4:
            owner = owner_chip * CORES + owner_core
            return scaled(lax.dynamic_slice(grad, (start, owner * cols), (part_rows, cols)))
        a, b, c, d = (grad[start : start + part_rows, n * cols : (n + 1) * cols] for n in range(owners))
        return scaled(jnp.where(owner_chip == 0, jnp.where(owner_core == 0, a, b), jnp.where(owner_core == 0, c, d)))

    targets = [(chip + off) % chips for off in (*range(1, chips), 0)]

    def gift(n, i):
        return core_swap(narrow(block(targets[n], 1 - core, i)))

    def chip_sum(n, i):
        return block(targets[n], core, i) + widen(gifts[n, i])

    gifts = {(n, 0): gift(n, 0) for n in range(chips)}
    gifts.update({(n, i): gift(n, i) for i in range(1, CHUNKS) for n in range(chips)})

    avgs, squares = [None] * CHUNKS, [None] * CHUNKS
    sums, halves, totals = {}, {}, {}
    is_end = (rep == 0) | (rep == 3)
    conv_steps = [*steps_of("rep"), *steps_of("dp")]
    conv_sum = grad_conv[0]
    chosen = [[chunk(x, i) for i in range(CHUNKS)] for x in (param_proj, m_proj, v_proj)]
    chosen = [either(values) for values in chosen]

    def average_of(total):
        return widen(total) * inverse

    def square_of(total):
        value = average_of(total)
        return jnp.sum(value * value, axis=0, keepdims=True)

    moving, outgoing = {}, {}
    rounds = CHUNKS + 2 if line else CHUNKS
    for r in range(rounds + 1):
        names = list(moving)
        there = dict(zip(names, together(*[moving[k] for k in names]))) if names else {}
        moving, waiting = {}, {}
        for k, value in there.items():
            if k[0] == "gift":
                gifts[k[1:]] = value
            elif k[0] == "average":
                avgs[k[1]] = value
            elif k[0] == "square":
                squares[k[1]] = value
            elif k[0] == "chosen":
                chosen[k[1]] = value
            elif k[0] == "outgoing":
                outgoing[k[1:]] = value

        if 0 <= r - 1 < CHUNKS:
            own = there["own", 2] if r == 3 else chip_sum(chips - 1, r - 1)
            for n in range(chips - 1):
                own = own + widen(there["chips", n])
            sums[r - 1] = narrow(own) if line else lax.psum(own, "rep")
        if ("pair", 0) in there:
            i = r - 2
            if i < CHUNKS:
                halves[i] = narrow(widen(sums[i]) + widen(there["pair", 0]))
            if i >= 2:
                waiting["average", i - 2] = average_of(jnp.where(is_end, there["pair", 0], totals[i - 2]))
        if ("middle", 0) in there:
            totals[r - 3] = narrow(widen(halves[r - 3]) + widen(there["middle", 0]))
            if r < rounds:
                waiting["square", r - 3] = square_of(totals[r - 3])
            else:
                squares[r - 3] = square_of(totals[r - 3])
        if ("conv", 0) in there:
            conv_sum = there["own conv", 0] + there["conv", 0]

        payloads = []
        if r < CHUNKS:
            for n in range(chips - 1):
                payloads.append(outgoing[n, r] if r else narrow(chip_sum(n, r)))
                moving["chips", n] = chip_shift(payloads[-1], n + 1)
        if r == 0:
            for k, value in gifts.items():
                if k[1] or k[0] == chips - 1:
                    moving["gift", *k] = value
        if line:
            i = r - 1
            if 0 <= i < CHUNKS + 2:
                if i < 2:
                    payload = sums[i]
                elif i < CHUNKS:
                    payload = jnp.where(is_end, sums[i], totals[i - 2])
                else:
                    payload = totals[i - 2]
                payloads.append(payload)
                moving["pair", 0] = lax.ppermute(payload, "rep", [(0, 1), (1, 0), (2, 3), (3, 2)])
            if 0 <= r - 2 < CHUNKS:
                payloads.append(halves[r - 2])
                moving["middle", 0] = lax.ppermute(halves[r - 2], "rep", [(1, 2), (2, 1)])
        if conv_steps and payloads:
            sent, *_ = together(conv_sum, *payloads)
            moving["own conv", 0] = sent
            moving["conv", 0] = exchange(sent, *conv_steps.pop(0))
        if r == 2:
            gifts[chips - 1, r] = together(gifts[chips - 1, r], moving["conv", 0])[0]
            moving["own", r] = chip_sum(chips - 1, r)
        if r + 1 < CHUNKS:
            for n in range(chips - 1):
                ready = moving["conv", 0]
                if r == 0:
                    gifts[n, 1], ready = together(moving.pop(("gift", n, 1)), ready)
                else:
                    gifts[n, r + 1], ready = together(gifts[n, r + 1], ready)
                moving["conv", 0] = ready
                moving["outgoing", n, r + 1] = narrow(chip_sum(n, r + 1))
        if r == rounds - 2:
            for n in range(len(chosen)):
                waiting["chosen", n] = chosen[n]
        moving.update(waiting)

    if not line:
        avgs = [average_of(sums[i]) for i in range(CHUNKS)]
        squares = [square_of(sums[i]) for i in range(CHUNKS)]
    for step in conv_steps:
        conv_sum = conv_sum + exchange(conv_sum, *step)
    conv_avg = conv_sum / replica_count
    conv_square = jnp.sum(conv_avg * conv_avg)

    square = sum(squares[1:], squares[0])
    square = square + jnp.where(me == 0, conv_square, 0.0) * (lax.broadcasted_iota(jnp.int32, square.shape, 1) == 0)
    hops = [*steps_of("dp"), *steps_of("tensor")]
    for step in hops if not line else hops[:-1]:
        square = square + exchange(square, *step)
    if line:
        size, step = lax.axis_size("tensor"), hops[-1][1]
        across = [(a * size + t, (a ^ 1) * size + (t ^ step)) for a in range(reps) for t in range(size)]
        theirs = lax.ppermute(square, ("rep", "tensor"), across)
        inner, other = exchange(square, "rep", 1), exchange(square, *hops[-1])
        square = jnp.where(is_end, inner, square) + jnp.where(is_end, theirs, other)
        arrived = moving["pair", 0]
        for n in range(CHUNKS - 1):
            if avgs[n] is None:
                avgs[n] = moving["average", n]
    clip_factor = clip_from(jnp.sum(square, keepdims=True))

    def last_average(after):
        if not line:
            return avgs[-1]
        return average_of(jnp.where(is_end, together(arrived, after)[0], totals[CHUNKS - 1]))

    if not (aligned and chips == 2 and reps % 2 == 0 and CHUNKS == 3):
        avgs[-1] = last_average(clip_factor)
        results = adamw_step(param_proj, m_proj, v_proj, clip_factor * jnp.concatenate(avgs))
        weights = results[0].astype(jnp.bfloat16)
        full = jnp.zeros(shape, jnp.bfloat16)
        for piece, owner in ((weights, me), (core_swap(weights), me ^ 1)):
            full = lax.dynamic_update_slice(full, piece, (0, owner * cols))
        for off in range(1, chips):
            got = chip_shift(weights, off)
            from_chip = (chip - off) % chips
            for piece, owner in ((got, from_chip * CORES + core), (core_swap(got), from_chip * CORES + 1 - core)):
                full = lax.dynamic_update_slice(full, piece, (0, owner * cols))
        conv_results = adamw_step(param_conv, m_conv, v_conv, clip_factor * conv_avg)
        ema_count = ema_proj.shape[0]
        row_block = lax.dynamic_slice_in_dim(full, me * ema_count, ema_count, 0)
        return (*results, 0.9 * ema_proj + 0.1 * widen(row_block), full, *conv_results)

    g = either(avgs)
    p, m, v = chosen
    first = adamw_step(p, m, v, clip_factor * g)[0].astype(jnp.bfloat16)
    got_first = chip_shift(first, 1)
    avgs[-1] = last_average(first)
    *results, weights, third = step_state(avgs, clip_factor, param_proj, m_proj, v_proj)
    weights, got_first, third = together(weights, got_first, third)

    got_third = chip_shift(third, 1)
    got_second = exchange(got_first, "rep", 1)
    got_first_other = core_swap(got_first)
    so_far = place([], shape, ema_proj, me, chip, core, [(0, weights, core_swap(weights))])
    clip, _ = together(clip_factor, so_far[0])
    conv_results = adamw_step(param_conv, m_conv, v_conv, clip * conv_avg)
    got_third, got_second, *_ = together(got_third, got_second, *so_far, conv_results[0])
    first_block = jnp.where(odd, 1, 0)
    pieces = [
        (first_block, got_first, got_first_other),
        (1 - first_block, got_second, core_swap(got_second)),
        (2, got_third, core_swap(got_third)),
    ]
    full, new_ema = place(so_far, shape, ema_proj, me, 1 - chip, core, pieces)
    return (*results, new_ema, full, *conv_results)


def solution(mesh):
    in_specs = (
        P(("rep", "dp"), "tensor", None),
        P(("rep", "dp"), None, "tensor"),
        P("tensor", "dp"),
        P("tensor", "dp"),
        P("tensor", "dp"),
        P(("tensor", "dp"), None),
        P(None, "tensor"),
        P(None, "tensor"),
        P(None, "tensor"),
    )
    out_specs = (
        P("tensor", "dp"),
        P("tensor", "dp"),
        P("tensor", "dp"),
        P(("tensor", "dp"), None),
        P("tensor", None),
        P(None, "tensor"),
        P(None, "tensor"),
        P(None, "tensor"),
    )
    return jax.shard_map(body, mesh=mesh, in_specs=in_specs, out_specs=out_specs, check_vma=False)
```

time: 265 us -> 126 us (0.48)
  waiting for transfers between devices: 157 us -> 30 us
  blocking collectives: 73.2 us -> 0 us
  starting transfers between devices: 0.11 us -> 46.9 us
  other arithmetic: 15.9 us -> 33.1 us
  between operations: 15.9 us -> 2.37 us
  Pallas kernels: 0 us -> 10 us
    reduce_scatter x1 -> x0, waiting for transfers between devices: 83.2 us -> none  [body(): lax.psum_scatter(grad_proj[0], 'dp', scatter_dimension=1, tiled=True)]
    psum x2 -> x0, blocking collectives: 73.2 us -> none  [the longest x1 58.9 us: body(): conv_avg = lax.psum(grad_conv[0], ('rep', 'dp')) / replica_count]
    ppermute x0 -> x33, starting transfers between devices: none -> 46.9 us  [the longest x19 24.2 us: exchange(): lax.ppermute(value, axis, [(i, i ^ step) for i in range(lax.axis_size(axi...]
    psum x1 -> x0, waiting for transfers between devices: 38.1 us -> none  [body(): proj_avg = lax.psum(owner_sum, 'rep') / replica_count]
    all_gather x1 -> x0, waiting for transfers between devices: 35.2 us -> none  [body(): lax.all_gather(new_param_proj.astype(jnp.bfloat16), 'dp', axis=1, tiled=T...]
    ppermute x0 -> x33, waiting for transfers between devices: none -> 30 us  [the longest x19 13.5 us: exchange(): lax.ppermute(value, axis, [(i, i ^ step) for i in range(lax.axis_size(axi...]
    convert_element_type x1 -> x9, other arithmetic: 7.62 us -> 20.4 us  [the longest x8 18.4 us: narrow(): return x.astype(jnp.float16)]
    pallas_call x0 -> x3, Pallas kernels: none -> 10 us  [the longest x2 5.9 us: place(): pl.pallas_call(kernel, in_specs=[pl.BlockSpec(memory_space=pltpu.SMEM), f...]
  transfers between devices with their start and end apart: 3 -> 33, of which waited for: 3 -> 14; matrix products, arithmetic and copies ran while one was open for 0% -> 18% of each run, Pallas kernels for 0% -> 5%
where the time goes in v3:
time: 126 us; the launch traced here: 125 us
  starting transfers between devices  46.9 us (37%)
  other arithmetic  33.1 us (26%)
  waiting for transfers between devices  30 us (24%)
  Pallas kernels  10 us (8%)
  local copies, waits for them, and re-layouts  2.56 us (2%)
  between operations  2.37 us (2%)
    ppermute x19, starting transfers between devices, exchange(): lax.ppermute(value, axis, [(i, i ^ step) for i in range(lax.axis_size(axi...  24.2 us
    convert_element_type x8, other arithmetic, narrow(): return x.astype(jnp.float16)  18.4 us
    ppermute x19, waiting for transfers between devices, exchange(): lax.ppermute(value, axis, [(i, i ^ step) for i in range(lax.axis_size(axi...  13.5 us
    ppermute x5, waiting for transfers between devices, chip_shift(): return lax.ppermute(x, 'dp', pairs)  11.1 us
    ppermute x5, starting transfers between devices, body(): lax.ppermute(payload, 'rep', [(0, 1), (1, 0), (2, 3), (3, 2)])  10.5 us
    pallas_call x2, Pallas kernels, place(): pl.pallas_call(kernel, in_specs=[pl.BlockSpec(memory_space=pltpu.SMEM), f...  5.9 us
    ppermute x5, starting transfers between devices, chip_shift(): return lax.ppermute(x, 'dp', pairs)  5.44 us
    ppermute x5, waiting for transfers between devices, body(): lax.ppermute(payload, 'rep', [(0, 1), (1, 0), (2, 3), (3, 2)])  5.41 us
  transfers between devices with their start and end apart: 33, of which 14 were waited for; matrix products, arithmetic and copies ran while one was open for 18% of the time, Pallas kernels for 5%

profile of v3, /device:TPU:1, one launch (start us, length us, event | category | flops | bytes accessed | tf_op | source)
XLA Modules:
  0.0 125.0 jit_solution(12863441865221061352)
XLA Ops:
  0.7 4.2 %select_convert_fusion = (f16[512,384]{1,0:T(8,128)(2,1)S(1)}, f16[512,384]{1,0:T(8,128)(2,1)S(1)}, f16[512,384]{1,0:T(8,128)(2,1)S(1)}, f16[512,384]{1,0:T(8,128)(2,1)S(1)}) fusion(pred[]{:T(512)S(6)} %eq.35, f32[1536,1536]{1,0:T(8,128)} %bitcast.10, pred[]{:T(512)S(6)} %eq.37, pred[]{:T(512)S(6)} %eq.38), kind=kLoop, calls=%fused_computation.29 | loop fusion | flops 2752512 | bytes 11010051 | tf_op jit(solution)/shard_map/convert_element_type | solution.py:55
  6.7 2.0 %add_convert_fusion.11 = f16[512,384]{1,0:T(8,128)(2,1)S(1)} fusion(f16[512,384]{1,0:T(8,128)(2,1)S(1)} %collective-permute-done, pred[]{:T(512)S(6)} %eq.35, f32[1536,1536]{1,0:T(8,128)} %bitcast.11, pred[]{:T(512)S(6)} %eq.36), kind=kLoop, calls=%fused_computation.34 | loop fusion | flops 1179648 | bytes 3932162 | tf_op jit(solution)/shard_map/convert_element_type | solution.py:55
  8.8 2.5 %collective-permute-start.7 = (f32[4,1664]{1,0:T(4,128)S(1)}, f32[4,1664]{1,0:T(4,128)S(1)}, u32[]{:S(2)}, u32[]{:S(2)}) collective-permute-start(f32[4,1664]{1,0:T(4,128)S(1)} %bitcast.17), channel_id=1, source_target_pairs={{0,8},{8,0},{16,24},{24,16},{1,9},{9,1},{17,25},{25,17},{2,10},{10... | collective-permute-start | bytes 79880 | tf_op jit(solution)/shard_map/ppermute | solution.py:39
  13.2 3.3 %add_convert_fusion.10 = (f16[512,384]{1,0:T(8,128)(2,1)S(1)}, f16[512,384]{1,0:T(8,128)(2,1)S(1)}, f16[512,384]{1,0:T(8,128)(2,1)S(1)}) fusion(f16[512,384]{1,0:T(8,128)(2,1)S(1)} %collective-permute-done.6, pred[]{:T(512)S(6)} %eq.35, f32[1536,1536]{1,0:T(8,128)} %bitcast.12, pred[]{:T(512)S(6)} %eq.36, pred[]{:T(512)S(6)} %eq.37, pred[]{:T(512)S(6)} %eq.38), kind=kLoop, calls=%fused_computation.28 | loop fusion | flops 2752512 | bytes 7864324 | tf_op jit(solution)/shard_map/convert_element_type | solution.py:55
  17.4 4.7 %collective-permute-done.1 = f16[512,384]{1,0:T(8,128)(2,1)S(1)} collective-permute-done((f16[512,384]{1,0:T(8,128)(2,1)S(1)}, f16[512,384]{1,0:T(8,128)(2,1)S(1)}, u32[]{:S(2)}, u32[]{:S(2)}) %collective-permute-start.1) | collective-permute-done | bytes 393248 | tf_op jit(solution)/shard_map/ppermute | solution.py:171
  22.9 2.1 %add_convert_fusion.9 = f16[512,384]{1,0:T(8,128)(2,1)S(1)} fusion(f16[512,384]{1,0:T(8,128)(2,1)S(1)} %collective-permute-done.1, f16[512,384]{1,0:T(8,128)(2,1)S(1)} %collective-permute-done.2, pred[]{:T(512)S(6)} %eq.38, f32[1536,1536]{1,0:T(8,128)} %bitcast.13, pred[]{:T(512)S(6)} %eq.36), kind=kLoop, calls=%fused_computation.27 | loop fusion | flops 1572864 | bytes 4325378 | tf_op jit(solution)/shard_map/convert_element_type | solution.py:55
  26.5 2.4 %collective-permute-start.10 = (f32[4,1664]{1,0:T(4,128)S(1)}, f32[4,1664]{1,0:T(4,128)S(1)}, u32[]{:S(2)}, u32[]{:S(2)}) collective-permute-start(f32[4,1664]{1,0:T(4,128)S(1)} %add.134), channel_id=1, source_target_pairs={{0,16},{8,24},{16,0},{24,8},{1,17},{9,25},{17,1},{25,9},{2,18},{10... | collective-permute-start | bytes 79880 | tf_op jit(solution)/shard_map/ppermute | solution.py:39
  28.8 4.1 %collective-permute-done.10 = f32[4,1664]{1,0:T(4,128)S(1)} collective-permute-done((f32[4,1664]{1,0:T(4,128)S(1)}, f32[4,1664]{1,0:T(4,128)S(1)}, u32[]{:S(2)}, u32[]{:S(2)}) %collective-permute-start.10) | collective-permute-done | bytes 26656 | tf_op jit(solution)/shard_map/ppermute | solution.py:39
  32.9 2.8 %add_convert_fusion.8 = f16[512,384]{1,0:T(8,128)(2,1)} fusion(f16[512,384]{1,0:T(8,128)(2,1)S(1)} %collective-permute-done.4, pred[]{:T(512)S(6)} %eq.35, f32[1536,1536]{1,0:T(8,128)} %bitcast.14, pred[]{:T(512)S(6)} %eq.36), kind=kLoop, calls=%fused_computation.26 | loop fusion | flops 1179648 | bytes 3932162 | tf_op jit(solution)/shard_map/convert_element_type | solution.py:55
  36.7 2.5 %add_convert_fusion.7 = f16[512,384]{1,0:T(8,128)(2,1)S(1)} fusion(f16[512,384]{1,0:T(8,128)(2,1)S(1)} %collective-permute-done.8, f16[512,384]{1,0:T(8,128)(2,1)S(1)} %collective-permute-done.3, pred[]{:T(512)S(6)} %eq.38, f32[1536,1536]{1,0:T(8,128)} %bitcast.15, pred[]{:T(512)S(6)} %eq.36), kind=kLoop, calls=%fused_computation.25 | loop fusion | flops 1572864 | bytes 4325378 | tf_op jit(solution)/shard_map/convert_element_type | solution.py:55
  39.3 4.9 %collective-permute-start.12 = (f16[512,384]{1,0:T(8,128)(2,1)S(1)}, f16[512,384]{1,0:T(8,128)(2,1)}, u32[]{:S(2)}, u32[]{:S(2)}) collective-permute-start(f16[512,384]{1,0:T(8,128)(2,1)S(1)} %add_convert_fusion.7), channel_id=1, source_target_pairs={{0,8},{8,0},{16,24},{24,16},{1,9},{9,1},{17,25},{25,17},{2,10},{10... | collective-permute-start | bytes 1179656 | tf_op jit(solution)/shard_map/ppermute | solution.py:279
  46.0 3.1 %collective-permute-start.14 = (f32[4,1664]{1,0:T(4,128)}, f32[4,1664]{1,0:T(4,128)}, u32[]{:S(2)}, u32[]{:S(2)}) collective-permute-start(f32[4,1664]{1,0:T(4,128)} %add.139), channel_id=1, source_target_pairs={{0,2},{2,0},{4,6},{6,4},{1,3},{3,1},{5,7},{7,5},{8,10},{10,8},{12,... | collective-permute-start | bytes 79880 | tf_op jit(solution)/shard_map/ppermute | solution.py:39
  50.4 2.0 %convert_add_fusion = f32[512,384]{1,0:T(8,128)S(1)} fusion(f16[512,384]{1,0:T(8,128)(2,1)S(1)} %copy-done.9, pred[]{:T(512)S(6)} %eq.38, f32[1536,1536]{1,0:T(8,128)} %bitcast.16, pred[]{:T(512)S(6)} %eq.36), kind=kLoop, calls=%fused_computation.23 | loop fusion | flops 983040 | bytes 4325378 | tf_op jit(solution)/shard_map/add | solution.py:202
  62.6 3.7 %collective-permute-start.18 = (f16[512,384]{1,0:T(8,128)(2,1)S(1)}, f16[512,384]{1,0:T(8,128)(2,1)}, u32[]{:S(2)}, u32[]{:S(2)}) collective-permute-start(f16[512,384]{1,0:T(8,128)(2,1)S(1)} %get-tuple-element.130), channel_id=1, source_target_pairs={{0,8},{8,0},{16,24},{24,16},{1,9},{9,1},{17,25},{25,17},{2,10},{10... | collective-permute-start | bytes 1179656 | tf_op jit(solution)/shard_map/ppermute | solution.py:279
  67.7 2.0 %multiply_reduce_fusion.3 = (f32[]{:T(128)}, f32[4,1664]{1,0:T(4,128)}) fusion(f32[4,1664]{1,0:T(4,128)} %copy-done.10, f32[4,1664]{1,0:T(4,128)} %collective-permute-done.17), kind=kLoop, calls=%fused_computation.53 | loop fusion | flops 26623 | bytes 79876 | tf_op jit(solution)/shard_map/reduce_sum | solution.py:310
  71.6 2.1 %multiply_reduce_fusion = (f32[384]{0:T(512)S(1)}, f16[512,384]{1,0:T(8,128)(2,1)}) fusion(f16[512,384]{1,0:T(8,128)(2,1)} %collective-permute-done.19, f16[512,384]{1,0:T(8,128)(2,1)} %get-tuple-element.139), kind=kLoop, calls=%fused_computation.10 | loop fusion | flops 1572480 | bytes 1181184 | tf_op jit(solution)/shard_map/reduce_sum | solution.py:220
  73.6 5.2 %collective-permute-start.20 = (f32[1,384]{1,0:T(1,128)S(1)}, f32[1,384]{1,0:T(1,128)S(1)}, u32[]{:S(2)}, u32[]{:S(2)}) collective-permute-start(f32[1,384]{1,0:T(1,128)S(1)} %fusion.8), channel_id=1, source_target_pairs={{0,2},{2,0},{4,6},{6,4},{1,3},{3,1},{5,7},{7,5},{8,10},{10,8},{12,... | collective-permute-start | bytes 4616 | tf_op jit(solution)/shard_map/ppermute | solution.py:39
  83.3 3.8 %collective-permute-start.23 = (f32[1,384]{1,0:T(1,128)S(1)}, f32[1,384]{1,0:T(1,128)S(1)}, u32[]{:S(2)}, u32[]{:S(2)}) collective-permute-start(f32[1,384]{1,0:T(1,128)S(1)} %add.154), channel_id=1, source_target_pairs={{0,9},{1,8},{8,1},{9,0},{16,25},{17,24},{24,17},{25,16},{2,11},{3,... | collective-permute-start | bytes 4616 | tf_op jit(solution)/shard_map/ppermute | solution.py:320
  93.7 2.4 %collective-permute-done.25 = f16[512,384]{1,0:T(8,128)(2,1)} collective-permute-done((f16[512,384]{1,0:T(8,128)(2,1)}, f16[512,384]{1,0:T(8,128)(2,1)}, u32[]{:S(2)}, u32[]{:S(2)}) %collective-permute-start.25) | collective-permute-done | bytes 393248 | tf_op jit(solution)/shard_map/ppermute | solution.py:279
  98.9 4.1 %shard_map.152 = (f32[1536,384]{1,0:T(8,128)}, f32[1536,384]{1,0:T(8,128)}, f32[1536,384]{1,0:T(8,128)}, bf16[1536,384]{1,0:T(8,128)(2,1)S(1)}, bf16[512,384]{1,0:T(8,128)(2,1)S(1)}) custom-call(f32[1,1]{1,0:T(1,128)} %bitcast.2.clip_ref, f32[1536,384]{1,0:T(8,128)S(1)} %copy-done.2, f32[1536,384]{1,0:T(8,128)S(1)} %copy-done.4, f32[1536,384]{1,0:T(8,128)S(1)} %copy-done.6, ...), custom_call_target="tpu_custom_call" | custom-call | flops 1 | bytes 1024 | tf_op jit(solution)/shard_map/pallas_call | solution.py:81
  103.0 2.9 %collective-permute-start.30 = (bf16[1536,384]{1,0:T(8,128)(2,1)S(1)}, bf16[1536,384]{1,0:T(8,128)(2,1)S(1)}, u32[]{:S(2)}, u32[]{:S(2)}) collective-permute-start(bf16[1536,384]{1,0:T(8,128)(2,1)S(1)} %get-tuple-element.112.refs_0_), channel_id=1, source_target_pairs={{0,2},{2,0},{4,6},{6,4},{1,3},{3,1},{5,7},{7,5},{8,10},{10,8},{12,... | collective-permute-start | bytes 3538952 | tf_op jit(solution)/shard_map/ppermute | solution.py:39
  108.6 2.7 %shard_map.153 = (bf16[1536,1536]{1,0:T(8,128)(2,1)}, f32[384,1536]{1,0:T(8,128)}) custom-call(s32[4]{0:T(128)S(1)} %pad_add_fusion.where_ref, f32[384,1536]{1,0:T(8,128)S(1)} %copy-done, bf16[1536,384]{1,0:T(8,128)(2,1)S(1)} %get-tuple-element.112.refs_0_, bf16[1536,384]{1,0:T(8,128)(2,1)S(1)} %collective-permute-done.30.refs_1_), custom_call_target="tpu_custom_call" | custom-call | flops 1 | bytes 1024 | tf_op jit(solution)/shard_map/pallas_call | solution.py:132
  112.0 6.4 %collective-permute-done.28.refs_4_ = bf16[512,384]{1,0:T(8,128)(2,1)} collective-permute-done((bf16[512,384]{1,0:T(8,128)(2,1)S(1)}, bf16[512,384]{1,0:T(8,128)(2,1)}, u32[]{:S(2)}, u32[]{:S(2)}) %collective-permute-start.28) | collective-permute-done | bytes 393248 | tf_op jit(solution)/shard_map/ppermute | solution.py:171
  121.7 3.2 %shard_map.154 = (bf16[1536,1536]{1,0:T(8,128)(2,1)}, f32[384,1536]{1,0:T(8,128)}) custom-call(s32[6]{0:T(128)S(1)} %stack.31.where_ref, f32[384,1536]{1,0:T(8,128)S(1)} %copy-done, bf16[512,384]{1,0:T(8,128)(2,1)S(1)} %collective-permute-done.26.refs_0_, ...), custom_call_target="tpu_custom_call", output_to_operand_aliasing={{0}: (8, {}), {1}: (9, {})} | custom-call | flops 1 | bytes 1024 | tf_op jit(solution)/shard_map/pallas_call | solution.py:132
  (108 shorter events, 43.4 us)
Async XLA Ops:
  5.1 8.1 %collective-permute-start.6 = (f16[512,384]{1,0:T(8,128)(2,1)S(1)}, f16[512,384]{1,0:T(8,128)(2,1)S(1)}, u32[]{:S(2)}, u32[]{:S(2)}) collective-permute-start(f16[512,384]{1,0:T(8,128)(2,1)S(1)} %get-tuple-element.134), channel_id=1, source_target_pairs={{0,2},{2,0},{4,6},{6,4},{1,3},{3,1},{5,7},{7,5},{8,10},{10,8},{12,... | collective-permute-start | bytes 1179656 | tf_op jit(solution)/shard_map/ppermute | solution.py:39
  11.3 6.2 %collective-permute-start.2 = (f16[512,384]{1,0:T(8,128)(2,1)S(1)}, f16[512,384]{1,0:T(8,128)(2,1)S(1)}, u32[]{:S(2)}, u32[]{:S(2)}) collective-permute-start(f16[512,384]{1,0:T(8,128)(2,1)S(1)} %get-tuple-element.135), channel_id=1, source_target_pairs={{0,2},{2,0},{4,6},{6,4},{1,3},{3,1},{5,7},{7,5},{8,10},{10,8},{12,... | collective-permute-start | bytes 1179656 | tf_op jit(solution)/shard_map/ppermute | solution.py:39
  11.9 5.5 %collective-permute-start.4 = (f16[512,384]{1,0:T(8,128)(2,1)S(1)}, f16[512,384]{1,0:T(8,128)(2,1)S(1)}, u32[]{:S(2)}, u32[]{:S(2)}) collective-permute-start(f16[512,384]{1,0:T(8,128)(2,1)S(1)} %get-tuple-element.137), channel_id=1, source_target_pairs={{0,2},{2,0},{4,6},{6,4},{1,3},{3,1},{5,7},{7,5},{8,10},{10,8},{12,... | collective-permute-start | bytes 1179656 | tf_op jit(solution)/shard_map/ppermute | solution.py:39
  11.9 10.2 %collective-permute-start.1 = (f16[512,384]{1,0:T(8,128)(2,1)S(1)}, f16[512,384]{1,0:T(8,128)(2,1)S(1)}, u32[]{:S(2)}, u32[]{:S(2)}) collective-permute-start(f16[512,384]{1,0:T(8,128)(2,1)S(1)} %add_convert_fusion.11), channel_id=1, source_target_pairs={{0,4},{2,6},{4,0},{6,2},{1,5},{3,7},{5,1},{7,3},{8,12},{10,14},{12... | collective-permute-start | bytes 1179656 | tf_op jit(solution)/shard_map/ppermute | solution.py:171
  16.5 5.6 %collective-permute-start.5 = (f16[512,384]{1,0:T(8,128)(2,1)S(1)}, f16[512,384]{1,0:T(8,128)(2,1)S(1)}, u32[]{:S(2)}, u32[]{:S(2)}) collective-permute-start(f16[512,384]{1,0:T(8,128)(2,1)S(1)} %get-tuple-element.132), channel_id=1, source_target_pairs={{0,2},{2,0},{4,6},{6,4},{1,3},{3,1},{5,7},{7,5},{8,10},{10,8},{12,... | collective-permute-start | bytes 1179656 | tf_op jit(solution)/shard_map/ppermute | solution.py:39
  25.0 10.8 %collective-permute-start.9 = (f16[512,384]{1,0:T(8,128)(2,1)S(1)}, f16[512,384]{1,0:T(8,128)(2,1)S(1)}, u32[]{:S(2)}, u32[]{:S(2)}) collective-permute-start(f16[512,384]{1,0:T(8,128)(2,1)S(1)} %add_convert_fusion.9), channel_id=1, source_target_pairs={{0,8},{8,0},{16,24},{24,16},{1,9},{9,1},{17,25},{25,17},{2,10},{10... | collective-permute-start | bytes 1179656 | tf_op jit(solution)/shard_map/ppermute | solution.py:279
  25.1 10.6 %collective-permute-start.8 = (f16[512,384]{1,0:T(8,128)(2,1)S(1)}, f16[512,384]{1,0:T(8,128)(2,1)S(1)}, u32[]{:S(2)}, u32[]{:S(2)}) collective-permute-start(f16[512,384]{1,0:T(8,128)(2,1)S(1)} %get-tuple-element.67), channel_id=1, source_target_pairs={{0,4},{2,6},{4,0},{6,2},{1,5},{3,7},{5,1},{7,3},{8,12},{10,14},{12... | collective-permute-start | bytes 1179656 | tf_op jit(solution)/shard_map/ppermute | solution.py:171
  26.5 6.5 %collective-permute-start.10 = (f32[4,1664]{1,0:T(4,128)S(1)}, f32[4,1664]{1,0:T(4,128)S(1)}, u32[]{:S(2)}, u32[]{:S(2)}) collective-permute-start(f32[4,1664]{1,0:T(4,128)S(1)} %add.134), channel_id=1, source_target_pairs={{0,16},{8,24},{16,0},{24,8},{1,17},{9,25},{17,1},{25,9},{2,18},{10... | collective-permute-start | bytes 79880 | tf_op jit(solution)/shard_map/ppermute | solution.py:39
  35.9 16.5 %collective-permute-start.13 = (f16[512,384]{1,0:T(8,128)(2,1)S(1)}, f16[512,384]{1,0:T(8,128)(2,1)S(1)}, u32[]{:S(2)}, u32[]{:S(2)}) collective-permute-start(f16[512,384]{1,0:T(8,128)(2,1)S(1)} %add_convert_fusion.6), channel_id=1, source_target_pairs={{8,16},{16,8},{9,17},{17,9},{10,18},{18,10},{11,19},{19,11},{12,20... | collective-permute-start | bytes 1179656 | tf_op jit(solution)/shard_map/ppermute | solution.py:282
  39.3 13.2 %collective-permute-start.12 = (f16[512,384]{1,0:T(8,128)(2,1)S(1)}, f16[512,384]{1,0:T(8,128)(2,1)}, u32[]{:S(2)}, u32[]{:S(2)}) collective-permute-start(f16[512,384]{1,0:T(8,128)(2,1)S(1)} %add_convert_fusion.7), channel_id=1, source_target_pairs={{0,8},{8,0},{16,24},{24,16},{1,9},{9,1},{17,25},{25,17},{2,10},{10... | collective-permute-start | bytes 1179656 | tf_op jit(solution)/shard_map/ppermute | solution.py:279
  44.2 8.3 %collective-permute-start.11 = (f16[512,384]{1,0:T(8,128)(2,1)}, f16[512,384]{1,0:T(8,128)(2,1)S(1)}, u32[]{:S(2)}, u32[]{:S(2)}) collective-permute-start(f16[512,384]{1,0:T(8,128)(2,1)} %add_convert_fusion.8), channel_id=1, source_target_pairs={{0,4},{2,6},{4,0},{6,2},{1,5},{3,7},{5,1},{7,3},{8,12},{10,14},{12... | collective-permute-start | bytes 1179656 | tf_op jit(solution)/shard_map/ppermute | solution.py:171
  54.0 7.4 %collective-permute-start.15 = (f16[512,384]{1,0:T(8,128)(2,1)S(1)}, f16[512,384]{1,0:T(8,128)(2,1)S(1)}, u32[]{:S(2)}, u32[]{:S(2)}) collective-permute-start(f16[512,384]{1,0:T(8,128)(2,1)S(1)} %broadcast_select_fusion), channel_id=1, source_target_pairs={{0,8},{8,0},{16,24},{24,16},{1,9},{9,1},{17,25},{25,17},{2,10},{10... | collective-permute-start | bytes 1179656 | tf_op jit(solution)/shard_map/ppermute | solution.py:279
  54.2 7.1 %collective-permute-start.16 = (f16[512,384]{1,0:T(8,128)(2,1)S(1)}, f16[512,384]{1,0:T(8,128)(2,1)S(1)}, u32[]{:S(2)}, u32[]{:S(2)}) collective-permute-start(f16[512,384]{1,0:T(8,128)(2,1)S(1)} %add_convert_fusion.3), channel_id=1, source_target_pairs={{8,16},{16,8},{9,17},{17,9},{10,18},{18,10},{11,19},{19,11},{12,20... | collective-permute-start | bytes 1179656 | tf_op jit(solution)/shard_map/ppermute | solution.py:282
  62.6 9.0 %collective-permute-start.18 = (f16[512,384]{1,0:T(8,128)(2,1)S(1)}, f16[512,384]{1,0:T(8,128)(2,1)}, u32[]{:S(2)}, u32[]{:S(2)}) collective-permute-start(f16[512,384]{1,0:T(8,128)(2,1)S(1)} %get-tuple-element.130), channel_id=1, source_target_pairs={{0,8},{8,0},{16,24},{24,16},{1,9},{9,1},{17,25},{25,17},{2,10},{10... | collective-permute-start | bytes 1179656 | tf_op jit(solution)/shard_map/ppermute | solution.py:279
  66.3 5.3 %collective-permute-start.19 = (f16[512,384]{1,0:T(8,128)(2,1)}, f16[512,384]{1,0:T(8,128)(2,1)}, u32[]{:S(2)}, u32[]{:S(2)}) collective-permute-start(f16[512,384]{1,0:T(8,128)(2,1)} %get-tuple-element.139), channel_id=1, source_target_pairs={{8,16},{16,8},{9,17},{17,9},{10,18},{18,10},{11,19},{19,11},{12,20... | collective-permute-start | bytes 1179656 | tf_op jit(solution)/shard_map/ppermute | solution.py:282
  73.6 6.0 %collective-permute-start.20 = (f32[1,384]{1,0:T(1,128)S(1)}, f32[1,384]{1,0:T(1,128)S(1)}, u32[]{:S(2)}, u32[]{:S(2)}) collective-permute-start(f32[1,384]{1,0:T(1,128)S(1)} %fusion.8), channel_id=1, source_target_pairs={{0,2},{2,0},{4,6},{6,4},{1,3},{3,1},{5,7},{7,5},{8,10},{10,8},{12,... | collective-permute-start | bytes 4616 | tf_op jit(solution)/shard_map/ppermute | solution.py:39
  82.1 6.5 %collective-permute-start.24 = (f32[1,384]{1,0:T(1,128)S(1)}, f32[1,384]{1,0:T(1,128)S(1)}, u32[]{:S(2)}, u32[]{:S(2)}) collective-permute-start(f32[1,384]{1,0:T(1,128)S(1)} %add.154), channel_id=1, source_target_pairs={{0,1},{1,0},{2,3},{3,2},{4,5},{5,4},{6,7},{7,6},{8,9},{9,8},{10,11... | collective-permute-start | bytes 4616 | tf_op jit(solution)/shard_map/ppermute | solution.py:39
  83.3 5.3 %collective-permute-start.23 = (f32[1,384]{1,0:T(1,128)S(1)}, f32[1,384]{1,0:T(1,128)S(1)}, u32[]{:S(2)}, u32[]{:S(2)}) collective-permute-start(f32[1,384]{1,0:T(1,128)S(1)} %add.154), channel_id=1, source_target_pairs={{0,9},{1,8},{8,1},{9,0},{16,25},{17,24},{24,17},{25,16},{2,11},{3,... | collective-permute-start | bytes 4616 | tf_op jit(solution)/shard_map/ppermute | solution.py:320
  87.1 9.0 %collective-permute-start.25 = (f16[512,384]{1,0:T(8,128)(2,1)}, f16[512,384]{1,0:T(8,128)(2,1)}, u32[]{:S(2)}, u32[]{:S(2)}) collective-permute-start(f16[512,384]{1,0:T(8,128)(2,1)} %get-tuple-element.128), channel_id=1, source_target_pairs={{0,8},{8,0},{16,24},{24,16},{1,9},{9,1},{17,25},{25,17},{2,10},{10... | collective-permute-start | bytes 1179656 | tf_op jit(solution)/shard_map/ppermute | solution.py:279
  92.9 10.2 %collective-permute-start.26 = (bf16[512,384]{1,0:T(8,128)(2,1)S(1)}, bf16[512,384]{1,0:T(8,128)(2,1)S(1)}, u32[]{:S(2)}, u32[]{:S(2)}) collective-permute-start(bf16[512,384]{1,0:T(8,128)(2,1)S(1)} %get-tuple-element.123), channel_id=1, source_target_pairs={{0,4},{2,6},{4,0},{6,2},{1,5},{3,7},{5,1},{7,3},{8,12},{10,14},{12... | collective-permute-start | bytes 1179656 | tf_op jit(solution)/shard_map/ppermute | solution.py:171
  103.0 5.6 %collective-permute-start.30 = (bf16[1536,384]{1,0:T(8,128)(2,1)S(1)}, bf16[1536,384]{1,0:T(8,128)(2,1)S(1)}, u32[]{:S(2)}, u32[]{:S(2)}) collective-permute-start(bf16[1536,384]{1,0:T(8,128)(2,1)S(1)} %get-tuple-element.112.refs_0_), channel_id=1, source_target_pairs={{0,2},{2,0},{4,6},{6,4},{1,3},{3,1},{5,7},{7,5},{8,10},{10,8},{12,... | collective-permute-start | bytes 3538952 | tf_op jit(solution)/shard_map/ppermute | solution.py:39
  106.1 12.4 %collective-permute-start.29 = (bf16[512,384]{1,0:T(8,128)(2,1)S(1)}, bf16[512,384]{1,0:T(8,128)(2,1)S(1)}, u32[]{:S(2)}, u32[]{:S(2)}) collective-permute-start(bf16[512,384]{1,0:T(8,128)(2,1)S(1)} %collective-permute-done.26.refs_0_), channel_id=1, source_target_pairs={{0,8},{8,0},{16,24},{24,16},{1,9},{9,1},{17,25},{25,17},{2,10},{10... | collective-permute-start | bytes 1179656 | tf_op jit(solution)/shard_map/ppermute | solution.py:39
  107.5 12.0 %collective-permute-start.27 = (bf16[512,384]{1,0:T(8,128)(2,1)S(1)}, bf16[512,384]{1,0:T(8,128)(2,1)S(1)}, u32[]{:S(2)}, u32[]{:S(2)}) collective-permute-start(bf16[512,384]{1,0:T(8,128)(2,1)S(1)} %collective-permute-done.26.refs_0_), channel_id=1, source_target_pairs={{0,2},{2,0},{4,6},{6,4},{1,3},{3,1},{5,7},{7,5},{8,10},{10,8},{12,... | collective-permute-start | bytes 1179656 | tf_op jit(solution)/shard_map/ppermute | solution.py:39
  107.8 10.6 %collective-permute-start.28 = (bf16[512,384]{1,0:T(8,128)(2,1)S(1)}, bf16[512,384]{1,0:T(8,128)(2,1)}, u32[]{:S(2)}, u32[]{:S(2)}) collective-permute-start(bf16[512,384]{1,0:T(8,128)(2,1)S(1)} %get-tuple-element.111), channel_id=1, source_target_pairs={{0,4},{2,6},{4,0},{6,2},{1,5},{3,7},{5,1},{7,3},{8,12},{10,14},{12... | collective-permute-start | bytes 1179656 | tf_op jit(solution)/shard_map/ppermute | solution.py:171
  (25 other events, 146.1 us)

commit v4 on v3

--- a/solution.py
+++ b/solution.py
@@ -194,23 +194,29 @@
         return scaled(jnp.where(owner_chip == 0, jnp.where(owner_core == 0, a, b), jnp.where(owner_core == 0, c, d)))
 
     targets = [(chip + off) % chips for off in (*range(1, chips), 0)]
-
-    def gift(n, i):
-        return core_swap(narrow(block(targets[n], 1 - core, i)))
+    own = chips - 1
+    gifts = {}
+
+    def give(n, i, core):
+        gifts[n, i] = core_swap(narrow(block(targets[n], 1 - core, i)))
 
     def chip_sum(n, i):
         return block(targets[n], core, i) + widen(gifts[n, i])
 
-    gifts = {(n, 0): gift(n, 0) for n in range(chips)}
-    gifts.update({(n, i): gift(n, i) for i in range(1, CHUNKS) for n in range(chips)})
+    for n in range(own):
+        give(n, 0, core)
+    outgoing = {(n, 0): narrow(chip_sum(n, 0)) for n in range(own)}
+    later_core = core
+    give(own, 0, later_core)
+    for i in range(1, CHUNKS):
+        for n in range(chips):
+            give(n, i, later_core)
 
     avgs, squares = [None] * CHUNKS, [None] * CHUNKS
     sums, halves, totals = {}, {}, {}
     is_end = (rep == 0) | (rep == 3)
     conv_steps = [*steps_of("rep"), *steps_of("dp")]
     conv_sum = grad_conv[0]
-    chosen = [[chunk(x, i) for i in range(CHUNKS)] for x in (param_proj, m_proj, v_proj)]
-    chosen = [either(values) for values in chosen]
 
     def average_of(total):
         return widen(total) * inverse
@@ -219,29 +225,34 @@
         value = average_of(total)
         return jnp.sum(value * value, axis=0, keepdims=True)
 
-    moving, outgoing = {}, {}
+    moving, own_sums = {}, {}
+
+    def chip_sum_after(n, i, payloads):
+        if i > 1:
+            gifts[n, i] = together(gifts[n, i], *payloads)[0]
+        total = chip_sum(n, i)
+        return total if n == own else narrow(total)
+
     rounds = CHUNKS + 2 if line else CHUNKS
     for r in range(rounds + 1):
         names = list(moving)
         there = dict(zip(names, together(*[moving[k] for k in names]))) if names else {}
         moving, waiting = {}, {}
         for k, value in there.items():
-            if k[0] == "gift":
-                gifts[k[1:]] = value
+            if k[0] == "own":
+                own_sums[k[1]] = value
             elif k[0] == "average":
                 avgs[k[1]] = value
             elif k[0] == "square":
                 squares[k[1]] = value
-            elif k[0] == "chosen":
-                chosen[k[1]] = value
             elif k[0] == "outgoing":
                 outgoing[k[1:]] = value
 
         if 0 <= r - 1 < CHUNKS:
-            own = there["own", 2] if r == 3 else chip_sum(chips - 1, r - 1)
-            for n in range(chips - 1):
-                own = own + widen(there["chips", n])
-            sums[r - 1] = narrow(own) if line else lax.psum(own, "rep")
+            total = own_sums[r - 1]
+            for n in range(own):
+                total = total + widen(there["chips", n])
+            sums[r - 1] = narrow(total) if line else lax.psum(total, "rep")
         if ("pair", 0) in there:
             i = r - 2
             if i < CHUNKS:
@@ -253,52 +264,37 @@
             if r < rounds:
                 waiting["square", r - 3] = square_of(totals[r - 3])
             else:
-                squares[r - 3] = square_of(totals[r - 3])
+                squares[r - 3] = square_of(together(totals[r - 3])[0])
         if ("conv", 0) in there:
             conv_sum = there["own conv", 0] + there["conv", 0]
 
         payloads = []
+        if line and 0 <= r - 2 < CHUNKS:
+            payloads.append(halves[r - 2])
+            moving["middle", 0] = lax.ppermute(halves[r - 2], "rep", [(1, 2), (2, 1)])
         if r < CHUNKS:
-            for n in range(chips - 1):
-                payloads.append(outgoing[n, r] if r else narrow(chip_sum(n, r)))
+            for n in range(own):
+                payloads.append(outgoing[n, r])
                 moving["chips", n] = chip_shift(payloads[-1], n + 1)
-        if r == 0:
-            for k, value in gifts.items():
-                if k[1] or k[0] == chips - 1:
-                    moving["gift", *k] = value
-        if line:
-            i = r - 1
-            if 0 <= i < CHUNKS + 2:
-                if i < 2:
-                    payload = sums[i]
-                elif i < CHUNKS:
-                    payload = jnp.where(is_end, sums[i], totals[i - 2])
-                else:
-                    payload = totals[i - 2]
-                payloads.append(payload)
-                moving["pair", 0] = lax.ppermute(payload, "rep", [(0, 1), (1, 0), (2, 3), (3, 2)])
-            if 0 <= r - 2 < CHUNKS:
-                payloads.append(halves[r - 2])
-                moving["middle", 0] = lax.ppermute(halves[r - 2], "rep", [(1, 2), (2, 1)])
+        i = r - 1
+        if line and 0 <= i < CHUNKS + 2:
+            if i < 2:
+                payload = sums[i]
+            elif i < CHUNKS:
+                payload = jnp.where(is_end, sums[i], totals[i - 2])
+            else:
+                payload = totals[i - 2]
+            payloads.append(payload)
+            moving["pair", 0] = lax.ppermute(payload, "rep", [(0, 1), (1, 0), (2, 3), (3, 2)])
+        if r < CHUNKS:
+            if r + 1 < CHUNKS:
+                for n in range(own):
+                    waiting["outgoing", n, r + 1] = chip_sum_after(n, r + 1, payloads)
+            waiting["own", r] = chip_sum_after(own, r, payloads)
         if conv_steps and payloads:
-            sent, *_ = together(conv_sum, *payloads)
+            sent, *_ = together(conv_sum, *payloads, *(waiting[k] for k in waiting if k[0] == "outgoing"))
             moving["own conv", 0] = sent
             moving["conv", 0] = exchange(sent, *conv_steps.pop(0))
-        if r == 2:
-            gifts[chips - 1, r] = together(gifts[chips - 1, r], moving["conv", 0])[0]
-            moving["own", r] = chip_sum(chips - 1, r)
-        if r + 1 < CHUNKS:
-            for n in range(chips - 1):
-                ready = moving["conv", 0]
-                if r == 0:
-                    gifts[n, 1], ready = together(moving.pop(("gift", n, 1)), ready)
-                else:
-                    gifts[n, r + 1], ready = together(gifts[n, r + 1], ready)
-                moving["conv", 0] = ready
-                moving["outgoing", n, r + 1] = narrow(chip_sum(n, r + 1))
-        if r == rounds - 2:
-            for n in range(len(chosen)):
-                waiting["chosen", n] = chosen[n]
         moving.update(waiting)
 
     if not line:
@@ -349,7 +345,8 @@
         return (*results, 0.9 * ema_proj + 0.1 * widen(row_block), full, *conv_results)
 
     g = either(avgs)
-    p, m, v = chosen
+    start = jnp.where(odd, part_rows, 0)
+    p, m, v = (lax.dynamic_slice(x, (start, 0), (part_rows, cols)) for x in (param_proj, m_proj, v_proj))
     first = adamw_step(p, m, v, clip_factor * g)[0].astype(jnp.bfloat16)
     got_first = chip_shift(first, 1)
     avgs[-1] = last_average(first)

time: 126 us -> 111 us (0.88)
  other arithmetic: 33.1 us -> 18.2 us
  starting transfers between devices: 46.9 us -> 48.5 us
    convert_element_type x8, other arithmetic: 18.4 us -> 6.38 us  [narrow(): return x.astype(jnp.float16)]
    ppermute x19, waiting for transfers between devices: 13.5 us -> 8.2 us  [exchange(): lax.ppermute(value, axis, [(i, i ^ step) for i in range(lax.axis_size(axi...]
    ppermute x5, waiting for transfers between devices: 5.41 us -> 9.7 us  [body(): lax.ppermute(payload, 'rep', [(0, 1), (1, 0), (2, 3), (3, 2)])]
    add x1 -> x2, other arithmetic: 2.03 us -> 5.41 us  [chip_sum(): return block(targets[n], core, i) + widen(gifts[n, i])]
    ppermute x5, starting transfers between devices: 5.44 us -> 7.7 us  [chip_shift(): return lax.ppermute(x, 'dp', pairs)]
    reduce_sum x3, other arithmetic: 2.46 us -> 0.54 us  [square_of(): return jnp.sum(value * value, axis=0, keepdims=True)]
    mul x2, other arithmetic: 2.15 us -> 0.41 us  [average_of(): return widen(total) * inverse]
    add x3, other arithmetic: 1.39 us -> 0.03 us  [body(): conv_sum = there['own conv', 0] + there['conv', 0]]
  transfers between devices with their start and end apart: 33 -> 33, of which waited for: 14 -> 17; matrix products, arithmetic and copies ran while one was open for 18% -> 10% of each run, Pallas kernels for 5% -> 6%
where the time goes in v4:
time: 111 us
  starting transfers between devices  48.5 us (44%)
  waiting for transfers between devices  30 us (27%)
  other arithmetic  18.2 us (16%)
  Pallas kernels  10 us (9%)
  between operations  2.37 us (2%)
  local copies, waits for them, and re-layouts  1.8 us (2%)
    ppermute x19, starting transfers between devices, exchange(): lax.ppermute(value, axis, [(i, i ^ step) for i in range(lax.axis_size(axi...  24.4 us
    ppermute x5, waiting for transfers between devices, chip_shift(): return lax.ppermute(x, 'dp', pairs)  12.1 us
    ppermute x5, starting transfers between devices, body(): lax.ppermute(payload, 'rep', [(0, 1), (1, 0), (2, 3), (3, 2)])  10.7 us
    ppermute x5, waiting for transfers between devices, body(): lax.ppermute(payload, 'rep', [(0, 1), (1, 0), (2, 3), (3, 2)])  9.7 us
    ppermute x19, waiting for transfers between devices, exchange(): lax.ppermute(value, axis, [(i, i ^ step) for i in range(lax.axis_size(axi...  8.2 us
    ppermute x5, starting transfers between devices, chip_shift(): return lax.ppermute(x, 'dp', pairs)  7.7 us
    convert_element_type x8, other arithmetic, narrow(): return x.astype(jnp.float16)  6.38 us
    pallas_call x2, Pallas kernels, place(): pl.pallas_call(kernel, in_specs=[pl.BlockSpec(memory_space=pltpu.SMEM), f...  5.9 us
  transfers between devices with their start and end apart: 33, of which 17 were waited for; matrix products, arithmetic and copies ran while one was open for 10% of the time, Pallas kernels for 6%

profile of v4, /device:TPU:1, one launch (start us, length us, event | category | flops | bytes accessed | tf_op | source)
XLA Modules:
  0.0 110.9 jit_solution(978190850832150873)
XLA Ops:
  0.7 2.1 %select_convert_fusion.3 = (f16[512,384]{1,0:T(8,128)(2,1)S(1)}, f16[512,384]{1,0:T(8,128)(2,1)S(1)}) fusion(pred[]{:T(512)S(6)} %eq.38, f32[1536,1536]{1,0:T(8,128)} %bitcast.10, pred[]{:T(512)S(6)} %eq.37, pred[]{:T(512)S(6)} %eq.35), kind=kLoop, calls=%fused_computation.30 | loop fusion | flops 1179648 | bytes 3932163 | tf_op jit(solution)/shard_map/convert_element_type | solution.py:55
  5.1 3.4 %convert_add_fusion.2 = (f32[512,384]{1,0:T(8,128)S(1)}, f16[512,384]{1,0:T(8,128)(2,1)S(1)}, f16[512,384]{1,0:T(8,128)(2,1)S(1)}) fusion(f16[512,384]{1,0:T(8,128)(2,1)S(1)} %collective-permute-done.4, pred[]{:T(512)S(6)} %eq.38, f32[1536,1536]{1,0:T(8,128)} %bitcast.11, pred[]{:T(512)S(6)} %eq.36, pred[]{:T(512)S(6)} %eq.37, pred[]{:T(512)S(6)} %eq.35, ...), kind=kLoop, calls=%fused_computation.29 | loop fusion | flops 2555904 | bytes 8650756 | tf_op jit(solution)/shard_map/add | solution.py:204
  8.7 2.6 %collective-permute-start.1 = (f16[512,384]{1,0:T(8,128)(2,1)S(1)}, f16[512,384]{1,0:T(8,128)(2,1)S(1)}, u32[]{:S(2)}, u32[]{:S(2)}) collective-permute-start(f16[512,384]{1,0:T(8,128)(2,1)S(1)} %get-tuple-element.121), channel_id=1, source_target_pairs={{0,4},{2,6},{4,0},{6,2},{1,5},{3,7},{5,1},{7,3},{8,12},{10,14},{12... | collective-permute-start | bytes 1179656 | tf_op jit(solution)/shard_map/ppermute | solution.py:171
  11.3 3.3 %select_convert_fusion.1 = (f16[512,384]{1,0:T(8,128)(2,1)S(1)}, f16[512,384]{1,0:T(8,128)(2,1)S(1)}, f16[512,384]{1,0:T(8,128)(2,1)S(1)}) fusion(pred[]{:T(512)S(6)} %eq.38, f32[1536,1536]{1,0:T(8,128)} %bitcast.12, pred[]{:T(512)S(6)} %eq.37, pred[]{:T(512)S(6)} %eq.35, f16[512,384]{1,0:T(8,128)(2,1)S(1)} %collective-permute-done.2, pred[]{:T(512)S(6)} %eq.36), kind=kLoop, calls=%fused_computation.25 | loop fusion | flops 2752512 | bytes 7864324 | tf_op jit(solution)/shard_map/convert_element_type | solution.py:55
  16.6 4.1 %collective-permute-done.1 = f16[512,384]{1,0:T(8,128)(2,1)S(1)} collective-permute-done((f16[512,384]{1,0:T(8,128)(2,1)S(1)}, f16[512,384]{1,0:T(8,128)(2,1)S(1)}, u32[]{:S(2)}, u32[]{:S(2)}) %collective-permute-start.1) | collective-permute-done | bytes 393248 | tf_op jit(solution)/shard_map/ppermute | solution.py:171
  23.9 2.4 %collective-permute-start.8 = (f32[4,1664]{1,0:T(4,128)S(1)}, f32[4,1664]{1,0:T(4,128)S(1)}, u32[]{:S(2)}, u32[]{:S(2)}) collective-permute-start(f32[4,1664]{1,0:T(4,128)S(1)} %add.137), channel_id=1, source_target_pairs={{0,16},{8,24},{16,0},{24,8},{1,17},{9,25},{17,1},{25,9},{2,18},{10... | collective-permute-start | bytes 79880 | tf_op jit(solution)/shard_map/ppermute | solution.py:39
  26.3 1.8 %collective-permute-start.14 = (f16[512,384]{1,0:T(8,128)(2,1)S(1)}, f16[512,384]{1,0:T(8,128)(2,1)S(1)}, u32[]{:S(2)}, u32[]{:S(2)}) collective-permute-start(f16[512,384]{1,0:T(8,128)(2,1)S(1)} %get-tuple-element.113), channel_id=1, source_target_pairs={{0,2},{2,0},{4,6},{6,4},{1,3},{3,1},{5,7},{7,5},{8,10},{10,8},{12,... | collective-permute-start | bytes 1179656 | tf_op jit(solution)/shard_map/ppermute | solution.py:39
  28.0 3.3 %collective-permute-done.6 = f16[512,384]{1,0:T(8,128)(2,1)S(1)} collective-permute-done((f16[512,384]{1,0:T(8,128)(2,1)S(1)}, f16[512,384]{1,0:T(8,128)(2,1)S(1)}, u32[]{:S(2)}, u32[]{:S(2)}) %collective-permute-start.6) | collective-permute-done | bytes 393248 | tf_op jit(solution)/shard_map/ppermute | solution.py:288
  35.4 2.8 %collective-permute-start.13 = (f32[4,1664]{1,0:T(4,128)S(1)}, f32[4,1664]{1,0:T(4,128)S(1)}, u32[]{:S(2)}, u32[]{:S(2)}) collective-permute-start(f32[4,1664]{1,0:T(4,128)S(1)} %add.142), channel_id=1, source_target_pairs={{0,2},{2,0},{4,6},{6,4},{1,3},{3,1},{5,7},{7,5},{8,10},{10,8},{12,... | collective-permute-start | bytes 79880 | tf_op jit(solution)/shard_map/ppermute | solution.py:39
  38.2 2.0 %convert_add_fusion = f32[512,384]{1,0:T(8,128)S(1)} fusion(f16[512,384]{1,0:T(8,128)(2,1)S(1)} %collective-permute-done.14, pred[]{:T(512)S(6)} %eq.38, f32[1536,1536]{1,0:T(8,128)} %bitcast.13, pred[]{:T(512)S(6)} %eq.36), kind=kLoop, calls=%fused_computation.20 | loop fusion | flops 983040 | bytes 4325378 | tf_op jit(solution)/shard_map/add | solution.py:204
  40.4 1.9 %collective-permute-done.11 = f16[512,384]{1,0:T(8,128)(2,1)S(1)} collective-permute-done((f16[512,384]{1,0:T(8,128)(2,1)S(1)}, f16[512,384]{1,0:T(8,128)(2,1)S(1)}, u32[]{:S(2)}, u32[]{:S(2)}) %collective-permute-start.11) | collective-permute-done | bytes 393248 | tf_op jit(solution)/shard_map/ppermute | solution.py:171
  42.7 3.2 %collective-permute-start.16 = (f16[512,384]{1,0:T(8,128)(2,1)S(1)}, f16[512,384]{1,0:T(8,128)(2,1)S(1)}, u32[]{:S(2)}, u32[]{:S(2)}) collective-permute-start(f16[512,384]{1,0:T(8,128)(2,1)S(1)} %broadcast_select_fusion), channel_id=1, source_target_pairs={{0,8},{8,0},{16,24},{24,16},{1,9},{9,1},{17,25},{25,17},{2,10},{10... | collective-permute-start | bytes 1179656 | tf_op jit(solution)/shard_map/ppermute | solution.py:288
  49.3 2.6 %collective-permute-done.16 = f16[512,384]{1,0:T(8,128)(2,1)S(1)} collective-permute-done((f16[512,384]{1,0:T(8,128)(2,1)S(1)}, f16[512,384]{1,0:T(8,128)(2,1)S(1)}, u32[]{:S(2)}, u32[]{:S(2)}) %collective-permute-start.16) | collective-permute-done | bytes 393248 | tf_op jit(solution)/shard_map/ppermute | solution.py:288
  52.5 3.1 %collective-permute-start.19 = (f16[512,384]{1,0:T(8,128)(2,1)S(1)}, f16[512,384]{1,0:T(8,128)(2,1)S(1)}, u32[]{:S(2)}, u32[]{:S(2)}) collective-permute-start(f16[512,384]{1,0:T(8,128)(2,1)S(1)} %get-tuple-element.112), channel_id=1, source_target_pairs={{0,8},{8,0},{16,24},{24,16},{1,9},{9,1},{17,25},{25,17},{2,10},{10... | collective-permute-start | bytes 1179656 | tf_op jit(solution)/shard_map/ppermute | solution.py:288
  58.2 2.6 %collective-permute-done.19 = f16[512,384]{1,0:T(8,128)(2,1)S(1)} collective-permute-done((f16[512,384]{1,0:T(8,128)(2,1)S(1)}, f16[512,384]{1,0:T(8,128)(2,1)S(1)}, u32[]{:S(2)}, u32[]{:S(2)}) %collective-permute-start.19) | collective-permute-done | bytes 393248 | tf_op jit(solution)/shard_map/ppermute | solution.py:288
  61.1 5.2 %collective-permute-start.20 = (f32[1,384]{1,0:T(1,128)S(1)}, f32[1,384]{1,0:T(1,128)S(1)}, u32[]{:S(2)}, u32[]{:S(2)}) collective-permute-start(f32[1,384]{1,0:T(1,128)S(1)} %fusion.8), channel_id=1, source_target_pairs={{0,2},{2,0},{4,6},{6,4},{1,3},{3,1},{5,7},{7,5},{8,10},{10,8},{12,... | collective-permute-start | bytes 4616 | tf_op jit(solution)/shard_map/ppermute | solution.py:39
  70.8 3.6 %collective-permute-start.23 = (f32[1,384]{1,0:T(1,128)S(1)}, f32[1,384]{1,0:T(1,128)S(1)}, u32[]{:S(2)}, u32[]{:S(2)}) collective-permute-start(f32[1,384]{1,0:T(1,128)S(1)} %add.156), channel_id=1, source_target_pairs={{0,9},{1,8},{8,1},{9,0},{16,25},{17,24},{24,17},{25,16},{2,11},{3,... | collective-permute-start | bytes 4616 | tf_op jit(solution)/shard_map/ppermute | solution.py:316
  78.2 2.6 %subtract_convert_fusion = (bf16[512,384]{1,0:T(8,128)(2,1)S(1)}, f32[512,384]{1,0:T(8,128)S(1)}) fusion(f32[1536,384]{1,0:T(8,128)} %v_ref.1, s32[]{:T(128)S(6)} %select_n.246, f32[512,384]{1,0:T(8,128)S(1)} %get-tuple-element.86.refs_0_, f32[1536,384]{1,0:T(8,128)} %m_ref.1, f32[1536,384]{1,0:T(8,128)} %p_ref.1, f32[]{:T(128)} %min.5, pred[]{:T(512)S(6)} %eq.42, ...), kind=kLoop, calls=%fused_computation.8 | loop fusion | flops 4128768 | bytes 5111818 | tf_op jit(solution)/shard_map/convert_element_type | solution.py:350
  84.9 4.1 %shard_map.152 = (f32[1536,384]{1,0:T(8,128)}, f32[1536,384]{1,0:T(8,128)}, f32[1536,384]{1,0:T(8,128)}, bf16[1536,384]{1,0:T(8,128)(2,1)S(1)}, bf16[512,384]{1,0:T(8,128)(2,1)S(1)}) custom-call(f32[1,1]{1,0:T(1,128)} %bitcast.2.clip_ref, f32[1536,384]{1,0:T(8,128)S(1)} %copy-done.1, f32[1536,384]{1,0:T(8,128)S(1)} %copy-done.2, f32[1536,384]{1,0:T(8,128)S(1)} %copy-done.3, ...), custom_call_target="tpu_custom_call" | custom-call | flops 1 | bytes 1024 | tf_op jit(solution)/shard_map/pallas_call | solution.py:81
  89.0 3.3 %collective-permute-start.30 = (bf16[1536,384]{1,0:T(8,128)(2,1)S(1)}, bf16[1536,384]{1,0:T(8,128)(2,1)S(1)}, u32[]{:S(2)}, u32[]{:S(2)}) collective-permute-start(bf16[1536,384]{1,0:T(8,128)(2,1)S(1)} %get-tuple-element.96.refs_0_), channel_id=1, source_target_pairs={{0,2},{2,0},{4,6},{6,4},{1,3},{3,1},{5,7},{7,5},{8,10},{10,8},{12,... | collective-permute-start | bytes 3538952 | tf_op jit(solution)/shard_map/ppermute | solution.py:39
  95.0 2.7 %shard_map.153 = (bf16[1536,1536]{1,0:T(8,128)(2,1)}, f32[384,1536]{1,0:T(8,128)}) custom-call(s32[4]{0:T(128)S(1)} %pad_add_fusion.where_ref, f32[384,1536]{1,0:T(8,128)S(1)} %copy-done, bf16[1536,384]{1,0:T(8,128)(2,1)S(1)} %get-tuple-element.96.refs_0_, bf16[1536,384]{1,0:T(8,128)(2,1)S(1)} %collective-permute-done.30.refs_1_), custom_call_target="tpu_custom_call" | custom-call | flops 1 | bytes 1024 | tf_op jit(solution)/shard_map/pallas_call | solution.py:132
  98.4 6.0 %collective-permute-done.28.refs_4_ = bf16[512,384]{1,0:T(8,128)(2,1)} collective-permute-done((bf16[512,384]{1,0:T(8,128)(2,1)S(1)}, bf16[512,384]{1,0:T(8,128)(2,1)}, u32[]{:S(2)}, u32[]{:S(2)}) %collective-permute-start.28) | collective-permute-done | bytes 393248 | tf_op jit(solution)/shard_map/ppermute | solution.py:171
  105.5 1.9 %collective-permute-done.31.refs_3_ = bf16[512,384]{1,0:T(8,128)(2,1)} collective-permute-done((bf16[512,384]{1,0:T(8,128)(2,1)S(1)}, bf16[512,384]{1,0:T(8,128)(2,1)}, u32[]{:S(2)}, u32[]{:S(2)}) %collective-permute-start.31) | collective-permute-done | bytes 393248 | tf_op jit(solution)/shard_map/ppermute | solution.py:39
  107.7 3.2 %shard_map.154 = (bf16[1536,1536]{1,0:T(8,128)(2,1)}, f32[384,1536]{1,0:T(8,128)}) custom-call(s32[6]{0:T(128)S(1)} %stack.31.where_ref, f32[384,1536]{1,0:T(8,128)S(1)} %copy-done, bf16[512,384]{1,0:T(8,128)(2,1)S(1)} %collective-permute-done.26.refs_0_, ...), custom_call_target="tpu_custom_call", output_to_operand_aliasing={{0}: (8, {}), {1}: (9, {})} | custom-call | flops 1 | bytes 1024 | tf_op jit(solution)/shard_map/pallas_call | solution.py:132
  (100 shorter events, 34.7 us)
Async XLA Ops:
  8.7 12.0 %collective-permute-start.1 = (f16[512,384]{1,0:T(8,128)(2,1)S(1)}, f16[512,384]{1,0:T(8,128)(2,1)S(1)}, u32[]{:S(2)}, u32[]{:S(2)}) collective-permute-start(f16[512,384]{1,0:T(8,128)(2,1)S(1)} %get-tuple-element.121), channel_id=1, source_target_pairs={{0,4},{2,6},{4,0},{6,2},{1,5},{3,7},{5,1},{7,3},{8,12},{10,14},{12... | collective-permute-start | bytes 1179656 | tf_op jit(solution)/shard_map/ppermute | solution.py:171
  14.6 8.7 %collective-permute-start.7 = (f16[512,384]{1,0:T(8,128)(2,1)S(1)}, f16[512,384]{1,0:T(8,128)(2,1)S(1)}, u32[]{:S(2)}, u32[]{:S(2)}) collective-permute-start(f16[512,384]{1,0:T(8,128)(2,1)S(1)} %get-tuple-element.117), channel_id=1, source_target_pairs={{0,2},{2,0},{4,6},{6,4},{1,3},{3,1},{5,7},{7,5},{8,10},{10,8},{12,... | collective-permute-start | bytes 1179656 | tf_op jit(solution)/shard_map/ppermute | solution.py:39
  15.1 8.3 %collective-permute-start.9 = (f16[512,384]{1,0:T(8,128)(2,1)S(1)}, f16[512,384]{1,0:T(8,128)(2,1)S(1)}, u32[]{:S(2)}, u32[]{:S(2)}) collective-permute-start(f16[512,384]{1,0:T(8,128)(2,1)S(1)} %get-tuple-element.116), channel_id=1, source_target_pairs={{0,2},{2,0},{4,6},{6,4},{1,3},{3,1},{5,7},{7,5},{8,10},{10,8},{12,... | collective-permute-start | bytes 1179656 | tf_op jit(solution)/shard_map/ppermute | solution.py:39
  15.2 5.5 %collective-permute-start.3 = (f32[4,1664]{1,0:T(4,128)S(1)}, f32[4,1664]{1,0:T(4,128)S(1)}, u32[]{:S(2)}, u32[]{:S(2)}) collective-permute-start(f32[4,1664]{1,0:T(4,128)S(1)} %bitcast.17), channel_id=1, source_target_pairs={{0,8},{8,0},{16,24},{24,16},{1,9},{9,1},{17,25},{25,17},{2,10},{10... | collective-permute-start | bytes 79880 | tf_op jit(solution)/shard_map/ppermute | solution.py:39
  20.8 10.6 %collective-permute-start.6 = (f16[512,384]{1,0:T(8,128)(2,1)S(1)}, f16[512,384]{1,0:T(8,128)(2,1)S(1)}, u32[]{:S(2)}, u32[]{:S(2)}) collective-permute-start(f16[512,384]{1,0:T(8,128)(2,1)S(1)} %add_convert_fusion.9), channel_id=1, source_target_pairs={{0,8},{8,0},{16,24},{24,16},{1,9},{9,1},{17,25},{25,17},{2,10},{10... | collective-permute-start | bytes 1179656 | tf_op jit(solution)/shard_map/ppermute | solution.py:288
  22.1 9.4 %collective-permute-start.5 = (f16[512,384]{1,0:T(8,128)(2,1)S(1)}, f16[512,384]{1,0:T(8,128)(2,1)S(1)}, u32[]{:S(2)}, u32[]{:S(2)}) collective-permute-start(f16[512,384]{1,0:T(8,128)(2,1)S(1)} %get-tuple-element.57), channel_id=1, source_target_pairs={{0,4},{2,6},{4,0},{6,2},{1,5},{3,7},{5,1},{7,3},{8,12},{10,14},{12... | collective-permute-start | bytes 1179656 | tf_op jit(solution)/shard_map/ppermute | solution.py:171
  23.9 7.6 %collective-permute-start.8 = (f32[4,1664]{1,0:T(4,128)S(1)}, f32[4,1664]{1,0:T(4,128)S(1)}, u32[]{:S(2)}, u32[]{:S(2)}) collective-permute-start(f32[4,1664]{1,0:T(4,128)S(1)} %add.137), channel_id=1, source_target_pairs={{0,16},{8,24},{16,0},{24,8},{1,17},{9,25},{17,1},{25,9},{2,18},{10... | collective-permute-start | bytes 79880 | tf_op jit(solution)/shard_map/ppermute | solution.py:39
  26.3 11.9 %collective-permute-start.14 = (f16[512,384]{1,0:T(8,128)(2,1)S(1)}, f16[512,384]{1,0:T(8,128)(2,1)S(1)}, u32[]{:S(2)}, u32[]{:S(2)}) collective-permute-start(f16[512,384]{1,0:T(8,128)(2,1)S(1)} %get-tuple-element.113), channel_id=1, source_target_pairs={{0,2},{2,0},{4,6},{6,4},{1,3},{3,1},{5,7},{7,5},{8,10},{10,8},{12,... | collective-permute-start | bytes 1179656 | tf_op jit(solution)/shard_map/ppermute | solution.py:39
  31.6 8.7 %collective-permute-start.12 = (f16[512,384]{1,0:T(8,128)(2,1)S(1)}, f16[512,384]{1,0:T(8,128)(2,1)S(1)}, u32[]{:S(2)}, u32[]{:S(2)}) collective-permute-start(f16[512,384]{1,0:T(8,128)(2,1)S(1)} %add_convert_fusion.7), channel_id=1, source_target_pairs={{0,8},{8,0},{16,24},{24,16},{1,9},{9,1},{17,25},{25,17},{2,10},{10... | collective-permute-start | bytes 1179656 | tf_op jit(solution)/shard_map/ppermute | solution.py:288
  33.4 7.0 %collective-permute-start.10 = (f16[512,384]{1,0:T(8,128)(2,1)S(1)}, f16[512,384]{1,0:T(8,128)(2,1)S(1)}, u32[]{:S(2)}, u32[]{:S(2)}) collective-permute-start(f16[512,384]{1,0:T(8,128)(2,1)S(1)} %add_convert_fusion.6), channel_id=1, source_target_pairs={{8,16},{16,8},{9,17},{17,9},{10,18},{18,10},{11,19},{19,11},{12,20... | collective-permute-start | bytes 1179656 | tf_op jit(solution)/shard_map/ppermute | solution.py:274
  34.1 8.2 %collective-permute-start.11 = (f16[512,384]{1,0:T(8,128)(2,1)S(1)}, f16[512,384]{1,0:T(8,128)(2,1)S(1)}, u32[]{:S(2)}, u32[]{:S(2)}) collective-permute-start(f16[512,384]{1,0:T(8,128)(2,1)S(1)} %get-tuple-element.67), channel_id=1, source_target_pairs={{0,4},{2,6},{4,0},{6,2},{1,5},{3,7},{5,1},{7,3},{8,12},{10,14},{12... | collective-permute-start | bytes 1179656 | tf_op jit(solution)/shard_map/ppermute | solution.py:171
  42.7 9.3 %collective-permute-start.16 = (f16[512,384]{1,0:T(8,128)(2,1)S(1)}, f16[512,384]{1,0:T(8,128)(2,1)S(1)}, u32[]{:S(2)}, u32[]{:S(2)}) collective-permute-start(f16[512,384]{1,0:T(8,128)(2,1)S(1)} %broadcast_select_fusion), channel_id=1, source_target_pairs={{0,8},{8,0},{16,24},{24,16},{1,9},{9,1},{17,25},{25,17},{2,10},{10... | collective-permute-start | bytes 1179656 | tf_op jit(solution)/shard_map/ppermute | solution.py:288
  45.9 6.1 %collective-permute-start.15 = (f16[512,384]{1,0:T(8,128)(2,1)S(1)}, f16[512,384]{1,0:T(8,128)(2,1)S(1)}, u32[]{:S(2)}, u32[]{:S(2)}) collective-permute-start(f16[512,384]{1,0:T(8,128)(2,1)S(1)} %add_convert_fusion.5), channel_id=1, source_target_pairs={{8,16},{16,8},{9,17},{17,9},{10,18},{18,10},{11,19},{19,11},{12,20... | collective-permute-start | bytes 1179656 | tf_op jit(solution)/shard_map/ppermute | solution.py:274
  52.5 8.3 %collective-permute-start.19 = (f16[512,384]{1,0:T(8,128)(2,1)S(1)}, f16[512,384]{1,0:T(8,128)(2,1)S(1)}, u32[]{:S(2)}, u32[]{:S(2)}) collective-permute-start(f16[512,384]{1,0:T(8,128)(2,1)S(1)} %get-tuple-element.112), channel_id=1, source_target_pairs={{0,8},{8,0},{16,24},{24,16},{1,9},{9,1},{17,25},{25,17},{2,10},{10... | collective-permute-start | bytes 1179656 | tf_op jit(solution)/shard_map/ppermute | solution.py:288
  55.6 5.2 %collective-permute-start.18 = (f16[512,384]{1,0:T(8,128)(2,1)S(1)}, f16[512,384]{1,0:T(8,128)(2,1)S(1)}, u32[]{:S(2)}, u32[]{:S(2)}) collective-permute-start(f16[512,384]{1,0:T(8,128)(2,1)S(1)} %get-tuple-element.125), channel_id=1, source_target_pairs={{8,16},{16,8},{9,17},{17,9},{10,18},{18,10},{11,19},{19,11},{12,20... | collective-permute-start | bytes 1179656 | tf_op jit(solution)/shard_map/ppermute | solution.py:274
  61.1 6.0 %collective-permute-start.20 = (f32[1,384]{1,0:T(1,128)S(1)}, f32[1,384]{1,0:T(1,128)S(1)}, u32[]{:S(2)}, u32[]{:S(2)}) collective-permute-start(f32[1,384]{1,0:T(1,128)S(1)} %fusion.8), channel_id=1, source_target_pairs={{0,2},{2,0},{4,6},{6,4},{1,3},{3,1},{5,7},{7,5},{8,10},{10,8},{12,... | collective-permute-start | bytes 4616 | tf_op jit(solution)/shard_map/ppermute | solution.py:39
  69.5 6.3 %collective-permute-start.24 = (f32[1,384]{1,0:T(1,128)S(1)}, f32[1,384]{1,0:T(1,128)S(1)}, u32[]{:S(2)}, u32[]{:S(2)}) collective-permute-start(f32[1,384]{1,0:T(1,128)S(1)} %add.156), channel_id=1, source_target_pairs={{0,1},{1,0},{2,3},{3,2},{4,5},{5,4},{6,7},{7,6},{8,9},{9,8},{10,11... | collective-permute-start | bytes 4616 | tf_op jit(solution)/shard_map/ppermute | solution.py:39
  70.8 5.1 %collective-permute-start.23 = (f32[1,384]{1,0:T(1,128)S(1)}, f32[1,384]{1,0:T(1,128)S(1)}, u32[]{:S(2)}, u32[]{:S(2)}) collective-permute-start(f32[1,384]{1,0:T(1,128)S(1)} %add.156), channel_id=1, source_target_pairs={{0,9},{1,8},{8,1},{9,0},{16,25},{17,24},{24,17},{25,16},{2,11},{3,... | collective-permute-start | bytes 4616 | tf_op jit(solution)/shard_map/ppermute | solution.py:316
  74.4 8.7 %collective-permute-start.25 = (f16[512,384]{1,0:T(8,128)(2,1)S(1)}, f16[512,384]{1,0:T(8,128)(2,1)S(1)}, u32[]{:S(2)}, u32[]{:S(2)}) collective-permute-start(f16[512,384]{1,0:T(8,128)(2,1)S(1)} %add_convert_fusion), channel_id=1, source_target_pairs={{0,8},{8,0},{16,24},{24,16},{1,9},{9,1},{17,25},{25,17},{2,10},{10... | collective-permute-start | bytes 1179656 | tf_op jit(solution)/shard_map/ppermute | solution.py:288
  80.7 8.3 %collective-permute-start.26 = (bf16[512,384]{1,0:T(8,128)(2,1)S(1)}, bf16[512,384]{1,0:T(8,128)(2,1)S(1)}, u32[]{:S(2)}, u32[]{:S(2)}) collective-permute-start(bf16[512,384]{1,0:T(8,128)(2,1)S(1)} %get-tuple-element.107), channel_id=1, source_target_pairs={{0,4},{2,6},{4,0},{6,2},{1,5},{3,7},{5,1},{7,3},{8,12},{10,14},{12... | collective-permute-start | bytes 1179656 | tf_op jit(solution)/shard_map/ppermute | solution.py:171
  89.0 6.0 %collective-permute-start.30 = (bf16[1536,384]{1,0:T(8,128)(2,1)S(1)}, bf16[1536,384]{1,0:T(8,128)(2,1)S(1)}, u32[]{:S(2)}, u32[]{:S(2)}) collective-permute-start(bf16[1536,384]{1,0:T(8,128)(2,1)S(1)} %get-tuple-element.96.refs_0_), channel_id=1, source_target_pairs={{0,2},{2,0},{4,6},{6,4},{1,3},{3,1},{5,7},{7,5},{8,10},{10,8},{12,... | collective-permute-start | bytes 3538952 | tf_op jit(solution)/shard_map/ppermute | solution.py:39
  92.4 12.0 %collective-permute-start.29 = (bf16[512,384]{1,0:T(8,128)(2,1)S(1)}, bf16[512,384]{1,0:T(8,128)(2,1)S(1)}, u32[]{:S(2)}, u32[]{:S(2)}) collective-permute-start(bf16[512,384]{1,0:T(8,128)(2,1)S(1)} %collective-permute-done.26.refs_0_), channel_id=1, source_target_pairs={{0,8},{8,0},{16,24},{24,16},{1,9},{9,1},{17,25},{25,17},{2,10},{10... | collective-permute-start | bytes 1179656 | tf_op jit(solution)/shard_map/ppermute | solution.py:39
  93.5 12.0 %collective-permute-start.27 = (bf16[512,384]{1,0:T(8,128)(2,1)S(1)}, bf16[512,384]{1,0:T(8,128)(2,1)S(1)}, u32[]{:S(2)}, u32[]{:S(2)}) collective-permute-start(bf16[512,384]{1,0:T(8,128)(2,1)S(1)} %collective-permute-done.26.refs_0_), channel_id=1, source_target_pairs={{0,2},{2,0},{4,6},{6,4},{1,3},{3,1},{5,7},{7,5},{8,10},{10,8},{12,... | collective-permute-start | bytes 1179656 | tf_op jit(solution)/shard_map/ppermute | solution.py:39
  93.8 10.6 %collective-permute-start.28 = (bf16[512,384]{1,0:T(8,128)(2,1)S(1)}, bf16[512,384]{1,0:T(8,128)(2,1)}, u32[]{:S(2)}, u32[]{:S(2)}) collective-permute-start(bf16[512,384]{1,0:T(8,128)(2,1)S(1)} %get-tuple-element.95), channel_id=1, source_target_pairs={{0,4},{2,6},{4,0},{6,2},{1,5},{3,7},{5,1},{7,3},{8,12},{10,14},{12... | collective-permute-start | bytes 1179656 | tf_op jit(solution)/shard_map/ppermute | solution.py:171
  (21 other events, 125.5 us)

commit v5 on v4

--- a/solution.py
+++ b/solution.py
@@ -64,45 +64,65 @@
     chunks = len(avgs)
     part = rows // chunks
 
-    def kernel(clip_ref, p_ref, m_ref, v_ref, *refs):
-        p_out, m_out, v_out, w_out, last_out = refs[-5:]
+    def kernel(clip_ref, *refs):
+        avg_refs, old_refs, new_refs = refs[:chunks], refs[chunks : chunks + 3], refs[chunks + 3 : chunks + 6]
+        w_out, last_out, near, sems = refs[chunks + 6 :]
+        loads, stores = [], []
         for k in range(chunks):
-
-            @pl.when(pl.program_id(0) == k)
-            def _():
-                p, m, v = adamw_step(p_ref[...], m_ref[...], v_ref[...], clip_ref[0, 0] * refs[k][...])
-                p_out[...], m_out[...], v_out[...] = p, m, v
-                w_out[...] = p.astype(jnp.bfloat16)
-                last_out[...] = p.astype(jnp.bfloat16)
-
-    chunk = pl.BlockSpec((part, cols), lambda i: (i, 0))
-    alone = pl.BlockSpec((part, cols), lambda i: (0, 0))
+            at = pl.ds(k * part, part)
+            for n in range(3):
+                loads.append(pltpu.make_async_copy(old_refs[n].at[at, :], near.at[n, at, :], sems.at[3 * k + n]))
+                loads[-1].start()
+        for k in range(chunks):
+            at = slice(k * part, (k + 1) * part)
+            for load in loads[3 * k : 3 * k + 3]:
+                load.wait()
+            new = adamw_step(near[0, at], near[1, at], near[2, at], clip_ref[0, 0] * avg_refs[k][...])
+            for n in range(3):
+                near[n, at] = new[n]
+                here = pl.ds(k * part, part)
+                sem = sems.at[3 * (chunks + k) + n]
+                stores.append(pltpu.make_async_copy(near.at[n, here, :], new_refs[n].at[here, :], sem))
+                stores[-1].start()
+            w_out[at, :] = new[0].astype(jnp.bfloat16)
+            if k == chunks - 1:
+                last_out[...] = new[0].astype(jnp.bfloat16)
+        for store in stores:
+            store.wait()
+
+    far, close = pl.BlockSpec(memory_space=pltpu.HBM), pl.BlockSpec(memory_space=pltpu.VMEM)
     whole = jax.ShapeDtypeStruct((rows, cols), jnp.float32)
     return pl.pallas_call(
         kernel,
-        grid=(chunks,),
-        in_specs=[pl.BlockSpec(memory_space=pltpu.SMEM)] + [chunk] * 3 + [alone] * chunks,
-        out_specs=[chunk] * 4 + [alone],
+        in_specs=[pl.BlockSpec(memory_space=pltpu.SMEM)] + [close] * chunks + [far] * 3,
+        out_specs=[far] * 3 + [close] * 2,
         out_shape=[whole, whole, whole]
         + [jax.ShapeDtypeStruct((rows, cols), jnp.bfloat16), jax.ShapeDtypeStruct((part, cols), jnp.bfloat16)],
+        scratch_shapes=[pltpu.VMEM((3, rows, cols), jnp.float32), pltpu.SemaphoreType.DMA((6 * chunks,))],
         cost_estimate=SMALL,
-        compiler_params=PARAMS,
-    )(clip, param, first, second, *avgs)
-
-
-def place(so_far, shape, ema, me, chip, core, pieces):
+        compiler_params=pltpu.CompilerParams(vmem_limit_bytes=48 * 2**20),
+    )(clip, *avgs, param, first, second)
+
+
+def place(so_far, shape, ema, rest, me, chip, core, pieces, written):
     rows, width = shape
     columns = width // 2
     cols = columns // CORES
-    ema_rows = ema.shape[0]
+    ema_rows = shape[0] // (width // cols)
     where = jnp.stack([jnp.int32(x) for x in (me, chip, core, *(block for block, _, _ in pieces))])
     values = [x for _, mine, theirs in pieces for x in (mine, theirs)]
-
-    def kernel(where_ref, ema_ref, *refs):
-        full_out, ema_out, near, ema_near, new_near, sems = refs[-6:]
+    starts = rest is None
+
+    def kernel(where_ref, old_ref, *refs):
+        outs = 3 if starts else 2
+        scratch = refs[-3:] if not starts else refs[-4:]
+        full_out, ema_out = refs[-len(scratch) - outs : -len(scratch)][:2]
+        near, new_near, sems = scratch[-3:]
         here = pl.ds(pl.multiple_of(where_ref[1] * columns, LANES), columns)
-        load = pltpu.make_async_copy(ema_ref.at[:, here], ema_near, sems.at[0])
-        load.start()
+        if starts:
+            rest_out, old_near = refs[-5], refs[-4]
+            load = pltpu.make_async_copy(old_ref, old_near, sems.at[0])
+            load.start()
         stores = []
         for k in range(len(pieces)):
             mine, theirs = refs[2 * k], refs[2 * k + 1]
@@ -118,34 +138,43 @@
                 near[at, :cols] = theirs[...]
                 near[at, cols:] = mine[...]
 
-            stores.append(pltpu.make_async_copy(near.at[at, :], full_out.at[at, here], sems.at[2 + k]))
-            stores[-1].start()
-        load.wait()
+            if k >= written:
+                stores.append(pltpu.make_async_copy(near.at[at, :], full_out.at[at, here], sems.at[2 + k]))
+                stores[-1].start()
         mine_rows = near[pl.ds(pl.multiple_of(where_ref[0] * ema_rows, 16), ema_rows), :]
-        new_near[...] = 0.9 * ema_near[...] + 0.1 * widen(mine_rows)
+        if starts:
+            load.wait()
+            there = pl.ds(pl.multiple_of((1 - where_ref[1]) * columns, LANES), columns)
+            new_near[...] = 0.9 * old_near[:, here] + 0.1 * widen(mine_rows)
+            rest_out[...] = 0.9 * old_near[:, there]
+        else:
+            new_near[...] = old_ref[...] + 0.1 * widen(mine_rows)
         stores.append(pltpu.make_async_copy(new_near, ema_out.at[:, here], sems.at[1]))
         stores[-1].start()
         for store in stores:
             store.wait()
 
     far = pl.BlockSpec(memory_space=pltpu.HBM)
+    close = pl.BlockSpec(memory_space=pltpu.VMEM)
+    old = jax.ShapeDtypeStruct((ema_rows, width), jnp.float32)
+    half = jax.ShapeDtypeStruct((ema_rows, columns), jnp.float32)
     return pl.pallas_call(
         kernel,
-        in_specs=[pl.BlockSpec(memory_space=pltpu.SMEM), far]
-        + [pl.BlockSpec(memory_space=pltpu.VMEM)] * len(values)
+        in_specs=[pl.BlockSpec(memory_space=pltpu.SMEM), far if starts else close]
+        + [close] * len(values)
         + [far] * len(so_far),
-        out_specs=[far, far],
-        out_shape=[jax.ShapeDtypeStruct(shape, jnp.bfloat16), jax.ShapeDtypeStruct(ema.shape, jnp.float32)],
+        out_specs=[far, far] + [close] * starts,
+        out_shape=[jax.ShapeDtypeStruct(shape, jnp.bfloat16), old] + [half] * starts,
         input_output_aliases={2 + len(values) + i: i for i in range(len(so_far))},
-        scratch_shapes=[
+        scratch_shapes=[pltpu.VMEM(old.shape, jnp.float32)] * starts
+        + [
             pltpu.VMEM((rows, columns), jnp.bfloat16),
-            pltpu.VMEM((ema_rows, columns), jnp.float32),
-            pltpu.VMEM((ema_rows, columns), jnp.float32),
+            pltpu.VMEM(half.shape, jnp.float32),
             pltpu.SemaphoreType.DMA((2 + len(pieces),)),
         ],
         cost_estimate=SMALL,
-        compiler_params=PARAMS,
-    )(where, ema, *values, *so_far)
+        compiler_params=pltpu.CompilerParams(vmem_limit_bytes=40 * 2**20),
+    )(where, ema if starts else rest, *values, *so_far)
 
 
 def body(grad_proj, grad_conv, param_proj, m_proj, v_proj, ema_proj, param_conv, m_conv, v_conv):
@@ -356,17 +385,19 @@
     got_third = chip_shift(third, 1)
     got_second = exchange(got_first, "rep", 1)
     got_first_other = core_swap(got_first)
-    so_far = place([], shape, ema_proj, me, chip, core, [(0, weights, core_swap(weights))])
+    *so_far, rest = place([], shape, ema_proj, None, me, chip, core, [(0, weights, core_swap(weights))], 0)
     clip, _ = together(clip_factor, so_far[0])
     conv_results = adamw_step(param_conv, m_conv, v_conv, clip * conv_avg)
-    got_third, got_second, *_ = together(got_third, got_second, *so_far, conv_results[0])
+    got_second, *_ = together(got_second, *so_far, conv_results[0])
+    got_second_other = core_swap(got_second)
+    got_third, _ = together(got_third, got_second)
     first_block = jnp.where(odd, 1, 0)
     pieces = [
         (first_block, got_first, got_first_other),
-        (1 - first_block, got_second, core_swap(got_second)),
+        (1 - first_block, got_second, got_second_other),
         (2, got_third, core_swap(got_third)),
     ]
-    full, new_ema = place(so_far, shape, ema_proj, me, 1 - chip, core, pieces)
+    full, new_ema = place(so_far, shape, None, rest, me, 1 - chip, core, pieces, 0)
     return (*results, new_ema, full, *conv_results)
 
 

time: 111 us -> 110 us (level)
  local copies, waits for them, and re-layouts: 1.8 us -> 0.12 us
    ppermute x5, waiting for transfers between devices: 12.1 us -> 7.36 us  [chip_shift(): return lax.ppermute(x, 'dp', pairs)]
    ppermute x19, waiting for transfers between devices: 8.2 us -> 12.5 us  [exchange(): lax.ppermute(value, axis, [(i, i ^ step) for i in range(lax.axis_size(axi...]
    unnamed x24 -> x16, local copies, waits for them, and re-layouts: 1.71 us -> 0.03 us
    pallas_call x1, Pallas kernels: 4.12 us -> 5.69 us  [step_state(): pl.pallas_call(kernel, in_specs=[pl.BlockSpec(memory_space=pltpu.SMEM)] +...]
  transfers between devices with their start and end apart: 33 -> 33, of which waited for: 17 -> 18; matrix products, arithmetic and copies ran while one was open for 10% -> 10% of each run, Pallas kernels for 6% -> 8%
where the time goes in v5:
time: 110 us
  starting transfers between devices  48.6 us (44%)
  waiting for transfers between devices  30.3 us (28%)
  other arithmetic  17.4 us (16%)
  Pallas kernels  10.9 us (10%)
  between operations  2.33 us (2%)
    ppermute x19, starting transfers between devices, exchange(): lax.ppermute(value, axis, [(i, i ^ step) for i in range(lax.axis_size(axi...  24.5 us
    ppermute x19, waiting for transfers between devices, exchange(): lax.ppermute(value, axis, [(i, i ^ step) for i in range(lax.axis_size(axi...  12.5 us
    ppermute x5, starting transfers between devices, body(): lax.ppermute(payload, 'rep', [(0, 1), (1, 0), (2, 3), (3, 2)])  10.7 us
    ppermute x5, waiting for transfers between devices, body(): lax.ppermute(payload, 'rep', [(0, 1), (1, 0), (2, 3), (3, 2)])  10.5 us
    ppermute x5, starting transfers between devices, chip_shift(): return lax.ppermute(x, 'dp', pairs)  7.7 us
    ppermute x5, waiting for transfers between devices, chip_shift(): return lax.ppermute(x, 'dp', pairs)  7.36 us
    convert_element_type x8, other arithmetic, narrow(): return x.astype(jnp.float16)  6.38 us
    pallas_call x1, Pallas kernels, step_state(): pl.pallas_call(kernel, in_specs=[pl.BlockSpec(memory_space=pltpu.SMEM)] +...  5.69 us
  transfers between devices with their start and end apart: 33, of which 18 were waited for; matrix products, arithmetic and copies ran while one was open for 10% of the time, Pallas kernels for 8%

profile of v5, /device:TPU:1, one launch (start us, length us, event | category | flops | bytes accessed | tf_op | source)
XLA Modules:
  0.0 109.6 jit_solution(856934089265368216)
XLA Ops:
  0.7 2.1 %select_convert_fusion.3 = (f16[512,384]{1,0:T(8,128)(2,1)S(1)}, f16[512,384]{1,0:T(8,128)(2,1)S(1)}) fusion(pred[]{:T(512)S(6)} %eq.38, f32[1536,1536]{1,0:T(8,128)} %bitcast.10, pred[]{:T(512)S(6)} %eq.37, pred[]{:T(512)S(6)} %eq.35), kind=kLoop, calls=%fused_computation.30 | loop fusion | flops 1179648 | bytes 3932163 | tf_op jit(solution)/shard_map/convert_element_type | solution.py:55
  5.1 3.4 %convert_add_fusion.2 = (f32[512,384]{1,0:T(8,128)S(1)}, f16[512,384]{1,0:T(8,128)(2,1)S(1)}, f16[512,384]{1,0:T(8,128)(2,1)S(1)}) fusion(f16[512,384]{1,0:T(8,128)(2,1)S(1)} %collective-permute-done.4, pred[]{:T(512)S(6)} %eq.38, f32[1536,1536]{1,0:T(8,128)} %bitcast.11, pred[]{:T(512)S(6)} %eq.36, pred[]{:T(512)S(6)} %eq.37, pred[]{:T(512)S(6)} %eq.35, ...), kind=kLoop, calls=%fused_computation.29 | loop fusion | flops 2555904 | bytes 8650756 | tf_op jit(solution)/shard_map/add | solution.py:233
  8.7 2.6 %collective-permute-start.1 = (f16[512,384]{1,0:T(8,128)(2,1)S(1)}, f16[512,384]{1,0:T(8,128)(2,1)S(1)}, u32[]{:S(2)}, u32[]{:S(2)}) collective-permute-start(f16[512,384]{1,0:T(8,128)(2,1)S(1)} %get-tuple-element.123), channel_id=1, source_target_pairs={{0,4},{2,6},{4,0},{6,2},{1,5},{3,7},{5,1},{7,3},{8,12},{10,14},{12... | collective-permute-start | bytes 1179656 | tf_op jit(solution)/shard_map/ppermute | solution.py:200
  11.3 3.3 %select_convert_fusion.1 = (f16[512,384]{1,0:T(8,128)(2,1)S(1)}, f16[512,384]{1,0:T(8,128)(2,1)S(1)}, f16[512,384]{1,0:T(8,128)(2,1)S(1)}) fusion(pred[]{:T(512)S(6)} %eq.38, f32[1536,1536]{1,0:T(8,128)} %bitcast.12, pred[]{:T(512)S(6)} %eq.37, pred[]{:T(512)S(6)} %eq.35, f16[512,384]{1,0:T(8,128)(2,1)S(1)} %collective-permute-done.2, pred[]{:T(512)S(6)} %eq.36), kind=kLoop, calls=%fused_computation.25 | loop fusion | flops 2752512 | bytes 7864324 | tf_op jit(solution)/shard_map/convert_element_type | solution.py:55
  16.6 4.1 %collective-permute-done.1 = f16[512,384]{1,0:T(8,128)(2,1)S(1)} collective-permute-done((f16[512,384]{1,0:T(8,128)(2,1)S(1)}, f16[512,384]{1,0:T(8,128)(2,1)S(1)}, u32[]{:S(2)}, u32[]{:S(2)}) %collective-permute-start.1) | collective-permute-done | bytes 393248 | tf_op jit(solution)/shard_map/ppermute | solution.py:200
  23.9 2.4 %collective-permute-start.8 = (f32[4,1664]{1,0:T(4,128)S(1)}, f32[4,1664]{1,0:T(4,128)S(1)}, u32[]{:S(2)}, u32[]{:S(2)}) collective-permute-start(f32[4,1664]{1,0:T(4,128)S(1)} %add.137), channel_id=1, source_target_pairs={{0,16},{8,24},{16,0},{24,8},{1,17},{9,25},{17,1},{25,9},{2,18},{10... | collective-permute-start | bytes 79880 | tf_op jit(solution)/shard_map/ppermute | solution.py:39
  26.3 1.8 %collective-permute-start.14 = (f16[512,384]{1,0:T(8,128)(2,1)S(1)}, f16[512,384]{1,0:T(8,128)(2,1)S(1)}, u32[]{:S(2)}, u32[]{:S(2)}) collective-permute-start(f16[512,384]{1,0:T(8,128)(2,1)S(1)} %get-tuple-element.115), channel_id=1, source_target_pairs={{0,2},{2,0},{4,6},{6,4},{1,3},{3,1},{5,7},{7,5},{8,10},{10,8},{12,... | collective-permute-start | bytes 1179656 | tf_op jit(solution)/shard_map/ppermute | solution.py:39
  28.0 3.3 %collective-permute-done.6 = f16[512,384]{1,0:T(8,128)(2,1)S(1)} collective-permute-done((f16[512,384]{1,0:T(8,128)(2,1)S(1)}, f16[512,384]{1,0:T(8,128)(2,1)S(1)}, u32[]{:S(2)}, u32[]{:S(2)}) %collective-permute-start.6) | collective-permute-done | bytes 393248 | tf_op jit(solution)/shard_map/ppermute | solution.py:317
  31.6 1.6 %collective-permute-start.12 = (f16[512,384]{1,0:T(8,128)(2,1)S(1)}, f16[512,384]{1,0:T(8,128)(2,1)S(1)}, u32[]{:S(2)}, u32[]{:S(2)}) collective-permute-start(f16[512,384]{1,0:T(8,128)(2,1)S(1)} %add_convert_fusion.7), channel_id=1, source_target_pairs={{0,8},{8,0},{16,24},{24,16},{1,9},{9,1},{17,25},{25,17},{2,10},{10... | collective-permute-start | bytes 1179656 | tf_op jit(solution)/shard_map/ppermute | solution.py:317
  35.4 2.8 %collective-permute-start.13 = (f32[4,1664]{1,0:T(4,128)S(1)}, f32[4,1664]{1,0:T(4,128)S(1)}, u32[]{:S(2)}, u32[]{:S(2)}) collective-permute-start(f32[4,1664]{1,0:T(4,128)S(1)} %add.142), channel_id=1, source_target_pairs={{0,2},{2,0},{4,6},{6,4},{1,3},{3,1},{5,7},{7,5},{8,10},{10,8},{12,... | collective-permute-start | bytes 79880 | tf_op jit(solution)/shard_map/ppermute | solution.py:39
  38.2 2.0 %convert_add_fusion = f32[512,384]{1,0:T(8,128)S(1)} fusion(f16[512,384]{1,0:T(8,128)(2,1)S(1)} %collective-permute-done.14, pred[]{:T(512)S(6)} %eq.38, f32[1536,1536]{1,0:T(8,128)} %bitcast.13, pred[]{:T(512)S(6)} %eq.36), kind=kLoop, calls=%fused_computation.20 | loop fusion | flops 983040 | bytes 4325378 | tf_op jit(solution)/shard_map/add | solution.py:233
  40.4 1.9 %collective-permute-done.11 = f16[512,384]{1,0:T(8,128)(2,1)S(1)} collective-permute-done((f16[512,384]{1,0:T(8,128)(2,1)S(1)}, f16[512,384]{1,0:T(8,128)(2,1)S(1)}, u32[]{:S(2)}, u32[]{:S(2)}) %collective-permute-start.11) | collective-permute-done | bytes 393248 | tf_op jit(solution)/shard_map/ppermute | solution.py:200
  42.7 3.2 %collective-permute-start.16 = (f16[512,384]{1,0:T(8,128)(2,1)S(1)}, f16[512,384]{1,0:T(8,128)(2,1)S(1)}, u32[]{:S(2)}, u32[]{:S(2)}) collective-permute-start(f16[512,384]{1,0:T(8,128)(2,1)S(1)} %broadcast_select_fusion), channel_id=1, source_target_pairs={{0,8},{8,0},{16,24},{24,16},{1,9},{9,1},{17,25},{25,17},{2,10},{10... | collective-permute-start | bytes 1179656 | tf_op jit(solution)/shard_map/ppermute | solution.py:317
  49.3 2.6 %collective-permute-done.16 = f16[512,384]{1,0:T(8,128)(2,1)S(1)} collective-permute-done((f16[512,384]{1,0:T(8,128)(2,1)S(1)}, f16[512,384]{1,0:T(8,128)(2,1)S(1)}, u32[]{:S(2)}, u32[]{:S(2)}) %collective-permute-start.16) | collective-permute-done | bytes 393248 | tf_op jit(solution)/shard_map/ppermute | solution.py:317
  52.5 3.1 %collective-permute-start.19 = (f16[512,384]{1,0:T(8,128)(2,1)S(1)}, f16[512,384]{1,0:T(8,128)(2,1)S(1)}, u32[]{:S(2)}, u32[]{:S(2)}) collective-permute-start(f16[512,384]{1,0:T(8,128)(2,1)S(1)} %get-tuple-element.114), channel_id=1, source_target_pairs={{0,8},{8,0},{16,24},{24,16},{1,9},{9,1},{17,25},{25,17},{2,10},{10... | collective-permute-start | bytes 1179656 | tf_op jit(solution)/shard_map/ppermute | solution.py:317
  57.6 3.2 %collective-permute-done.19 = f16[512,384]{1,0:T(8,128)(2,1)S(1)} collective-permute-done((f16[512,384]{1,0:T(8,128)(2,1)S(1)}, f16[512,384]{1,0:T(8,128)(2,1)S(1)}, u32[]{:S(2)}, u32[]{:S(2)}) %collective-permute-start.19) | collective-permute-done | bytes 393248 | tf_op jit(solution)/shard_map/ppermute | solution.py:317
  61.1 5.2 %collective-permute-start.20 = (f32[1,384]{1,0:T(1,128)S(1)}, f32[1,384]{1,0:T(1,128)S(1)}, u32[]{:S(2)}, u32[]{:S(2)}) collective-permute-start(f32[1,384]{1,0:T(1,128)S(1)} %fusion.8), channel_id=1, source_target_pairs={{0,2},{2,0},{4,6},{6,4},{1,3},{3,1},{5,7},{7,5},{8,10},{10,8},{12,... | collective-permute-start | bytes 4616 | tf_op jit(solution)/shard_map/ppermute | solution.py:39
  70.8 3.6 %collective-permute-start.23 = (f32[1,384]{1,0:T(1,128)S(1)}, f32[1,384]{1,0:T(1,128)S(1)}, u32[]{:S(2)}, u32[]{:S(2)}) collective-permute-start(f32[1,384]{1,0:T(1,128)S(1)} %add.156), channel_id=1, source_target_pairs={{0,9},{1,8},{8,1},{9,0},{16,25},{17,24},{24,17},{25,16},{2,11},{3,... | collective-permute-start | bytes 4616 | tf_op jit(solution)/shard_map/ppermute | solution.py:345
  78.1 2.4 %subtract_convert_fusion = (bf16[512,384]{1,0:T(8,128)(2,1)S(1)}, f32[512,384]{1,0:T(8,128)S(1)}) fusion(f32[1536,384]{1,0:T(8,128)} %refs_5_.1, s32[]{:T(128)S(6)} %select_n.246, f32[512,384]{1,0:T(8,128)S(1)} %get-tuple-element.87.refs_0_, f32[1536,384]{1,0:T(8,128)} %refs_4_.1, f32[1536,384]{1,0:T(8,128)} %refs_3_.1, f32[]{:T(128)} %min.5, pred[]{:T(512)S(6)} %eq.42, ...), kind=kLoop, calls=%fused_computation.8 | loop fusion | flops 4128768 | bytes 5111818 | tf_op jit(solution)/shard_map/convert_element_type | solution.py:379
  83.2 5.7 %shard_map.152 = (f32[1536,384]{1,0:T(8,128)}, f32[1536,384]{1,0:T(8,128)}, f32[1536,384]{1,0:T(8,128)}, bf16[1536,384]{1,0:T(8,128)(2,1)S(1)}, bf16[512,384]{1,0:T(8,128)(2,1)S(1)}) custom-call(f32[1,1]{1,0:T(1,128)} %bitcast.2.clip_ref, f32[512,384]{1,0:T(8,128)S(1)} %get-tuple-element.87.refs_0_, f32[512,384]{1,0:T(8,128)S(1)} %get-tuple-element.110.refs_1_, ...), custom_call_target="tpu_custom_call" | custom-call | flops 1 | bytes 1024 | tf_op jit(solution)/shard_map/pallas_call | solution.py:95
  88.9 3.3 %collective-permute-start.27 = (bf16[1536,384]{1,0:T(8,128)(2,1)S(1)}, bf16[1536,384]{1,0:T(8,128)(2,1)S(1)}, u32[]{:S(2)}, u32[]{:S(2)}) collective-permute-start(bf16[1536,384]{1,0:T(8,128)(2,1)S(1)} %get-tuple-element.95.refs_0_), channel_id=1, source_target_pairs={{0,2},{2,0},{4,6},{6,4},{1,3},{3,1},{5,7},{7,5},{8,10},{10,8},{12,... | collective-permute-start | bytes 3538952 | tf_op jit(solution)/shard_map/ppermute | solution.py:39
  95.0 2.7 %shard_map.153 = (bf16[1536,1536]{1,0:T(8,128)(2,1)}, f32[384,1536]{1,0:T(8,128)}, f32[384,768]{1,0:T(8,128)S(1)}) custom-call(s32[4]{0:T(128)S(1)} %pad_add_fusion.where_ref, f32[384,1536]{1,0:T(8,128)S(1)} %copy-done, bf16[1536,384]{1,0:T(8,128)(2,1)S(1)} %get-tuple-element.95.refs_0_, bf16[1536,384]{1,0:T(8,128)(2,1)S(1)} %collective-permute-done.27.refs_1_), custom_call_target="tpu_custom_call" | custom-call | flops 1 | bytes 1024 | tf_op jit(solution)/shard_map/pallas_call | solution.py:161
  98.4 4.6 %collective-permute-done.29.refs_2_ = bf16[512,384]{1,0:T(8,128)(2,1)S(1)} collective-permute-done((bf16[512,384]{1,0:T(8,128)(2,1)S(1)}, bf16[512,384]{1,0:T(8,128)(2,1)S(1)}, u32[]{:S(2)}, u32[]{:S(2)}) %collective-permute-start.29) | collective-permute-done | bytes 393248 | tf_op jit(solution)/shard_map/ppermute | solution.py:39
  107.2 2.5 %shard_map.154 = (bf16[1536,1536]{1,0:T(8,128)(2,1)}, f32[384,1536]{1,0:T(8,128)}) custom-call(s32[6]{0:T(128)S(1)} %stack.31.where_ref, f32[384,768]{1,0:T(8,128)S(1)} %get-tuple-element.96.old_ref, bf16[512,384]{1,0:T(8,128)(2,1)S(1)} %collective-permute-done.26.refs_0_, ...), custom_call_target="tpu_custom_call", output_to_operand_aliasing={{0}: (8, {}), {1}: (9, {})} | custom-call | flops 1 | bytes 1024 | tf_op jit(solution)/shard_map/pallas_call | solution.py:161
  (92 shorter events, 33.9 us)
Async XLA Ops:
  8.7 12.0 %collective-permute-start.1 = (f16[512,384]{1,0:T(8,128)(2,1)S(1)}, f16[512,384]{1,0:T(8,128)(2,1)S(1)}, u32[]{:S(2)}, u32[]{:S(2)}) collective-permute-start(f16[512,384]{1,0:T(8,128)(2,1)S(1)} %get-tuple-element.123), channel_id=1, source_target_pairs={{0,4},{2,6},{4,0},{6,2},{1,5},{3,7},{5,1},{7,3},{8,12},{10,14},{12... | collective-permute-start | bytes 1179656 | tf_op jit(solution)/shard_map/ppermute | solution.py:200
  14.6 8.7 %collective-permute-start.7 = (f16[512,384]{1,0:T(8,128)(2,1)S(1)}, f16[512,384]{1,0:T(8,128)(2,1)S(1)}, u32[]{:S(2)}, u32[]{:S(2)}) collective-permute-start(f16[512,384]{1,0:T(8,128)(2,1)S(1)} %get-tuple-element.119), channel_id=1, source_target_pairs={{0,2},{2,0},{4,6},{6,4},{1,3},{3,1},{5,7},{7,5},{8,10},{10,8},{12,... | collective-permute-start | bytes 1179656 | tf_op jit(solution)/shard_map/ppermute | solution.py:39
  15.1 8.3 %collective-permute-start.9 = (f16[512,384]{1,0:T(8,128)(2,1)S(1)}, f16[512,384]{1,0:T(8,128)(2,1)S(1)}, u32[]{:S(2)}, u32[]{:S(2)}) collective-permute-start(f16[512,384]{1,0:T(8,128)(2,1)S(1)} %get-tuple-element.118), channel_id=1, source_target_pairs={{0,2},{2,0},{4,6},{6,4},{1,3},{3,1},{5,7},{7,5},{8,10},{10,8},{12,... | collective-permute-start | bytes 1179656 | tf_op jit(solution)/shard_map/ppermute | solution.py:39
  15.2 5.5 %collective-permute-start.3 = (f32[4,1664]{1,0:T(4,128)S(1)}, f32[4,1664]{1,0:T(4,128)S(1)}, u32[]{:S(2)}, u32[]{:S(2)}) collective-permute-start(f32[4,1664]{1,0:T(4,128)S(1)} %bitcast.17), channel_id=1, source_target_pairs={{0,8},{8,0},{16,24},{24,16},{1,9},{9,1},{17,25},{25,17},{2,10},{10... | collective-permute-start | bytes 79880 | tf_op jit(solution)/shard_map/ppermute | solution.py:39
  20.8 10.6 %collective-permute-start.6 = (f16[512,384]{1,0:T(8,128)(2,1)S(1)}, f16[512,384]{1,0:T(8,128)(2,1)S(1)}, u32[]{:S(2)}, u32[]{:S(2)}) collective-permute-start(f16[512,384]{1,0:T(8,128)(2,1)S(1)} %add_convert_fusion.9), channel_id=1, source_target_pairs={{0,8},{8,0},{16,24},{24,16},{1,9},{9,1},{17,25},{25,17},{2,10},{10... | collective-permute-start | bytes 1179656 | tf_op jit(solution)/shard_map/ppermute | solution.py:317
  22.1 9.4 %collective-permute-start.5 = (f16[512,384]{1,0:T(8,128)(2,1)S(1)}, f16[512,384]{1,0:T(8,128)(2,1)S(1)}, u32[]{:S(2)}, u32[]{:S(2)}) collective-permute-start(f16[512,384]{1,0:T(8,128)(2,1)S(1)} %get-tuple-element.58), channel_id=1, source_target_pairs={{0,4},{2,6},{4,0},{6,2},{1,5},{3,7},{5,1},{7,3},{8,12},{10,14},{12... | collective-permute-start | bytes 1179656 | tf_op jit(solution)/shard_map/ppermute | solution.py:200
  23.9 7.6 %collective-permute-start.8 = (f32[4,1664]{1,0:T(4,128)S(1)}, f32[4,1664]{1,0:T(4,128)S(1)}, u32[]{:S(2)}, u32[]{:S(2)}) collective-permute-start(f32[4,1664]{1,0:T(4,128)S(1)} %add.137), channel_id=1, source_target_pairs={{0,16},{8,24},{16,0},{24,8},{1,17},{9,25},{17,1},{25,9},{2,18},{10... | collective-permute-start | bytes 79880 | tf_op jit(solution)/shard_map/ppermute | solution.py:39
  26.3 11.9 %collective-permute-start.14 = (f16[512,384]{1,0:T(8,128)(2,1)S(1)}, f16[512,384]{1,0:T(8,128)(2,1)S(1)}, u32[]{:S(2)}, u32[]{:S(2)}) collective-permute-start(f16[512,384]{1,0:T(8,128)(2,1)S(1)} %get-tuple-element.115), channel_id=1, source_target_pairs={{0,2},{2,0},{4,6},{6,4},{1,3},{3,1},{5,7},{7,5},{8,10},{10,8},{12,... | collective-permute-start | bytes 1179656 | tf_op jit(solution)/shard_map/ppermute | solution.py:39
  31.6 8.7 %collective-permute-start.12 = (f16[512,384]{1,0:T(8,128)(2,1)S(1)}, f16[512,384]{1,0:T(8,128)(2,1)S(1)}, u32[]{:S(2)}, u32[]{:S(2)}) collective-permute-start(f16[512,384]{1,0:T(8,128)(2,1)S(1)} %add_convert_fusion.7), channel_id=1, source_target_pairs={{0,8},{8,0},{16,24},{24,16},{1,9},{9,1},{17,25},{25,17},{2,10},{10... | collective-permute-start | bytes 1179656 | tf_op jit(solution)/shard_map/ppermute | solution.py:317
  33.4 7.0 %collective-permute-start.10 = (f16[512,384]{1,0:T(8,128)(2,1)S(1)}, f16[512,384]{1,0:T(8,128)(2,1)S(1)}, u32[]{:S(2)}, u32[]{:S(2)}) collective-permute-start(f16[512,384]{1,0:T(8,128)(2,1)S(1)} %add_convert_fusion.6), channel_id=1, source_target_pairs={{8,16},{16,8},{9,17},{17,9},{10,18},{18,10},{11,19},{19,11},{12,20... | collective-permute-start | bytes 1179656 | tf_op jit(solution)/shard_map/ppermute | solution.py:303
  34.1 8.2 %collective-permute-start.11 = (f16[512,384]{1,0:T(8,128)(2,1)S(1)}, f16[512,384]{1,0:T(8,128)(2,1)S(1)}, u32[]{:S(2)}, u32[]{:S(2)}) collective-permute-start(f16[512,384]{1,0:T(8,128)(2,1)S(1)} %get-tuple-element.68), channel_id=1, source_target_pairs={{0,4},{2,6},{4,0},{6,2},{1,5},{3,7},{5,1},{7,3},{8,12},{10,14},{12... | collective-permute-start | bytes 1179656 | tf_op jit(solution)/shard_map/ppermute | solution.py:200
  42.7 9.3 %collective-permute-start.16 = (f16[512,384]{1,0:T(8,128)(2,1)S(1)}, f16[512,384]{1,0:T(8,128)(2,1)S(1)}, u32[]{:S(2)}, u32[]{:S(2)}) collective-permute-start(f16[512,384]{1,0:T(8,128)(2,1)S(1)} %broadcast_select_fusion), channel_id=1, source_target_pairs={{0,8},{8,0},{16,24},{24,16},{1,9},{9,1},{17,25},{25,17},{2,10},{10... | collective-permute-start | bytes 1179656 | tf_op jit(solution)/shard_map/ppermute | solution.py:317
  45.9 6.1 %collective-permute-start.15 = (f16[512,384]{1,0:T(8,128)(2,1)S(1)}, f16[512,384]{1,0:T(8,128)(2,1)S(1)}, u32[]{:S(2)}, u32[]{:S(2)}) collective-permute-start(f16[512,384]{1,0:T(8,128)(2,1)S(1)} %add_convert_fusion.5), channel_id=1, source_target_pairs={{8,16},{16,8},{9,17},{17,9},{10,18},{18,10},{11,19},{19,11},{12,20... | collective-permute-start | bytes 1179656 | tf_op jit(solution)/shard_map/ppermute | solution.py:303
  52.5 8.3 %collective-permute-start.19 = (f16[512,384]{1,0:T(8,128)(2,1)S(1)}, f16[512,384]{1,0:T(8,128)(2,1)S(1)}, u32[]{:S(2)}, u32[]{:S(2)}) collective-permute-start(f16[512,384]{1,0:T(8,128)(2,1)S(1)} %get-tuple-element.114), channel_id=1, source_target_pairs={{0,8},{8,0},{16,24},{24,16},{1,9},{9,1},{17,25},{25,17},{2,10},{10... | collective-permute-start | bytes 1179656 | tf_op jit(solution)/shard_map/ppermute | solution.py:317
  55.6 5.2 %collective-permute-start.18 = (f16[512,384]{1,0:T(8,128)(2,1)S(1)}, f16[512,384]{1,0:T(8,128)(2,1)S(1)}, u32[]{:S(2)}, u32[]{:S(2)}) collective-permute-start(f16[512,384]{1,0:T(8,128)(2,1)S(1)} %get-tuple-element.127), channel_id=1, source_target_pairs={{8,16},{16,8},{9,17},{17,9},{10,18},{18,10},{11,19},{19,11},{12,20... | collective-permute-start | bytes 1179656 | tf_op jit(solution)/shard_map/ppermute | solution.py:303
  61.1 6.0 %collective-permute-start.20 = (f32[1,384]{1,0:T(1,128)S(1)}, f32[1,384]{1,0:T(1,128)S(1)}, u32[]{:S(2)}, u32[]{:S(2)}) collective-permute-start(f32[1,384]{1,0:T(1,128)S(1)} %fusion.8), channel_id=1, source_target_pairs={{0,2},{2,0},{4,6},{6,4},{1,3},{3,1},{5,7},{7,5},{8,10},{10,8},{12,... | collective-permute-start | bytes 4616 | tf_op jit(solution)/shard_map/ppermute | solution.py:39
  69.5 6.3 %collective-permute-start.24 = (f32[1,384]{1,0:T(1,128)S(1)}, f32[1,384]{1,0:T(1,128)S(1)}, u32[]{:S(2)}, u32[]{:S(2)}) collective-permute-start(f32[1,384]{1,0:T(1,128)S(1)} %add.156), channel_id=1, source_target_pairs={{0,1},{1,0},{2,3},{3,2},{4,5},{5,4},{6,7},{7,6},{8,9},{9,8},{10,11... | collective-permute-start | bytes 4616 | tf_op jit(solution)/shard_map/ppermute | solution.py:39
  70.8 5.1 %collective-permute-start.23 = (f32[1,384]{1,0:T(1,128)S(1)}, f32[1,384]{1,0:T(1,128)S(1)}, u32[]{:S(2)}, u32[]{:S(2)}) collective-permute-start(f32[1,384]{1,0:T(1,128)S(1)} %add.156), channel_id=1, source_target_pairs={{0,9},{1,8},{8,1},{9,0},{16,25},{17,24},{24,17},{25,16},{2,11},{3,... | collective-permute-start | bytes 4616 | tf_op jit(solution)/shard_map/ppermute | solution.py:345
  74.4 8.7 %collective-permute-start.25 = (f16[512,384]{1,0:T(8,128)(2,1)S(1)}, f16[512,384]{1,0:T(8,128)(2,1)S(1)}, u32[]{:S(2)}, u32[]{:S(2)}) collective-permute-start(f16[512,384]{1,0:T(8,128)(2,1)S(1)} %add_convert_fusion), channel_id=1, source_target_pairs={{0,8},{8,0},{16,24},{24,16},{1,9},{9,1},{17,25},{25,17},{2,10},{10... | collective-permute-start | bytes 1179656 | tf_op jit(solution)/shard_map/ppermute | solution.py:317
  80.5 8.3 %collective-permute-start.26 = (bf16[512,384]{1,0:T(8,128)(2,1)S(1)}, bf16[512,384]{1,0:T(8,128)(2,1)S(1)}, u32[]{:S(2)}, u32[]{:S(2)}) collective-permute-start(bf16[512,384]{1,0:T(8,128)(2,1)S(1)} %get-tuple-element.109), channel_id=1, source_target_pairs={{0,4},{2,6},{4,0},{6,2},{1,5},{3,7},{5,1},{7,3},{8,12},{10,14},{12... | collective-permute-start | bytes 1179656 | tf_op jit(solution)/shard_map/ppermute | solution.py:200
  88.9 6.1 %collective-permute-start.27 = (bf16[1536,384]{1,0:T(8,128)(2,1)S(1)}, bf16[1536,384]{1,0:T(8,128)(2,1)S(1)}, u32[]{:S(2)}, u32[]{:S(2)}) collective-permute-start(bf16[1536,384]{1,0:T(8,128)(2,1)S(1)} %get-tuple-element.95.refs_0_), channel_id=1, source_target_pairs={{0,2},{2,0},{4,6},{6,4},{1,3},{3,1},{5,7},{7,5},{8,10},{10,8},{12,... | collective-permute-start | bytes 3538952 | tf_op jit(solution)/shard_map/ppermute | solution.py:39
  92.2 10.8 %collective-permute-start.29 = (bf16[512,384]{1,0:T(8,128)(2,1)S(1)}, bf16[512,384]{1,0:T(8,128)(2,1)S(1)}, u32[]{:S(2)}, u32[]{:S(2)}) collective-permute-start(bf16[512,384]{1,0:T(8,128)(2,1)S(1)} %collective-permute-done.26.refs_0_), channel_id=1, source_target_pairs={{0,8},{8,0},{16,24},{24,16},{1,9},{9,1},{17,25},{25,17},{2,10},{10... | collective-permute-start | bytes 1179656 | tf_op jit(solution)/shard_map/ppermute | solution.py:39
  93.4 11.9 %collective-permute-start.28 = (bf16[512,384]{1,0:T(8,128)(2,1)S(1)}, bf16[512,384]{1,0:T(8,128)(2,1)S(1)}, u32[]{:S(2)}, u32[]{:S(2)}) collective-permute-start(bf16[512,384]{1,0:T(8,128)(2,1)S(1)} %collective-permute-done.26.refs_0_), channel_id=1, source_target_pairs={{0,2},{2,0},{4,6},{6,4},{1,3},{3,1},{5,7},{7,5},{8,10},{10,8},{12,... | collective-permute-start | bytes 1179656 | tf_op jit(solution)/shard_map/ppermute | solution.py:39
  93.7 10.5 %collective-permute-start.31 = (bf16[512,384]{1,0:T(8,128)(2,1)S(1)}, bf16[512,384]{1,0:T(8,128)(2,1)S(1)}, u32[]{:S(2)}, u32[]{:S(2)}) collective-permute-start(bf16[512,384]{1,0:T(8,128)(2,1)S(1)} %get-tuple-element.102), channel_id=1, source_target_pairs={{0,4},{2,6},{4,0},{6,2},{1,5},{3,7},{5,1},{7,3},{8,12},{10,14},{12... | collective-permute-start | bytes 1179656 | tf_op jit(solution)/shard_map/ppermute | solution.py:200
  (17 other events, 109.7 us)

commit v6 on v5

--- a/solution.py
+++ b/solution.py
@@ -336,6 +336,8 @@
 
     square = sum(squares[1:], squares[0])
     square = square + jnp.where(me == 0, conv_square, 0.0) * (lax.broadcasted_iota(jnp.int32, square.shape, 1) == 0)
+    if square.shape[1] % LANES == 0:
+        square = jnp.sum(square.reshape(-1, LANES), axis=0, keepdims=True)
     hops = [*steps_of("dp"), *steps_of("tensor")]
     for step in hops if not line else hops[:-1]:
         square = square + exchange(square, *step)
@@ -380,7 +382,7 @@
     got_first = chip_shift(first, 1)
     avgs[-1] = last_average(first)
     *results, weights, third = step_state(avgs, clip_factor, param_proj, m_proj, v_proj)
-    weights, got_first, third = together(weights, got_first, third)
+    weights, got_first = together(weights, got_first)
 
     got_third = chip_shift(third, 1)
     got_second = exchange(got_first, "rep", 1)

time: 110 us -> 110 us (level)
    ppermute x5, waiting for transfers between devices: 7.36 us -> 6.15 us  [chip_shift(): return lax.ppermute(x, 'dp', pairs)]
  transfers between devices with their start and end apart: 33 -> 33, of which waited for: 18 -> 17; matrix products, arithmetic and copies ran while one was open for 10% -> 10% of each run, Pallas kernels for 8% -> 8%
where the time goes in v6:
time: 110 us; the launch traced here: 109 us
  starting transfers between devices  48.9 us (44%)
  waiting for transfers between devices  29.7 us (27%)
  other arithmetic  17.4 us (16%)
  Pallas kernels  10.9 us (10%)
  between operations  2.33 us (2%)
    ppermute x19, starting transfers between devices, exchange(): lax.ppermute(value, axis, [(i, i ^ step) for i in range(lax.axis_size(axi...  24.7 us
    ppermute x19, waiting for transfers between devices, exchange(): lax.ppermute(value, axis, [(i, i ^ step) for i in range(lax.axis_size(axi...  13 us
    ppermute x5, starting transfers between devices, body(): lax.ppermute(payload, 'rep', [(0, 1), (1, 0), (2, 3), (3, 2)])  10.7 us
    ppermute x5, waiting for transfers between devices, body(): lax.ppermute(payload, 'rep', [(0, 1), (1, 0), (2, 3), (3, 2)])  10.5 us
    ppermute x5, starting transfers between devices, chip_shift(): return lax.ppermute(x, 'dp', pairs)  7.76 us
    convert_element_type x8, other arithmetic, narrow(): return x.astype(jnp.float16)  6.38 us
    ppermute x5, waiting for transfers between devices, chip_shift(): return lax.ppermute(x, 'dp', pairs)  6.15 us
    pallas_call x1, Pallas kernels, step_state(): pl.pallas_call(kernel, in_specs=[pl.BlockSpec(memory_space=pltpu.SMEM)] +...  5.69 us
  transfers between devices with their start and end apart: 33, of which 17 were waited for; matrix products, arithmetic and copies ran while one was open for 10% of the time, Pallas kernels for 8%

profile of v6, /device:TPU:1, one launch (start us, length us, event | category | flops | bytes accessed | tf_op | source)
XLA Modules:
  0.0 109.4 jit_solution(9542221109885812549)
XLA Ops:
  0.7 2.1 %select_convert_fusion.3 = (f16[512,384]{1,0:T(8,128)(2,1)S(1)}, f16[512,384]{1,0:T(8,128)(2,1)S(1)}) fusion(pred[]{:T(512)S(6)} %eq.38, f32[1536,1536]{1,0:T(8,128)} %bitcast.14, pred[]{:T(512)S(6)} %eq.37, pred[]{:T(512)S(6)} %eq.35), kind=kLoop, calls=%fused_computation.30 | loop fusion | flops 1179648 | bytes 3932163 | tf_op jit(solution)/shard_map/convert_element_type | solution.py:55
  5.1 3.4 %convert_add_fusion.2 = (f32[512,384]{1,0:T(8,128)S(1)}, f16[512,384]{1,0:T(8,128)(2,1)S(1)}, f16[512,384]{1,0:T(8,128)(2,1)S(1)}) fusion(f16[512,384]{1,0:T(8,128)(2,1)S(1)} %collective-permute-done.4, pred[]{:T(512)S(6)} %eq.38, f32[1536,1536]{1,0:T(8,128)} %bitcast.15, pred[]{:T(512)S(6)} %eq.36, pred[]{:T(512)S(6)} %eq.37, pred[]{:T(512)S(6)} %eq.35, ...), kind=kLoop, calls=%fused_computation.29 | loop fusion | flops 2555904 | bytes 8650756 | tf_op jit(solution)/shard_map/add | solution.py:233
  8.7 2.6 %collective-permute-start.1 = (f16[512,384]{1,0:T(8,128)(2,1)S(1)}, f16[512,384]{1,0:T(8,128)(2,1)S(1)}, u32[]{:S(2)}, u32[]{:S(2)}) collective-permute-start(f16[512,384]{1,0:T(8,128)(2,1)S(1)} %get-tuple-element.121), channel_id=1, source_target_pairs={{0,4},{2,6},{4,0},{6,2},{1,5},{3,7},{5,1},{7,3},{8,12},{10,14},{12... | collective-permute-start | bytes 1179656 | tf_op jit(solution)/shard_map/ppermute | solution.py:200
  11.3 3.3 %select_convert_fusion.1 = (f16[512,384]{1,0:T(8,128)(2,1)S(1)}, f16[512,384]{1,0:T(8,128)(2,1)S(1)}, f16[512,384]{1,0:T(8,128)(2,1)S(1)}) fusion(pred[]{:T(512)S(6)} %eq.38, f32[1536,1536]{1,0:T(8,128)} %bitcast.16, pred[]{:T(512)S(6)} %eq.37, pred[]{:T(512)S(6)} %eq.35, f16[512,384]{1,0:T(8,128)(2,1)S(1)} %collective-permute-done.2, pred[]{:T(512)S(6)} %eq.36), kind=kLoop, calls=%fused_computation.25 | loop fusion | flops 2752512 | bytes 7864324 | tf_op jit(solution)/shard_map/convert_element_type | solution.py:55
  16.6 4.1 %collective-permute-done.1 = f16[512,384]{1,0:T(8,128)(2,1)S(1)} collective-permute-done((f16[512,384]{1,0:T(8,128)(2,1)S(1)}, f16[512,384]{1,0:T(8,128)(2,1)S(1)}, u32[]{:S(2)}, u32[]{:S(2)}) %collective-permute-start.1) | collective-permute-done | bytes 393248 | tf_op jit(solution)/shard_map/ppermute | solution.py:200
  23.9 2.4 %collective-permute-start.8 = (f32[4,1664]{1,0:T(4,128)S(1)}, f32[4,1664]{1,0:T(4,128)S(1)}, u32[]{:S(2)}, u32[]{:S(2)}) collective-permute-start(f32[4,1664]{1,0:T(4,128)S(1)} %add.137), channel_id=1, source_target_pairs={{0,16},{8,24},{16,0},{24,8},{1,17},{9,25},{17,1},{25,9},{2,18},{10... | collective-permute-start | bytes 79880 | tf_op jit(solution)/shard_map/ppermute | solution.py:39
  26.3 1.8 %collective-permute-start.14 = (f16[512,384]{1,0:T(8,128)(2,1)S(1)}, f16[512,384]{1,0:T(8,128)(2,1)S(1)}, u32[]{:S(2)}, u32[]{:S(2)}) collective-permute-start(f16[512,384]{1,0:T(8,128)(2,1)S(1)} %get-tuple-element.113), channel_id=1, source_target_pairs={{0,2},{2,0},{4,6},{6,4},{1,3},{3,1},{5,7},{7,5},{8,10},{10,8},{12,... | collective-permute-start | bytes 1179656 | tf_op jit(solution)/shard_map/ppermute | solution.py:39
  28.0 3.3 %collective-permute-done.6 = f16[512,384]{1,0:T(8,128)(2,1)S(1)} collective-permute-done((f16[512,384]{1,0:T(8,128)(2,1)S(1)}, f16[512,384]{1,0:T(8,128)(2,1)S(1)}, u32[]{:S(2)}, u32[]{:S(2)}) %collective-permute-start.6) | collective-permute-done | bytes 393248 | tf_op jit(solution)/shard_map/ppermute | solution.py:317
  31.6 1.6 %collective-permute-start.12 = (f16[512,384]{1,0:T(8,128)(2,1)S(1)}, f16[512,384]{1,0:T(8,128)(2,1)S(1)}, u32[]{:S(2)}, u32[]{:S(2)}) collective-permute-start(f16[512,384]{1,0:T(8,128)(2,1)S(1)} %add_convert_fusion.7), channel_id=1, source_target_pairs={{0,8},{8,0},{16,24},{24,16},{1,9},{9,1},{17,25},{25,17},{2,10},{10... | collective-permute-start | bytes 1179656 | tf_op jit(solution)/shard_map/ppermute | solution.py:317
  35.4 2.8 %collective-permute-start.13 = (f32[4,1664]{1,0:T(4,128)S(1)}, f32[4,1664]{1,0:T(4,128)S(1)}, u32[]{:S(2)}, u32[]{:S(2)}) collective-permute-start(f32[4,1664]{1,0:T(4,128)S(1)} %add.142), channel_id=1, source_target_pairs={{0,2},{2,0},{4,6},{6,4},{1,3},{3,1},{5,7},{7,5},{8,10},{10,8},{12,... | collective-permute-start | bytes 79880 | tf_op jit(solution)/shard_map/ppermute | solution.py:39
  38.2 2.0 %convert_add_fusion = f32[512,384]{1,0:T(8,128)S(1)} fusion(f16[512,384]{1,0:T(8,128)(2,1)S(1)} %collective-permute-done.14, pred[]{:T(512)S(6)} %eq.38, f32[1536,1536]{1,0:T(8,128)} %bitcast.17, pred[]{:T(512)S(6)} %eq.36), kind=kLoop, calls=%fused_computation.20 | loop fusion | flops 983040 | bytes 4325378 | tf_op jit(solution)/shard_map/add | solution.py:233
  40.4 1.9 %collective-permute-done.11 = f16[512,384]{1,0:T(8,128)(2,1)S(1)} collective-permute-done((f16[512,384]{1,0:T(8,128)(2,1)S(1)}, f16[512,384]{1,0:T(8,128)(2,1)S(1)}, u32[]{:S(2)}, u32[]{:S(2)}) %collective-permute-start.11) | collective-permute-done | bytes 393248 | tf_op jit(solution)/shard_map/ppermute | solution.py:200
  42.7 3.2 %collective-permute-start.16 = (f16[512,384]{1,0:T(8,128)(2,1)S(1)}, f16[512,384]{1,0:T(8,128)(2,1)S(1)}, u32[]{:S(2)}, u32[]{:S(2)}) collective-permute-start(f16[512,384]{1,0:T(8,128)(2,1)S(1)} %broadcast_select_fusion), channel_id=1, source_target_pairs={{0,8},{8,0},{16,24},{24,16},{1,9},{9,1},{17,25},{25,17},{2,10},{10... | collective-permute-start | bytes 1179656 | tf_op jit(solution)/shard_map/ppermute | solution.py:317
  49.3 2.6 %collective-permute-done.16 = f16[512,384]{1,0:T(8,128)(2,1)S(1)} collective-permute-done((f16[512,384]{1,0:T(8,128)(2,1)S(1)}, f16[512,384]{1,0:T(8,128)(2,1)S(1)}, u32[]{:S(2)}, u32[]{:S(2)}) %collective-permute-start.16) | collective-permute-done | bytes 393248 | tf_op jit(solution)/shard_map/ppermute | solution.py:317
  52.5 3.1 %collective-permute-start.19 = (f16[512,384]{1,0:T(8,128)(2,1)S(1)}, f16[512,384]{1,0:T(8,128)(2,1)S(1)}, u32[]{:S(2)}, u32[]{:S(2)}) collective-permute-start(f16[512,384]{1,0:T(8,128)(2,1)S(1)} %get-tuple-element.112), channel_id=1, source_target_pairs={{0,8},{8,0},{16,24},{24,16},{1,9},{9,1},{17,25},{25,17},{2,10},{10... | collective-permute-start | bytes 1179656 | tf_op jit(solution)/shard_map/ppermute | solution.py:317
  57.6 3.2 %collective-permute-done.19 = f16[512,384]{1,0:T(8,128)(2,1)S(1)} collective-permute-done((f16[512,384]{1,0:T(8,128)(2,1)S(1)}, f16[512,384]{1,0:T(8,128)(2,1)S(1)}, u32[]{:S(2)}, u32[]{:S(2)}) %collective-permute-start.19) | collective-permute-done | bytes 393248 | tf_op jit(solution)/shard_map/ppermute | solution.py:317
  61.1 5.2 %collective-permute-start.20 = (f32[1,128]{1,0:T(1,128)S(1)}, f32[1,128]{1,0:T(1,128)S(1)}, u32[]{:S(2)}, u32[]{:S(2)}) collective-permute-start(f32[1,128]{1,0:T(1,128)S(1)} %bitcast.23), channel_id=1, source_target_pairs={{0,2},{2,0},{4,6},{6,4},{1,3},{3,1},{5,7},{7,5},{8,10},{10,8},{12,... | collective-permute-start | bytes 1544 | tf_op jit(solution)/shard_map/ppermute | solution.py:39
  70.7 3.6 %collective-permute-start.23 = (f32[1,128]{1,0:T(1,128)S(1)}, f32[1,128]{1,0:T(1,128)S(1)}, u32[]{:S(2)}, u32[]{:S(2)}) collective-permute-start(f32[1,128]{1,0:T(1,128)S(1)} %add.156), channel_id=1, source_target_pairs={{0,9},{1,8},{8,1},{9,0},{16,25},{17,24},{24,17},{25,16},{2,11},{3,... | collective-permute-start | bytes 1544 | tf_op jit(solution)/shard_map/ppermute | solution.py:347
  78.1 2.4 %subtract_convert_fusion = (bf16[512,384]{1,0:T(8,128)(2,1)S(1)}, f32[512,384]{1,0:T(8,128)S(1)}) fusion(f32[1536,384]{1,0:T(8,128)} %refs_5_.1, s32[]{:T(128)S(6)} %select_n.246, f32[512,384]{1,0:T(8,128)S(1)} %get-tuple-element.86.refs_0_, f32[1536,384]{1,0:T(8,128)} %refs_4_.1, f32[1536,384]{1,0:T(8,128)} %refs_3_.1, f32[]{:T(128)} %min.5, pred[]{:T(512)S(6)} %eq.42, ...), kind=kLoop, calls=%fused_computation.8 | loop fusion | flops 4128768 | bytes 5111818 | tf_op jit(solution)/shard_map/convert_element_type | solution.py:381
  83.2 5.7 %shard_map.152 = (f32[1536,384]{1,0:T(8,128)}, f32[1536,384]{1,0:T(8,128)}, f32[1536,384]{1,0:T(8,128)}, bf16[1536,384]{1,0:T(8,128)(2,1)S(1)}, bf16[512,384]{1,0:T(8,128)(2,1)S(1)}) custom-call(f32[1,1]{1,0:T(1,128)} %bitcast.3.clip_ref, f32[512,384]{1,0:T(8,128)S(1)} %get-tuple-element.86.refs_0_, f32[512,384]{1,0:T(8,128)S(1)} %get-tuple-element.108.refs_1_, ...), custom_call_target="tpu_custom_call" | custom-call | flops 1 | bytes 1024 | tf_op jit(solution)/shard_map/pallas_call | solution.py:95
  88.9 3.2 %collective-permute-start.27 = (bf16[1536,384]{1,0:T(8,128)(2,1)S(1)}, bf16[1536,384]{1,0:T(8,128)(2,1)S(1)}, u32[]{:S(2)}, u32[]{:S(2)}) collective-permute-start(bf16[1536,384]{1,0:T(8,128)(2,1)S(1)} %get-tuple-element.93.refs_0_), channel_id=1, source_target_pairs={{0,2},{2,0},{4,6},{6,4},{1,3},{3,1},{5,7},{7,5},{8,10},{10,8},{12,... | collective-permute-start | bytes 3538952 | tf_op jit(solution)/shard_map/ppermute | solution.py:39
  95.2 2.7 %shard_map.153 = (bf16[1536,1536]{1,0:T(8,128)(2,1)}, f32[384,1536]{1,0:T(8,128)}, f32[384,768]{1,0:T(8,128)S(1)}) custom-call(s32[4]{0:T(128)S(1)} %pad_add_fusion.where_ref, f32[384,1536]{1,0:T(8,128)S(1)} %copy-done, bf16[1536,384]{1,0:T(8,128)(2,1)S(1)} %get-tuple-element.93.refs_0_, bf16[1536,384]{1,0:T(8,128)(2,1)S(1)} %collective-permute-done.27.refs_1_), custom_call_target="tpu_custom_call" | custom-call | flops 1 | bytes 1024 | tf_op jit(solution)/shard_map/pallas_call | solution.py:161
  98.7 5.2 %collective-permute-done.29.refs_2_ = bf16[512,384]{1,0:T(8,128)(2,1)S(1)} collective-permute-done((bf16[512,384]{1,0:T(8,128)(2,1)S(1)}, bf16[512,384]{1,0:T(8,128)(2,1)S(1)}, u32[]{:S(2)}, u32[]{:S(2)}) %collective-permute-start.29) | collective-permute-done | bytes 393248 | tf_op jit(solution)/shard_map/ppermute | solution.py:39
  106.9 2.5 %shard_map.154 = (bf16[1536,1536]{1,0:T(8,128)(2,1)}, f32[384,1536]{1,0:T(8,128)}) custom-call(s32[6]{0:T(128)S(1)} %stack.31.where_ref, f32[384,768]{1,0:T(8,128)S(1)} %get-tuple-element.94.old_ref, bf16[512,384]{1,0:T(8,128)(2,1)S(1)} %collective-permute-done.26.refs_0_, ...), custom_call_target="tpu_custom_call", output_to_operand_aliasing={{0}: (8, {}), {1}: (9, {})} | custom-call | flops 1 | bytes 1024 | tf_op jit(solution)/shard_map/pallas_call | solution.py:161
  (93 shorter events, 33.1 us)
Async XLA Ops:
  8.7 12.0 %collective-permute-start.1 = (f16[512,384]{1,0:T(8,128)(2,1)S(1)}, f16[512,384]{1,0:T(8,128)(2,1)S(1)}, u32[]{:S(2)}, u32[]{:S(2)}) collective-permute-start(f16[512,384]{1,0:T(8,128)(2,1)S(1)} %get-tuple-element.121), channel_id=1, source_target_pairs={{0,4},{2,6},{4,0},{6,2},{1,5},{3,7},{5,1},{7,3},{8,12},{10,14},{12... | collective-permute-start | bytes 1179656 | tf_op jit(solution)/shard_map/ppermute | solution.py:200
  14.6 8.7 %collective-permute-start.7 = (f16[512,384]{1,0:T(8,128)(2,1)S(1)}, f16[512,384]{1,0:T(8,128)(2,1)S(1)}, u32[]{:S(2)}, u32[]{:S(2)}) collective-permute-start(f16[512,384]{1,0:T(8,128)(2,1)S(1)} %get-tuple-element.117), channel_id=1, source_target_pairs={{0,2},{2,0},{4,6},{6,4},{1,3},{3,1},{5,7},{7,5},{8,10},{10,8},{12,... | collective-permute-start | bytes 1179656 | tf_op jit(solution)/shard_map/ppermute | solution.py:39
  15.1 8.3 %collective-permute-start.9 = (f16[512,384]{1,0:T(8,128)(2,1)S(1)}, f16[512,384]{1,0:T(8,128)(2,1)S(1)}, u32[]{:S(2)}, u32[]{:S(2)}) collective-permute-start(f16[512,384]{1,0:T(8,128)(2,1)S(1)} %get-tuple-element.116), channel_id=1, source_target_pairs={{0,2},{2,0},{4,6},{6,4},{1,3},{3,1},{5,7},{7,5},{8,10},{10,8},{12,... | collective-permute-start | bytes 1179656 | tf_op jit(solution)/shard_map/ppermute | solution.py:39
  15.2 5.5 %collective-permute-start.3 = (f32[4,1664]{1,0:T(4,128)S(1)}, f32[4,1664]{1,0:T(4,128)S(1)}, u32[]{:S(2)}, u32[]{:S(2)}) collective-permute-start(f32[4,1664]{1,0:T(4,128)S(1)} %bitcast.21), channel_id=1, source_target_pairs={{0,8},{8,0},{16,24},{24,16},{1,9},{9,1},{17,25},{25,17},{2,10},{10... | collective-permute-start | bytes 79880 | tf_op jit(solution)/shard_map/ppermute | solution.py:39
  20.8 10.6 %collective-permute-start.6 = (f16[512,384]{1,0:T(8,128)(2,1)S(1)}, f16[512,384]{1,0:T(8,128)(2,1)S(1)}, u32[]{:S(2)}, u32[]{:S(2)}) collective-permute-start(f16[512,384]{1,0:T(8,128)(2,1)S(1)} %add_convert_fusion.9), channel_id=1, source_target_pairs={{0,8},{8,0},{16,24},{24,16},{1,9},{9,1},{17,25},{25,17},{2,10},{10... | collective-permute-start | bytes 1179656 | tf_op jit(solution)/shard_map/ppermute | solution.py:317
  22.1 9.4 %collective-permute-start.5 = (f16[512,384]{1,0:T(8,128)(2,1)S(1)}, f16[512,384]{1,0:T(8,128)(2,1)S(1)}, u32[]{:S(2)}, u32[]{:S(2)}) collective-permute-start(f16[512,384]{1,0:T(8,128)(2,1)S(1)} %get-tuple-element.57), channel_id=1, source_target_pairs={{0,4},{2,6},{4,0},{6,2},{1,5},{3,7},{5,1},{7,3},{8,12},{10,14},{12... | collective-permute-start | bytes 1179656 | tf_op jit(solution)/shard_map/ppermute | solution.py:200
  23.9 7.6 %collective-permute-start.8 = (f32[4,1664]{1,0:T(4,128)S(1)}, f32[4,1664]{1,0:T(4,128)S(1)}, u32[]{:S(2)}, u32[]{:S(2)}) collective-permute-start(f32[4,1664]{1,0:T(4,128)S(1)} %add.137), channel_id=1, source_target_pairs={{0,16},{8,24},{16,0},{24,8},{1,17},{9,25},{17,1},{25,9},{2,18},{10... | collective-permute-start | bytes 79880 | tf_op jit(solution)/shard_map/ppermute | solution.py:39
  26.3 11.9 %collective-permute-start.14 = (f16[512,384]{1,0:T(8,128)(2,1)S(1)}, f16[512,384]{1,0:T(8,128)(2,1)S(1)}, u32[]{:S(2)}, u32[]{:S(2)}) collective-permute-start(f16[512,384]{1,0:T(8,128)(2,1)S(1)} %get-tuple-element.113), channel_id=1, source_target_pairs={{0,2},{2,0},{4,6},{6,4},{1,3},{3,1},{5,7},{7,5},{8,10},{10,8},{12,... | collective-permute-start | bytes 1179656 | tf_op jit(solution)/shard_map/ppermute | solution.py:39
  31.6 8.7 %collective-permute-start.12 = (f16[512,384]{1,0:T(8,128)(2,1)S(1)}, f16[512,384]{1,0:T(8,128)(2,1)S(1)}, u32[]{:S(2)}, u32[]{:S(2)}) collective-permute-start(f16[512,384]{1,0:T(8,128)(2,1)S(1)} %add_convert_fusion.7), channel_id=1, source_target_pairs={{0,8},{8,0},{16,24},{24,16},{1,9},{9,1},{17,25},{25,17},{2,10},{10... | collective-permute-start | bytes 1179656 | tf_op jit(solution)/shard_map/ppermute | solution.py:317
  33.4 7.0 %collective-permute-start.10 = (f16[512,384]{1,0:T(8,128)(2,1)S(1)}, f16[512,384]{1,0:T(8,128)(2,1)S(1)}, u32[]{:S(2)}, u32[]{:S(2)}) collective-permute-start(f16[512,384]{1,0:T(8,128)(2,1)S(1)} %add_convert_fusion.6), channel_id=1, source_target_pairs={{8,16},{16,8},{9,17},{17,9},{10,18},{18,10},{11,19},{19,11},{12,20... | collective-permute-start | bytes 1179656 | tf_op jit(solution)/shard_map/ppermute | solution.py:303
  34.1 8.2 %collective-permute-start.11 = (f16[512,384]{1,0:T(8,128)(2,1)S(1)}, f16[512,384]{1,0:T(8,128)(2,1)S(1)}, u32[]{:S(2)}, u32[]{:S(2)}) collective-permute-start(f16[512,384]{1,0:T(8,128)(2,1)S(1)} %get-tuple-element.67), channel_id=1, source_target_pairs={{0,4},{2,6},{4,0},{6,2},{1,5},{3,7},{5,1},{7,3},{8,12},{10,14},{12... | collective-permute-start | bytes 1179656 | tf_op jit(solution)/shard_map/ppermute | solution.py:200
  42.7 9.3 %collective-permute-start.16 = (f16[512,384]{1,0:T(8,128)(2,1)S(1)}, f16[512,384]{1,0:T(8,128)(2,1)S(1)}, u32[]{:S(2)}, u32[]{:S(2)}) collective-permute-start(f16[512,384]{1,0:T(8,128)(2,1)S(1)} %broadcast_select_fusion), channel_id=1, source_target_pairs={{0,8},{8,0},{16,24},{24,16},{1,9},{9,1},{17,25},{25,17},{2,10},{10... | collective-permute-start | bytes 1179656 | tf_op jit(solution)/shard_map/ppermute | solution.py:317
  45.9 6.1 %collective-permute-start.15 = (f16[512,384]{1,0:T(8,128)(2,1)S(1)}, f16[512,384]{1,0:T(8,128)(2,1)S(1)}, u32[]{:S(2)}, u32[]{:S(2)}) collective-permute-start(f16[512,384]{1,0:T(8,128)(2,1)S(1)} %add_convert_fusion.5), channel_id=1, source_target_pairs={{8,16},{16,8},{9,17},{17,9},{10,18},{18,10},{11,19},{19,11},{12,20... | collective-permute-start | bytes 1179656 | tf_op jit(solution)/shard_map/ppermute | solution.py:303
  52.5 8.3 %collective-permute-start.19 = (f16[512,384]{1,0:T(8,128)(2,1)S(1)}, f16[512,384]{1,0:T(8,128)(2,1)S(1)}, u32[]{:S(2)}, u32[]{:S(2)}) collective-permute-start(f16[512,384]{1,0:T(8,128)(2,1)S(1)} %get-tuple-element.112), channel_id=1, source_target_pairs={{0,8},{8,0},{16,24},{24,16},{1,9},{9,1},{17,25},{25,17},{2,10},{10... | collective-permute-start | bytes 1179656 | tf_op jit(solution)/shard_map/ppermute | solution.py:317
  55.6 5.2 %collective-permute-start.18 = (f16[512,384]{1,0:T(8,128)(2,1)S(1)}, f16[512,384]{1,0:T(8,128)(2,1)S(1)}, u32[]{:S(2)}, u32[]{:S(2)}) collective-permute-start(f16[512,384]{1,0:T(8,128)(2,1)S(1)} %get-tuple-element.125), channel_id=1, source_target_pairs={{8,16},{16,8},{9,17},{17,9},{10,18},{18,10},{11,19},{19,11},{12,20... | collective-permute-start | bytes 1179656 | tf_op jit(solution)/shard_map/ppermute | solution.py:303
  61.1 6.0 %collective-permute-start.20 = (f32[1,128]{1,0:T(1,128)S(1)}, f32[1,128]{1,0:T(1,128)S(1)}, u32[]{:S(2)}, u32[]{:S(2)}) collective-permute-start(f32[1,128]{1,0:T(1,128)S(1)} %bitcast.23), channel_id=1, source_target_pairs={{0,2},{2,0},{4,6},{6,4},{1,3},{3,1},{5,7},{7,5},{8,10},{10,8},{12,... | collective-permute-start | bytes 1544 | tf_op jit(solution)/shard_map/ppermute | solution.py:39
  69.5 6.3 %collective-permute-start.24 = (f32[1,128]{1,0:T(1,128)S(1)}, f32[1,128]{1,0:T(1,128)S(1)}, u32[]{:S(2)}, u32[]{:S(2)}) collective-permute-start(f32[1,128]{1,0:T(1,128)S(1)} %add.156), channel_id=1, source_target_pairs={{0,1},{1,0},{2,3},{3,2},{4,5},{5,4},{6,7},{7,6},{8,9},{9,8},{10,11... | collective-permute-start | bytes 1544 | tf_op jit(solution)/shard_map/ppermute | solution.py:39
  70.7 5.1 %collective-permute-start.23 = (f32[1,128]{1,0:T(1,128)S(1)}, f32[1,128]{1,0:T(1,128)S(1)}, u32[]{:S(2)}, u32[]{:S(2)}) collective-permute-start(f32[1,128]{1,0:T(1,128)S(1)} %add.156), channel_id=1, source_target_pairs={{0,9},{1,8},{8,1},{9,0},{16,25},{17,24},{24,17},{25,16},{2,11},{3,... | collective-permute-start | bytes 1544 | tf_op jit(solution)/shard_map/ppermute | solution.py:347
  74.4 8.7 %collective-permute-start.25 = (f16[512,384]{1,0:T(8,128)(2,1)S(1)}, f16[512,384]{1,0:T(8,128)(2,1)S(1)}, u32[]{:S(2)}, u32[]{:S(2)}) collective-permute-start(f16[512,384]{1,0:T(8,128)(2,1)S(1)} %add_convert_fusion), channel_id=1, source_target_pairs={{0,8},{8,0},{16,24},{24,16},{1,9},{9,1},{17,25},{25,17},{2,10},{10... | collective-permute-start | bytes 1179656 | tf_op jit(solution)/shard_map/ppermute | solution.py:317
  80.5 8.4 %collective-permute-start.26 = (bf16[512,384]{1,0:T(8,128)(2,1)S(1)}, bf16[512,384]{1,0:T(8,128)(2,1)S(1)}, u32[]{:S(2)}, u32[]{:S(2)}) collective-permute-start(bf16[512,384]{1,0:T(8,128)(2,1)S(1)} %get-tuple-element.107), channel_id=1, source_target_pairs={{0,4},{2,6},{4,0},{6,2},{1,5},{3,7},{5,1},{7,3},{8,12},{10,14},{12... | collective-permute-start | bytes 1179656 | tf_op jit(solution)/shard_map/ppermute | solution.py:200
  88.9 6.3 %collective-permute-start.27 = (bf16[1536,384]{1,0:T(8,128)(2,1)S(1)}, bf16[1536,384]{1,0:T(8,128)(2,1)S(1)}, u32[]{:S(2)}, u32[]{:S(2)}) collective-permute-start(bf16[1536,384]{1,0:T(8,128)(2,1)S(1)} %get-tuple-element.93.refs_0_), channel_id=1, source_target_pairs={{0,2},{2,0},{4,6},{6,4},{1,3},{3,1},{5,7},{7,5},{8,10},{10,8},{12,... | collective-permute-start | bytes 3538952 | tf_op jit(solution)/shard_map/ppermute | solution.py:39
  92.2 11.7 %collective-permute-start.31 = (bf16[512,384]{1,0:T(8,128)(2,1)S(1)}, bf16[512,384]{1,0:T(8,128)(2,1)S(1)}, u32[]{:S(2)}, u32[]{:S(2)}) collective-permute-start(bf16[512,384]{1,0:T(8,128)(2,1)S(1)} %get-tuple-element.100), channel_id=1, source_target_pairs={{0,4},{2,6},{4,0},{6,2},{1,5},{3,7},{5,1},{7,3},{8,12},{10,14},{12... | collective-permute-start | bytes 1179656 | tf_op jit(solution)/shard_map/ppermute | solution.py:200
  93.5 10.4 %collective-permute-start.29 = (bf16[512,384]{1,0:T(8,128)(2,1)S(1)}, bf16[512,384]{1,0:T(8,128)(2,1)S(1)}, u32[]{:S(2)}, u32[]{:S(2)}) collective-permute-start(bf16[512,384]{1,0:T(8,128)(2,1)S(1)} %collective-permute-done.26.refs_0_), channel_id=1, source_target_pairs={{0,8},{8,0},{16,24},{24,16},{1,9},{9,1},{17,25},{25,17},{2,10},{10... | collective-permute-start | bytes 1179656 | tf_op jit(solution)/shard_map/ppermute | solution.py:39
  94.6 10.5 %collective-permute-start.28 = (bf16[512,384]{1,0:T(8,128)(2,1)S(1)}, bf16[512,384]{1,0:T(8,128)(2,1)S(1)}, u32[]{:S(2)}, u32[]{:S(2)}) collective-permute-start(bf16[512,384]{1,0:T(8,128)(2,1)S(1)} %collective-permute-done.26.refs_0_), channel_id=1, source_target_pairs={{0,2},{2,0},{4,6},{6,4},{1,3},{3,1},{5,7},{7,5},{8,10},{10,8},{12,... | collective-permute-start | bytes 1179656 | tf_op jit(solution)/shard_map/ppermute | solution.py:39
  (17 other events, 110.9 us)

commit v7 on v6

--- a/solution.py
+++ b/solution.py
@@ -100,7 +100,7 @@
         + [jax.ShapeDtypeStruct((rows, cols), jnp.bfloat16), jax.ShapeDtypeStruct((part, cols), jnp.bfloat16)],
         scratch_shapes=[pltpu.VMEM((3, rows, cols), jnp.float32), pltpu.SemaphoreType.DMA((6 * chunks,))],
         cost_estimate=SMALL,
-        compiler_params=pltpu.CompilerParams(vmem_limit_bytes=48 * 2**20),
+        compiler_params=pltpu.CompilerParams(vmem_limit_bytes=50 * 2**20),
     )(clip, *avgs, param, first, second)
 
 

time: 110 us -> 110 us (level)
  no operation moved by 1% of the time
where the time goes in v7:
time: 110 us; the launch traced here: 109 us
  starting transfers between devices  48.9 us (44%)
  waiting for transfers between devices  29.7 us (27%)
  other arithmetic  17.4 us (16%)
  Pallas kernels  10.9 us (10%)
  between operations  2.33 us (2%)
    ppermute x19, starting transfers between devices, exchange(): lax.ppermute(value, axis, [(i, i ^ step) for i in range(lax.axis_size(axi...  24.7 us
    ppermute x19, waiting for transfers between devices, exchange(): lax.ppermute(value, axis, [(i, i ^ step) for i in range(lax.axis_size(axi...  13 us
    ppermute x5, starting transfers between devices, body(): lax.ppermute(payload, 'rep', [(0, 1), (1, 0), (2, 3), (3, 2)])  10.7 us
    ppermute x5, waiting for transfers between devices, body(): lax.ppermute(payload, 'rep', [(0, 1), (1, 0), (2, 3), (3, 2)])  10.5 us
    ppermute x5, starting transfers between devices, chip_shift(): return lax.ppermute(x, 'dp', pairs)  7.76 us
    convert_element_type x8, other arithmetic, narrow(): return x.astype(jnp.float16)  6.38 us
    ppermute x5, waiting for transfers between devices, chip_shift(): return lax.ppermute(x, 'dp', pairs)  6.15 us
    pallas_call x1, Pallas kernels, step_state(): pl.pallas_call(kernel, in_specs=[pl.BlockSpec(memory_space=pltpu.SMEM)] +...  5.69 us
  transfers between devices with their start and end apart: 33, of which 17 were waited for; matrix products, arithmetic and copies ran while one was open for 10% of the time, Pallas kernels for 8%

profile of v7, /device:TPU:1, one launch (start us, length us, event | category | flops | bytes accessed | tf_op | source)
XLA Modules:
  0.0 109.4 jit_solution(2433200791553562576)
XLA Ops:
  0.7 2.1 %select_convert_fusion.3 = (f16[512,384]{1,0:T(8,128)(2,1)S(1)}, f16[512,384]{1,0:T(8,128)(2,1)S(1)}) fusion(pred[]{:T(512)S(6)} %eq.38, f32[1536,1536]{1,0:T(8,128)} %bitcast.14, pred[]{:T(512)S(6)} %eq.37, pred[]{:T(512)S(6)} %eq.35), kind=kLoop, calls=%fused_computation.30 | loop fusion | flops 1179648 | bytes 3932163 | tf_op jit(solution)/shard_map/convert_element_type | solution.py:55
  5.1 3.4 %convert_add_fusion.2 = (f32[512,384]{1,0:T(8,128)S(1)}, f16[512,384]{1,0:T(8,128)(2,1)S(1)}, f16[512,384]{1,0:T(8,128)(2,1)S(1)}) fusion(f16[512,384]{1,0:T(8,128)(2,1)S(1)} %collective-permute-done.4, pred[]{:T(512)S(6)} %eq.38, f32[1536,1536]{1,0:T(8,128)} %bitcast.15, pred[]{:T(512)S(6)} %eq.36, pred[]{:T(512)S(6)} %eq.37, pred[]{:T(512)S(6)} %eq.35, ...), kind=kLoop, calls=%fused_computation.29 | loop fusion | flops 2555904 | bytes 8650756 | tf_op jit(solution)/shard_map/add | solution.py:233
  8.7 2.6 %collective-permute-start.1 = (f16[512,384]{1,0:T(8,128)(2,1)S(1)}, f16[512,384]{1,0:T(8,128)(2,1)S(1)}, u32[]{:S(2)}, u32[]{:S(2)}) collective-permute-start(f16[512,384]{1,0:T(8,128)(2,1)S(1)} %get-tuple-element.121), channel_id=1, source_target_pairs={{0,4},{2,6},{4,0},{6,2},{1,5},{3,7},{5,1},{7,3},{8,12},{10,14},{12... | collective-permute-start | bytes 1179656 | tf_op jit(solution)/shard_map/ppermute | solution.py:200
  11.3 3.3 %select_convert_fusion.1 = (f16[512,384]{1,0:T(8,128)(2,1)S(1)}, f16[512,384]{1,0:T(8,128)(2,1)S(1)}, f16[512,384]{1,0:T(8,128)(2,1)S(1)}) fusion(pred[]{:T(512)S(6)} %eq.38, f32[1536,1536]{1,0:T(8,128)} %bitcast.16, pred[]{:T(512)S(6)} %eq.37, pred[]{:T(512)S(6)} %eq.35, f16[512,384]{1,0:T(8,128)(2,1)S(1)} %collective-permute-done.2, pred[]{:T(512)S(6)} %eq.36), kind=kLoop, calls=%fused_computation.25 | loop fusion | flops 2752512 | bytes 7864324 | tf_op jit(solution)/shard_map/convert_element_type | solution.py:55
  16.6 4.1 %collective-permute-done.1 = f16[512,384]{1,0:T(8,128)(2,1)S(1)} collective-permute-done((f16[512,384]{1,0:T(8,128)(2,1)S(1)}, f16[512,384]{1,0:T(8,128)(2,1)S(1)}, u32[]{:S(2)}, u32[]{:S(2)}) %collective-permute-start.1) | collective-permute-done | bytes 393248 | tf_op jit(solution)/shard_map/ppermute | solution.py:200
  23.9 2.4 %collective-permute-start.8 = (f32[4,1664]{1,0:T(4,128)S(1)}, f32[4,1664]{1,0:T(4,128)S(1)}, u32[]{:S(2)}, u32[]{:S(2)}) collective-permute-start(f32[4,1664]{1,0:T(4,128)S(1)} %add.137), channel_id=1, source_target_pairs={{0,16},{8,24},{16,0},{24,8},{1,17},{9,25},{17,1},{25,9},{2,18},{10... | collective-permute-start | bytes 79880 | tf_op jit(solution)/shard_map/ppermute | solution.py:39
  26.3 1.8 %collective-permute-start.14 = (f16[512,384]{1,0:T(8,128)(2,1)S(1)}, f16[512,384]{1,0:T(8,128)(2,1)S(1)}, u32[]{:S(2)}, u32[]{:S(2)}) collective-permute-start(f16[512,384]{1,0:T(8,128)(2,1)S(1)} %get-tuple-element.113), channel_id=1, source_target_pairs={{0,2},{2,0},{4,6},{6,4},{1,3},{3,1},{5,7},{7,5},{8,10},{10,8},{12,... | collective-permute-start | bytes 1179656 | tf_op jit(solution)/shard_map/ppermute | solution.py:39
  28.0 3.3 %collective-permute-done.6 = f16[512,384]{1,0:T(8,128)(2,1)S(1)} collective-permute-done((f16[512,384]{1,0:T(8,128)(2,1)S(1)}, f16[512,384]{1,0:T(8,128)(2,1)S(1)}, u32[]{:S(2)}, u32[]{:S(2)}) %collective-permute-start.6) | collective-permute-done | bytes 393248 | tf_op jit(solution)/shard_map/ppermute | solution.py:317
  31.6 1.6 %collective-permute-start.12 = (f16[512,384]{1,0:T(8,128)(2,1)S(1)}, f16[512,384]{1,0:T(8,128)(2,1)S(1)}, u32[]{:S(2)}, u32[]{:S(2)}) collective-permute-start(f16[512,384]{1,0:T(8,128)(2,1)S(1)} %add_convert_fusion.7), channel_id=1, source_target_pairs={{0,8},{8,0},{16,24},{24,16},{1,9},{9,1},{17,25},{25,17},{2,10},{10... | collective-permute-start | bytes 1179656 | tf_op jit(solution)/shard_map/ppermute | solution.py:317
  35.4 2.8 %collective-permute-start.13 = (f32[4,1664]{1,0:T(4,128)S(1)}, f32[4,1664]{1,0:T(4,128)S(1)}, u32[]{:S(2)}, u32[]{:S(2)}) collective-permute-start(f32[4,1664]{1,0:T(4,128)S(1)} %add.142), channel_id=1, source_target_pairs={{0,2},{2,0},{4,6},{6,4},{1,3},{3,1},{5,7},{7,5},{8,10},{10,8},{12,... | collective-permute-start | bytes 79880 | tf_op jit(solution)/shard_map/ppermute | solution.py:39
  38.2 2.0 %convert_add_fusion = f32[512,384]{1,0:T(8,128)S(1)} fusion(f16[512,384]{1,0:T(8,128)(2,1)S(1)} %collective-permute-done.14, pred[]{:T(512)S(6)} %eq.38, f32[1536,1536]{1,0:T(8,128)} %bitcast.17, pred[]{:T(512)S(6)} %eq.36), kind=kLoop, calls=%fused_computation.20 | loop fusion | flops 983040 | bytes 4325378 | tf_op jit(solution)/shard_map/add | solution.py:233
  40.4 1.9 %collective-permute-done.11 = f16[512,384]{1,0:T(8,128)(2,1)S(1)} collective-permute-done((f16[512,384]{1,0:T(8,128)(2,1)S(1)}, f16[512,384]{1,0:T(8,128)(2,1)S(1)}, u32[]{:S(2)}, u32[]{:S(2)}) %collective-permute-start.11) | collective-permute-done | bytes 393248 | tf_op jit(solution)/shard_map/ppermute | solution.py:200
  42.7 3.2 %collective-permute-start.16 = (f16[512,384]{1,0:T(8,128)(2,1)S(1)}, f16[512,384]{1,0:T(8,128)(2,1)S(1)}, u32[]{:S(2)}, u32[]{:S(2)}) collective-permute-start(f16[512,384]{1,0:T(8,128)(2,1)S(1)} %broadcast_select_fusion), channel_id=1, source_target_pairs={{0,8},{8,0},{16,24},{24,16},{1,9},{9,1},{17,25},{25,17},{2,10},{10... | collective-permute-start | bytes 1179656 | tf_op jit(solution)/shard_map/ppermute | solution.py:317
  49.3 2.6 %collective-permute-done.16 = f16[512,384]{1,0:T(8,128)(2,1)S(1)} collective-permute-done((f16[512,384]{1,0:T(8,128)(2,1)S(1)}, f16[512,384]{1,0:T(8,128)(2,1)S(1)}, u32[]{:S(2)}, u32[]{:S(2)}) %collective-permute-start.16) | collective-permute-done | bytes 393248 | tf_op jit(solution)/shard_map/ppermute | solution.py:317
  52.5 3.1 %collective-permute-start.19 = (f16[512,384]{1,0:T(8,128)(2,1)S(1)}, f16[512,384]{1,0:T(8,128)(2,1)S(1)}, u32[]{:S(2)}, u32[]{:S(2)}) collective-permute-start(f16[512,384]{1,0:T(8,128)(2,1)S(1)} %get-tuple-element.112), channel_id=1, source_target_pairs={{0,8},{8,0},{16,24},{24,16},{1,9},{9,1},{17,25},{25,17},{2,10},{10... | collective-permute-start | bytes 1179656 | tf_op jit(solution)/shard_map/ppermute | solution.py:317
  57.6 3.2 %collective-permute-done.19 = f16[512,384]{1,0:T(8,128)(2,1)S(1)} collective-permute-done((f16[512,384]{1,0:T(8,128)(2,1)S(1)}, f16[512,384]{1,0:T(8,128)(2,1)S(1)}, u32[]{:S(2)}, u32[]{:S(2)}) %collective-permute-start.19) | collective-permute-done | bytes 393248 | tf_op jit(solution)/shard_map/ppermute | solution.py:317
  61.1 5.2 %collective-permute-start.20 = (f32[1,128]{1,0:T(1,128)S(1)}, f32[1,128]{1,0:T(1,128)S(1)}, u32[]{:S(2)}, u32[]{:S(2)}) collective-permute-start(f32[1,128]{1,0:T(1,128)S(1)} %bitcast.23), channel_id=1, source_target_pairs={{0,2},{2,0},{4,6},{6,4},{1,3},{3,1},{5,7},{7,5},{8,10},{10,8},{12,... | collective-permute-start | bytes 1544 | tf_op jit(solution)/shard_map/ppermute | solution.py:39
  70.7 3.6 %collective-permute-start.23 = (f32[1,128]{1,0:T(1,128)S(1)}, f32[1,128]{1,0:T(1,128)S(1)}, u32[]{:S(2)}, u32[]{:S(2)}) collective-permute-start(f32[1,128]{1,0:T(1,128)S(1)} %add.156), channel_id=1, source_target_pairs={{0,9},{1,8},{8,1},{9,0},{16,25},{17,24},{24,17},{25,16},{2,11},{3,... | collective-permute-start | bytes 1544 | tf_op jit(solution)/shard_map/ppermute | solution.py:347
  78.1 2.4 %subtract_convert_fusion = (bf16[512,384]{1,0:T(8,128)(2,1)S(1)}, f32[512,384]{1,0:T(8,128)S(1)}) fusion(f32[1536,384]{1,0:T(8,128)} %refs_5_.1, s32[]{:T(128)S(6)} %select_n.246, f32[512,384]{1,0:T(8,128)S(1)} %get-tuple-element.86.refs_0_, f32[1536,384]{1,0:T(8,128)} %refs_4_.1, f32[1536,384]{1,0:T(8,128)} %refs_3_.1, f32[]{:T(128)} %min.5, pred[]{:T(512)S(6)} %eq.42, ...), kind=kLoop, calls=%fused_computation.8 | loop fusion | flops 4128768 | bytes 5111818 | tf_op jit(solution)/shard_map/convert_element_type | solution.py:381
  83.2 5.7 %shard_map.152 = (f32[1536,384]{1,0:T(8,128)}, f32[1536,384]{1,0:T(8,128)}, f32[1536,384]{1,0:T(8,128)}, bf16[1536,384]{1,0:T(8,128)(2,1)S(1)}, bf16[512,384]{1,0:T(8,128)(2,1)S(1)}) custom-call(f32[1,1]{1,0:T(1,128)} %bitcast.3.clip_ref, f32[512,384]{1,0:T(8,128)S(1)} %get-tuple-element.86.refs_0_, f32[512,384]{1,0:T(8,128)S(1)} %get-tuple-element.108.refs_1_, ...), custom_call_target="tpu_custom_call" | custom-call | flops 1 | bytes 1024 | tf_op jit(solution)/shard_map/pallas_call | solution.py:95
  88.9 3.2 %collective-permute-start.27 = (bf16[1536,384]{1,0:T(8,128)(2,1)S(1)}, bf16[1536,384]{1,0:T(8,128)(2,1)S(1)}, u32[]{:S(2)}, u32[]{:S(2)}) collective-permute-start(bf16[1536,384]{1,0:T(8,128)(2,1)S(1)} %get-tuple-element.93.refs_0_), channel_id=1, source_target_pairs={{0,2},{2,0},{4,6},{6,4},{1,3},{3,1},{5,7},{7,5},{8,10},{10,8},{12,... | collective-permute-start | bytes 3538952 | tf_op jit(solution)/shard_map/ppermute | solution.py:39
  95.2 2.7 %shard_map.153 = (bf16[1536,1536]{1,0:T(8,128)(2,1)}, f32[384,1536]{1,0:T(8,128)}, f32[384,768]{1,0:T(8,128)S(1)}) custom-call(s32[4]{0:T(128)S(1)} %pad_add_fusion.where_ref, f32[384,1536]{1,0:T(8,128)S(1)} %copy-done, bf16[1536,384]{1,0:T(8,128)(2,1)S(1)} %get-tuple-element.93.refs_0_, bf16[1536,384]{1,0:T(8,128)(2,1)S(1)} %collective-permute-done.27.refs_1_), custom_call_target="tpu_custom_call" | custom-call | flops 1 | bytes 1024 | tf_op jit(solution)/shard_map/pallas_call | solution.py:161
  98.7 5.2 %collective-permute-done.29.refs_2_ = bf16[512,384]{1,0:T(8,128)(2,1)S(1)} collective-permute-done((bf16[512,384]{1,0:T(8,128)(2,1)S(1)}, bf16[512,384]{1,0:T(8,128)(2,1)S(1)}, u32[]{:S(2)}, u32[]{:S(2)}) %collective-permute-start.29) | collective-permute-done | bytes 393248 | tf_op jit(solution)/shard_map/ppermute | solution.py:39
  106.9 2.5 %shard_map.154 = (bf16[1536,1536]{1,0:T(8,128)(2,1)}, f32[384,1536]{1,0:T(8,128)}) custom-call(s32[6]{0:T(128)S(1)} %stack.31.where_ref, f32[384,768]{1,0:T(8,128)S(1)} %get-tuple-element.94.old_ref, bf16[512,384]{1,0:T(8,128)(2,1)S(1)} %collective-permute-done.26.refs_0_, ...), custom_call_target="tpu_custom_call", output_to_operand_aliasing={{0}: (8, {}), {1}: (9, {})} | custom-call | flops 1 | bytes 1024 | tf_op jit(solution)/shard_map/pallas_call | solution.py:161
  (93 shorter events, 33.1 us)
Async XLA Ops:
  8.7 12.0 %collective-permute-start.1 = (f16[512,384]{1,0:T(8,128)(2,1)S(1)}, f16[512,384]{1,0:T(8,128)(2,1)S(1)}, u32[]{:S(2)}, u32[]{:S(2)}) collective-permute-start(f16[512,384]{1,0:T(8,128)(2,1)S(1)} %get-tuple-element.121), channel_id=1, source_target_pairs={{0,4},{2,6},{4,0},{6,2},{1,5},{3,7},{5,1},{7,3},{8,12},{10,14},{12... | collective-permute-start | bytes 1179656 | tf_op jit(solution)/shard_map/ppermute | solution.py:200
  14.6 8.7 %collective-permute-start.7 = (f16[512,384]{1,0:T(8,128)(2,1)S(1)}, f16[512,384]{1,0:T(8,128)(2,1)S(1)}, u32[]{:S(2)}, u32[]{:S(2)}) collective-permute-start(f16[512,384]{1,0:T(8,128)(2,1)S(1)} %get-tuple-element.117), channel_id=1, source_target_pairs={{0,2},{2,0},{4,6},{6,4},{1,3},{3,1},{5,7},{7,5},{8,10},{10,8},{12,... | collective-permute-start | bytes 1179656 | tf_op jit(solution)/shard_map/ppermute | solution.py:39
  15.1 8.3 %collective-permute-start.9 = (f16[512,384]{1,0:T(8,128)(2,1)S(1)}, f16[512,384]{1,0:T(8,128)(2,1)S(1)}, u32[]{:S(2)}, u32[]{:S(2)}) collective-permute-start(f16[512,384]{1,0:T(8,128)(2,1)S(1)} %get-tuple-element.116), channel_id=1, source_target_pairs={{0,2},{2,0},{4,6},{6,4},{1,3},{3,1},{5,7},{7,5},{8,10},{10,8},{12,... | collective-permute-start | bytes 1179656 | tf_op jit(solution)/shard_map/ppermute | solution.py:39
  15.2 5.5 %collective-permute-start.3 = (f32[4,1664]{1,0:T(4,128)S(1)}, f32[4,1664]{1,0:T(4,128)S(1)}, u32[]{:S(2)}, u32[]{:S(2)}) collective-permute-start(f32[4,1664]{1,0:T(4,128)S(1)} %bitcast.21), channel_id=1, source_target_pairs={{0,8},{8,0},{16,24},{24,16},{1,9},{9,1},{17,25},{25,17},{2,10},{10... | collective-permute-start | bytes 79880 | tf_op jit(solution)/shard_map/ppermute | solution.py:39
  20.8 10.6 %collective-permute-start.6 = (f16[512,384]{1,0:T(8,128)(2,1)S(1)}, f16[512,384]{1,0:T(8,128)(2,1)S(1)}, u32[]{:S(2)}, u32[]{:S(2)}) collective-permute-start(f16[512,384]{1,0:T(8,128)(2,1)S(1)} %add_convert_fusion.9), channel_id=1, source_target_pairs={{0,8},{8,0},{16,24},{24,16},{1,9},{9,1},{17,25},{25,17},{2,10},{10... | collective-permute-start | bytes 1179656 | tf_op jit(solution)/shard_map/ppermute | solution.py:317
  22.1 9.4 %collective-permute-start.5 = (f16[512,384]{1,0:T(8,128)(2,1)S(1)}, f16[512,384]{1,0:T(8,128)(2,1)S(1)}, u32[]{:S(2)}, u32[]{:S(2)}) collective-permute-start(f16[512,384]{1,0:T(8,128)(2,1)S(1)} %get-tuple-element.57), channel_id=1, source_target_pairs={{0,4},{2,6},{4,0},{6,2},{1,5},{3,7},{5,1},{7,3},{8,12},{10,14},{12... | collective-permute-start | bytes 1179656 | tf_op jit(solution)/shard_map/ppermute | solution.py:200
  23.9 7.6 %collective-permute-start.8 = (f32[4,1664]{1,0:T(4,128)S(1)}, f32[4,1664]{1,0:T(4,128)S(1)}, u32[]{:S(2)}, u32[]{:S(2)}) collective-permute-start(f32[4,1664]{1,0:T(4,128)S(1)} %add.137), channel_id=1, source_target_pairs={{0,16},{8,24},{16,0},{24,8},{1,17},{9,25},{17,1},{25,9},{2,18},{10... | collective-permute-start | bytes 79880 | tf_op jit(solution)/shard_map/ppermute | solution.py:39
  26.3 11.9 %collective-permute-start.14 = (f16[512,384]{1,0:T(8,128)(2,1)S(1)}, f16[512,384]{1,0:T(8,128)(2,1)S(1)}, u32[]{:S(2)}, u32[]{:S(2)}) collective-permute-start(f16[512,384]{1,0:T(8,128)(2,1)S(1)} %get-tuple-element.113), channel_id=1, source_target_pairs={{0,2},{2,0},{4,6},{6,4},{1,3},{3,1},{5,7},{7,5},{8,10},{10,8},{12,... | collective-permute-start | bytes 1179656 | tf_op jit(solution)/shard_map/ppermute | solution.py:39
  31.6 8.7 %collective-permute-start.12 = (f16[512,384]{1,0:T(8,128)(2,1)S(1)}, f16[512,384]{1,0:T(8,128)(2,1)S(1)}, u32[]{:S(2)}, u32[]{:S(2)}) collective-permute-start(f16[512,384]{1,0:T(8,128)(2,1)S(1)} %add_convert_fusion.7), channel_id=1, source_target_pairs={{0,8},{8,0},{16,24},{24,16},{1,9},{9,1},{17,25},{25,17},{2,10},{10... | collective-permute-start | bytes 1179656 | tf_op jit(solution)/shard_map/ppermute | solution.py:317
  33.4 7.0 %collective-permute-start.10 = (f16[512,384]{1,0:T(8,128)(2,1)S(1)}, f16[512,384]{1,0:T(8,128)(2,1)S(1)}, u32[]{:S(2)}, u32[]{:S(2)}) collective-permute-start(f16[512,384]{1,0:T(8,128)(2,1)S(1)} %add_convert_fusion.6), channel_id=1, source_target_pairs={{8,16},{16,8},{9,17},{17,9},{10,18},{18,10},{11,19},{19,11},{12,20... | collective-permute-start | bytes 1179656 | tf_op jit(solution)/shard_map/ppermute | solution.py:303
  34.1 8.2 %collective-permute-start.11 = (f16[512,384]{1,0:T(8,128)(2,1)S(1)}, f16[512,384]{1,0:T(8,128)(2,1)S(1)}, u32[]{:S(2)}, u32[]{:S(2)}) collective-permute-start(f16[512,384]{1,0:T(8,128)(2,1)S(1)} %get-tuple-element.67), channel_id=1, source_target_pairs={{0,4},{2,6},{4,0},{6,2},{1,5},{3,7},{5,1},{7,3},{8,12},{10,14},{12... | collective-permute-start | bytes 1179656 | tf_op jit(solution)/shard_map/ppermute | solution.py:200
  42.7 9.3 %collective-permute-start.16 = (f16[512,384]{1,0:T(8,128)(2,1)S(1)}, f16[512,384]{1,0:T(8,128)(2,1)S(1)}, u32[]{:S(2)}, u32[]{:S(2)}) collective-permute-start(f16[512,384]{1,0:T(8,128)(2,1)S(1)} %broadcast_select_fusion), channel_id=1, source_target_pairs={{0,8},{8,0},{16,24},{24,16},{1,9},{9,1},{17,25},{25,17},{2,10},{10... | collective-permute-start | bytes 1179656 | tf_op jit(solution)/shard_map/ppermute | solution.py:317
  45.9 6.1 %collective-permute-start.15 = (f16[512,384]{1,0:T(8,128)(2,1)S(1)}, f16[512,384]{1,0:T(8,128)(2,1)S(1)}, u32[]{:S(2)}, u32[]{:S(2)}) collective-permute-start(f16[512,384]{1,0:T(8,128)(2,1)S(1)} %add_convert_fusion.5), channel_id=1, source_target_pairs={{8,16},{16,8},{9,17},{17,9},{10,18},{18,10},{11,19},{19,11},{12,20... | collective-permute-start | bytes 1179656 | tf_op jit(solution)/shard_map/ppermute | solution.py:303
  52.5 8.3 %collective-permute-start.19 = (f16[512,384]{1,0:T(8,128)(2,1)S(1)}, f16[512,384]{1,0:T(8,128)(2,1)S(1)}, u32[]{:S(2)}, u32[]{:S(2)}) collective-permute-start(f16[512,384]{1,0:T(8,128)(2,1)S(1)} %get-tuple-element.112), channel_id=1, source_target_pairs={{0,8},{8,0},{16,24},{24,16},{1,9},{9,1},{17,25},{25,17},{2,10},{10... | collective-permute-start | bytes 1179656 | tf_op jit(solution)/shard_map/ppermute | solution.py:317
  55.6 5.2 %collective-permute-start.18 = (f16[512,384]{1,0:T(8,128)(2,1)S(1)}, f16[512,384]{1,0:T(8,128)(2,1)S(1)}, u32[]{:S(2)}, u32[]{:S(2)}) collective-permute-start(f16[512,384]{1,0:T(8,128)(2,1)S(1)} %get-tuple-element.125), channel_id=1, source_target_pairs={{8,16},{16,8},{9,17},{17,9},{10,18},{18,10},{11,19},{19,11},{12,20... | collective-permute-start | bytes 1179656 | tf_op jit(solution)/shard_map/ppermute | solution.py:303
  61.1 6.0 %collective-permute-start.20 = (f32[1,128]{1,0:T(1,128)S(1)}, f32[1,128]{1,0:T(1,128)S(1)}, u32[]{:S(2)}, u32[]{:S(2)}) collective-permute-start(f32[1,128]{1,0:T(1,128)S(1)} %bitcast.23), channel_id=1, source_target_pairs={{0,2},{2,0},{4,6},{6,4},{1,3},{3,1},{5,7},{7,5},{8,10},{10,8},{12,... | collective-permute-start | bytes 1544 | tf_op jit(solution)/shard_map/ppermute | solution.py:39
  69.5 6.3 %collective-permute-start.24 = (f32[1,128]{1,0:T(1,128)S(1)}, f32[1,128]{1,0:T(1,128)S(1)}, u32[]{:S(2)}, u32[]{:S(2)}) collective-permute-start(f32[1,128]{1,0:T(1,128)S(1)} %add.156), channel_id=1, source_target_pairs={{0,1},{1,0},{2,3},{3,2},{4,5},{5,4},{6,7},{7,6},{8,9},{9,8},{10,11... | collective-permute-start | bytes 1544 | tf_op jit(solution)/shard_map/ppermute | solution.py:39
  70.7 5.1 %collective-permute-start.23 = (f32[1,128]{1,0:T(1,128)S(1)}, f32[1,128]{1,0:T(1,128)S(1)}, u32[]{:S(2)}, u32[]{:S(2)}) collective-permute-start(f32[1,128]{1,0:T(1,128)S(1)} %add.156), channel_id=1, source_target_pairs={{0,9},{1,8},{8,1},{9,0},{16,25},{17,24},{24,17},{25,16},{2,11},{3,... | collective-permute-start | bytes 1544 | tf_op jit(solution)/shard_map/ppermute | solution.py:347
  74.4 8.7 %collective-permute-start.25 = (f16[512,384]{1,0:T(8,128)(2,1)S(1)}, f16[512,384]{1,0:T(8,128)(2,1)S(1)}, u32[]{:S(2)}, u32[]{:S(2)}) collective-permute-start(f16[512,384]{1,0:T(8,128)(2,1)S(1)} %add_convert_fusion), channel_id=1, source_target_pairs={{0,8},{8,0},{16,24},{24,16},{1,9},{9,1},{17,25},{25,17},{2,10},{10... | collective-permute-start | bytes 1179656 | tf_op jit(solution)/shard_map/ppermute | solution.py:317
  80.5 8.4 %collective-permute-start.26 = (bf16[512,384]{1,0:T(8,128)(2,1)S(1)}, bf16[512,384]{1,0:T(8,128)(2,1)S(1)}, u32[]{:S(2)}, u32[]{:S(2)}) collective-permute-start(bf16[512,384]{1,0:T(8,128)(2,1)S(1)} %get-tuple-element.107), channel_id=1, source_target_pairs={{0,4},{2,6},{4,0},{6,2},{1,5},{3,7},{5,1},{7,3},{8,12},{10,14},{12... | collective-permute-start | bytes 1179656 | tf_op jit(solution)/shard_map/ppermute | solution.py:200
  88.9 6.3 %collective-permute-start.27 = (bf16[1536,384]{1,0:T(8,128)(2,1)S(1)}, bf16[1536,384]{1,0:T(8,128)(2,1)S(1)}, u32[]{:S(2)}, u32[]{:S(2)}) collective-permute-start(bf16[1536,384]{1,0:T(8,128)(2,1)S(1)} %get-tuple-element.93.refs_0_), channel_id=1, source_target_pairs={{0,2},{2,0},{4,6},{6,4},{1,3},{3,1},{5,7},{7,5},{8,10},{10,8},{12,... | collective-permute-start | bytes 3538952 | tf_op jit(solution)/shard_map/ppermute | solution.py:39
  92.2 11.7 %collective-permute-start.31 = (bf16[512,384]{1,0:T(8,128)(2,1)S(1)}, bf16[512,384]{1,0:T(8,128)(2,1)S(1)}, u32[]{:S(2)}, u32[]{:S(2)}) collective-permute-start(bf16[512,384]{1,0:T(8,128)(2,1)S(1)} %get-tuple-element.100), channel_id=1, source_target_pairs={{0,4},{2,6},{4,0},{6,2},{1,5},{3,7},{5,1},{7,3},{8,12},{10,14},{12... | collective-permute-start | bytes 1179656 | tf_op jit(solution)/shard_map/ppermute | solution.py:200
  93.5 10.4 %collective-permute-start.29 = (bf16[512,384]{1,0:T(8,128)(2,1)S(1)}, bf16[512,384]{1,0:T(8,128)(2,1)S(1)}, u32[]{:S(2)}, u32[]{:S(2)}) collective-permute-start(bf16[512,384]{1,0:T(8,128)(2,1)S(1)} %collective-permute-done.26.refs_0_), channel_id=1, source_target_pairs={{0,8},{8,0},{16,24},{24,16},{1,9},{9,1},{17,25},{25,17},{2,10},{10... | collective-permute-start | bytes 1179656 | tf_op jit(solution)/shard_map/ppermute | solution.py:39
  94.6 10.5 %collective-permute-start.28 = (bf16[512,384]{1,0:T(8,128)(2,1)S(1)}, bf16[512,384]{1,0:T(8,128)(2,1)S(1)}, u32[]{:S(2)}, u32[]{:S(2)}) collective-permute-start(bf16[512,384]{1,0:T(8,128)(2,1)S(1)} %collective-permute-done.26.refs_0_), channel_id=1, source_target_pairs={{0,2},{2,0},{4,6},{6,4},{1,3},{3,1},{5,7},{7,5},{8,10},{10,8},{12,... | collective-permute-start | bytes 1179656 | tf_op jit(solution)/shard_map/ppermute | solution.py:39
  (17 other events, 110.9 us)
